TPU v7x, 32 devices: a whole 2x2x4 slice. The times are simulated.
32 devices in a mesh: dp: 8 (over z, x), blk: 4 (over y, core).
Axes of the slice: x: 2, y: 2, z: 4, core: 2. Of those that a mesh axis runs over, the one named last changes fastest.
Arguments:
- tokens: bfloat16 [64, 512, 1024], P('dp', 'blk'), may hold values from -6 to 6
- lengths: int32 [64], P('dp'), may hold values from 128 to 512, as said below
- teacher: bfloat16 [64, 512, 1024], P('dp', 'blk'), may hold values from -18 to 18
- out_grad: bfloat16 [64, 512, 1024], P('dp', 'blk'), may hold values from -6 to 6
- w_query: bfloat16 [1024, 1024], P(('dp', 'blk')), may hold values from -0.1875 to 0.1875
- w_key: bfloat16 [1024, 1024], P(('dp', 'blk')), may hold values from -0.1875 to 0.1875
- w_value: bfloat16 [1024, 1024], P(('dp', 'blk')), may hold values from -0.1875 to 0.1875
- w_output: bfloat16 [1024, 1024], P(('dp', 'blk')), may hold values from -1.5 to 1.5
- gain_one: bfloat16 [1024], P(('dp', 'blk')), may hold values from 0.099609375 to 1.8984375
- shift_one: bfloat16 [1024], P(('dp', 'blk')), may hold values from -3 to 3
- w_inner: bfloat16 [1024, 4096], P(('dp', 'blk')), may hold values from -0.1875 to 0.1875
- bias_inner: bfloat16 [4096], P(('dp', 'blk')), may hold values from -3 to 3
- w_outer: bfloat16 [4096, 1024], P(('dp', 'blk')), may hold values from -0.09375 to 0.09375
- bias_outer: bfloat16 [1024], P(('dp', 'blk')), may hold values from -3 to 3
- gain_two: bfloat16 [1024], P(('dp', 'blk')), may hold values from 0.099609375 to 1.8984375
- shift_two: bfloat16 [1024], P(('dp', 'blk')), may hold values from -3 to 3
Outputs:
- mse_loss: float32 [], replicated
- layer_out: bfloat16 [64, 512, 1024], P('dp', 'blk')
- grad_tokens: float32 [64, 512, 1024], P('dp', 'blk')
- grad_query: float32 [1024, 1024], P(('dp', 'blk'))
- grad_key: float32 [1024, 1024], P(('dp', 'blk'))
- grad_value: float32 [1024, 1024], P(('dp', 'blk'))
- grad_output: float32 [1024, 1024], P(('dp', 'blk'))
- grad_gain_one: float32 [1024], P(('dp', 'blk'))
- grad_shift_one: float32 [1024], P(('dp', 'blk'))
- grad_inner: float32 [1024, 4096], P(('dp', 'blk'))
- grad_bias_inner: float32 [4096], P(('dp', 'blk'))
- grad_outer: float32 [4096, 1024], P(('dp', 'blk'))
- grad_bias_outer: float32 [1024], P(('dp', 'blk'))
- grad_gain_two: float32 [1024], P(('dp', 'blk'))
- grad_shift_two: float32 [1024], P(('dp', 'blk'))
Inputs may be any that keep to these rules, and one draw needn't show every extreme that they name: `lengths`: each aligned block of 8 sequences, those of one index of dp, holds one sequence of full length 512, which one drawn from the seed.
All inputs are finite; a program needn't handle non-finite values.
Results may differ from a plain program's by a relative error of at most 0.019.
Values may be sent and summed in bfloat16 or wider, within the bound.
A program may use at most 320 MiB of HBM per device.

v0:
```python
import math

import jax
import jax.numpy as jnp
from jax import lax
from jax.sharding import PartitionSpec as P

H = 16
DH = 64


def normalize(values):
    row_mean = jnp.mean(values, axis=-1, keepdims=True)
    centred = values - row_mean
    spread = jnp.mean(centred * centred, axis=-1, keepdims=True)
    inverse = lax.rsqrt(spread + 1e-12)
    return (centred * inverse, inverse)


def norm_back(grad_out, normal, inverse, gain_vec):
    scaled = grad_out * gain_vec
    middle = jnp.mean(scaled, axis=-1, keepdims=True)
    projected = jnp.mean(scaled * normal, axis=-1, keepdims=True)
    return inverse * (scaled - middle - normal * projected)


def gelu_slope(inner):
    cumulative = 0.5 * (1.0 + lax.erf(inner * (1.0 / math.sqrt(2.0))))
    density = jnp.exp(-0.5 * inner * inner) * (1.0 / math.sqrt(2.0 * math.pi))
    return cumulative + inner * density


def matmul_t(left, right):
    return lax.dot_general(
        left, right, (((0,), (0,)), ((), ())), preferred_element_type=jnp.float32
    )


def matmul_rt(left, right):
    return lax.dot_general(
        left, right, (((1,), (1,)), ((), ())), preferred_element_type=jnp.float32
    )


def shards(
    tokens,
    lengths,
    teacher,
    out_grad,
    w_query,
    w_key,
    w_value,
    w_output,
    gain_one,
    shift_one,
    w_inner,
    bias_inner,
    w_outer,
    bias_outer,
    gain_two,
    shift_two,
):
    seq_count, stretch_len, width = tokens.shape
    heads = H
    head_size = DH
    scaling = 1.0 / math.sqrt(DH)
    f32 = jnp.float32
    bf16 = jnp.bfloat16
    full_query, full_key, full_value, full_output, full_gain_one, full_shift_one = (
        lax.all_gather(w_query, ("dp", "blk"), axis=0, tiled=True),
        lax.all_gather(w_key, ("dp", "blk"), axis=0, tiled=True),
        lax.all_gather(w_value, ("dp", "blk"), axis=0, tiled=True),
        lax.all_gather(w_output, ("dp", "blk"), axis=0, tiled=True),
        lax.all_gather(gain_one, ("dp", "blk"), axis=0, tiled=True),
        lax.all_gather(shift_one, ("dp", "blk"), axis=0, tiled=True),
    )
    full_inner, full_bias_inner, full_outer, full_bias_outer, full_gain_two, full_shift_two = (
        lax.all_gather(w_inner, ("dp", "blk"), axis=0, tiled=True),
        lax.all_gather(bias_inner, ("dp", "blk"), axis=0, tiled=True),
        lax.all_gather(w_outer, ("dp", "blk"), axis=0, tiled=True),
        lax.all_gather(bias_outer, ("dp", "blk"), axis=0, tiled=True),
        lax.all_gather(gain_two, ("dp", "blk"), axis=0, tiled=True),
        lax.all_gather(shift_two, ("dp", "blk"), axis=0, tiled=True),
    )
    own_start = lax.axis_index("blk") * stretch_len
    positions = own_start + jnp.arange(stretch_len)
    valid = (positions[None, :] < lengths[:, None]).astype(f32)
    valid_rows = valid.reshape(-1, 1)
    token_rows = tokens.reshape(-1, width)
    queries = jnp.dot(token_rows, full_query, preferred_element_type=f32).astype(bf16)
    key_rows = jnp.dot(token_rows, full_key, preferred_element_type=f32).astype(bf16)
    value_rows = jnp.dot(token_rows, full_value, preferred_element_type=f32).astype(bf16)
    query_heads = queries.reshape(seq_count, stretch_len, heads, head_size)
    key_blocks = key_rows.reshape(seq_count, stretch_len, width)
    value_blocks = value_rows.reshape(seq_count, stretch_len, width)

    def score_block(piece_keys):
        key_span = piece_keys.shape[1]
        key_heads = piece_keys.reshape(seq_count, key_span, heads, head_size)
        scores = (
            jnp.einsum("sqhd,skhd->shqk", query_heads, key_heads, preferred_element_type=f32)
            * scaling
        )
        key_pos = jnp.arange(key_span)
        allowed = (key_pos[None, :] < lengths[:, None])[:, None, None, :]
        return (jnp.where(allowed, scores, -1e30), allowed)

    def widen(per_head):
        return jnp.repeat(jnp.transpose(per_head, (0, 2, 1)), head_size, axis=-1)

    pieces = (
        lax.all_gather(key_blocks, "blk", axis=1, tiled=True),
        lax.all_gather(value_blocks, "blk", axis=1, tiled=True),
    )
    top_score = jnp.full((seq_count, heads, stretch_len), -1e30, f32)
    summed = jnp.zeros((seq_count, stretch_len, width), f32)
    scores, allowed = score_block(pieces[0])
    new_top = jnp.maximum(top_score, jnp.max(scores, axis=-1))
    weights = jnp.where(allowed, jnp.exp(scores - new_top[..., None]), 0.0)
    factor = jnp.exp(top_score - new_top)
    denominator = jnp.sum(weights, axis=-1)
    value_heads = pieces[1].reshape(seq_count, -1, heads, head_size)
    update = jnp.einsum(
        "shqk,skhd->sqhd", weights.astype(bf16), value_heads, preferred_element_type=f32
    )
    summed = summed * widen(factor) + update.reshape(seq_count, stretch_len, width)
    top_score, denominator, summed = (new_top, denominator, summed)
    attended = summed / widen(denominator)
    log_total = top_score + jnp.log(denominator)
    mixed = attended.reshape(-1, width).astype(bf16)
    branch = jnp.dot(mixed, full_output, preferred_element_type=f32)
    gain_vec_one = full_gain_one.astype(f32)
    gain_vec_two = full_gain_two.astype(f32)
    normal_one, inverse_one = normalize(token_rows.astype(f32) + branch)
    normed = normal_one * gain_vec_one + full_shift_one.astype(f32)
    normed_low = normed.astype(bf16)
    inner = jnp.dot(normed_low, full_inner, preferred_element_type=f32) + full_bias_inner.astype(
        f32
    )
    active_low = jax.nn.gelu(inner, approximate=False).astype(bf16)
    outer = jnp.dot(active_low, full_outer, preferred_element_type=f32) + full_bias_outer.astype(
        f32
    )
    normal_two, inverse_two = normalize(normed + outer)
    result = normal_two * gain_vec_two + full_shift_two.astype(f32)
    deviation = result - teacher.reshape(-1, width).astype(f32)
    square_part = jnp.sum(deviation * deviation * valid_rows)
    count_part = jnp.sum(valid)
    square_total, valid_count = lax.psum((square_part, count_part), ("dp", "blk"))
    inv_count = 1.0 / (valid_count * width)
    grad_result = (
        out_grad.reshape(-1, width).astype(f32) * valid_rows
        + 2.0 * deviation * valid_rows * inv_count
    )
    grad_gain_two = jnp.sum(grad_result * normal_two, axis=0)
    grad_shift_two = jnp.sum(grad_result, axis=0)
    grad_sum_two = norm_back(grad_result, normal_two, inverse_two, gain_vec_two)
    back_inner, back_outer = (
        lax.all_gather(w_inner, ("dp", "blk"), axis=0, tiled=True),
        lax.all_gather(w_outer, ("dp", "blk"), axis=0, tiled=True),
    )
    grad_outer_low = grad_sum_two.astype(bf16)
    grad_w_outer = matmul_t(active_low, grad_outer_low)
    grad_b_outer = jnp.sum(grad_outer_low.astype(f32), axis=0)
    grad_active = matmul_rt(grad_outer_low, back_outer)
    grad_inner_low = (grad_active * gelu_slope(inner)).astype(bf16)
    grad_w_inner = matmul_t(normed_low, grad_inner_low)
    grad_b_inner = jnp.sum(grad_inner_low.astype(f32), axis=0)
    ffn_totals = (
        lax.psum_scatter(grad_w_inner, ("dp", "blk"), scatter_dimension=0, tiled=True),
        lax.psum_scatter(grad_b_inner, ("dp", "blk"), scatter_dimension=0, tiled=True),
        lax.psum_scatter(grad_w_outer, ("dp", "blk"), scatter_dimension=0, tiled=True),
        lax.psum_scatter(grad_b_outer, ("dp", "blk"), scatter_dimension=0, tiled=True),
        lax.psum_scatter(grad_gain_two, ("dp", "blk"), scatter_dimension=0, tiled=True),
        lax.psum_scatter(grad_shift_two, ("dp", "blk"), scatter_dimension=0, tiled=True),
    )
    grad_normed = grad_sum_two + matmul_rt(grad_inner_low, back_inner)
    grad_gain_one = jnp.sum(grad_normed * normal_one, axis=0)
    grad_shift_one = jnp.sum(grad_normed, axis=0)
    grad_sum_one = norm_back(grad_normed, normal_one, inverse_one, gain_vec_one)
    back_query, back_key, back_value, back_output = (
        lax.all_gather(w_query, ("dp", "blk"), axis=0, tiled=True),
        lax.all_gather(w_key, ("dp", "blk"), axis=0, tiled=True),
        lax.all_gather(w_value, ("dp", "blk"), axis=0, tiled=True),
        lax.all_gather(w_output, ("dp", "blk"), axis=0, tiled=True),
    )
    grad_branch = grad_sum_one.astype(bf16)
    grad_w_output = matmul_t(mixed, grad_branch)
    grad_mixed = matmul_rt(grad_branch, back_output).astype(bf16)
    grad_heads = grad_mixed.reshape(seq_count, stretch_len, heads, head_size)
    row_delta = jnp.einsum(
        "sqhd,sqhd->shq",
        grad_heads.astype(f32),
        attended.reshape(seq_count, stretch_len, heads, head_size),
    )
    pieces = (
        lax.all_gather(key_blocks, "blk", axis=1, tiled=True),
        lax.all_gather(value_blocks, "blk", axis=1, tiled=True),
    )
    key_span = pieces[0].shape[1]
    query_key_span = pieces[0].shape[1]
    scores, allowed = score_block(pieces[0])
    probability = jnp.where(allowed, jnp.exp(scores - log_total[..., None]), 0.0)
    key_heads = pieces[0].reshape(seq_count, query_key_span, heads, head_size)
    value_heads = pieces[1].reshape(seq_count, query_key_span, heads, head_size)
    grad_probs = jnp.einsum("sqhd,skhd->shqk", grad_heads, value_heads, preferred_element_type=f32)
    grad_scores = (probability * (grad_probs - row_delta[..., None])).astype(bf16)
    query_part = jnp.einsum("shqk,skhd->sqhd", grad_scores, key_heads, preferred_element_type=f32)
    probability, grad_scores, query_part = (
        probability,
        grad_scores,
        query_part.reshape(seq_count, stretch_len, width) * scaling,
    )
    value_part = jnp.einsum(
        "shqk,sqhd->skhd", probability.astype(bf16), grad_heads, preferred_element_type=f32
    ).reshape(seq_count, key_span, width)
    key_part = jnp.einsum("shqk,sqhd->skhd", grad_scores, query_heads, preferred_element_type=f32)
    grad_k = key_part.reshape(seq_count, key_span, width) * scaling
    own_keys, own_values = (
        lax.psum_scatter(
            grad_k.astype(jnp.bfloat16), "blk", scatter_dimension=1, tiled=True
        ).astype(jnp.float32),
        lax.psum_scatter(
            value_part.astype(jnp.bfloat16), "blk", scatter_dimension=1, tiled=True
        ).astype(jnp.float32),
    )
    grad_q_low = query_part.reshape(-1, width).astype(bf16)
    grad_k_low = own_keys.reshape(-1, width).astype(bf16)
    grad_v_low = own_values.reshape(-1, width).astype(bf16)
    grad_w_query = matmul_t(token_rows, grad_q_low)
    grad_w_key = matmul_t(token_rows, grad_k_low)
    grad_w_value = matmul_t(token_rows, grad_v_low)
    attn_totals = (
        lax.psum_scatter(grad_w_query, ("dp", "blk"), scatter_dimension=0, tiled=True),
        lax.psum_scatter(grad_w_key, ("dp", "blk"), scatter_dimension=0, tiled=True),
        lax.psum_scatter(grad_w_value, ("dp", "blk"), scatter_dimension=0, tiled=True),
        lax.psum_scatter(grad_w_output, ("dp", "blk"), scatter_dimension=0, tiled=True),
        lax.psum_scatter(grad_gain_one, ("dp", "blk"), scatter_dimension=0, tiled=True),
        lax.psum_scatter(grad_shift_one, ("dp", "blk"), scatter_dimension=0, tiled=True),
    )
    grad_input = (
        grad_sum_one
        + matmul_rt(grad_q_low, back_query)
        + matmul_rt(grad_k_low, back_key)
        + matmul_rt(grad_v_low, back_value)
    )
    mse_loss = square_total * inv_count
    layer_out = result.reshape(seq_count, stretch_len, width).astype(bf16)
    return (
        mse_loss,
        layer_out,
        grad_input.reshape(seq_count, stretch_len, width),
        attn_totals[0],
        attn_totals[1],
        attn_totals[2],
        attn_totals[3],
        attn_totals[4],
        attn_totals[5],
        ffn_totals[0],
        ffn_totals[1],
        ffn_totals[2],
        ffn_totals[3],
        ffn_totals[4],
        ffn_totals[5],
    )


def solution(mesh):
    placed = (
        P("dp", "blk", None),
        P("dp"),
        P("dp", "blk", None),
        P("dp", "blk", None),
        P(("dp", "blk"), None),
        P(("dp", "blk"), None),
        P(("dp", "blk"), None),
        P(("dp", "blk"), None),
        P(("dp", "blk")),
        P(("dp", "blk")),
        P(("dp", "blk"), None),
        P(("dp", "blk")),
        P(("dp", "blk"), None),
        P(("dp", "blk")),
        P(("dp", "blk")),
        P(("dp", "blk")),
    )
    return jax.shard_map(
        shards,
        mesh=mesh,
        in_specs=placed,
        out_specs=(
            P(),
            P("dp", "blk", None),
            P("dp", "blk", None),
            P(("dp", "blk"), None),
            P(("dp", "blk"), None),
            P(("dp", "blk"), None),
            P(("dp", "blk"), None),
            P(("dp", "blk")),
            P(("dp", "blk")),
            P(("dp", "blk"), None),
            P(("dp", "blk")),
            P(("dp", "blk"), None),
            P(("dp", "blk")),
            P(("dp", "blk")),
            P(("dp", "blk")),
        ),
        check_vma=False,
    )
```

profile of v0, /device:TPU:0, one launch (start us, length us, event | category | flops | bytes accessed | tf_op | source)
XLA Modules:
  0.0 1710.0 jit_solution(13812580776576377223)
XLA Ops:
  9.4 60.6 %all-gather.12.cloned.1.call-done = bf16[1024,1024]{1,0:T(8,128)(2,1)} async-done(((bf16[32,1024]{1,0:T(8,128)(2,1)}), bf16[1024,1024]{1,0:T(8,128)(2,1)}) %all-gather.12.cloned.1.call-update) | async-done | bytes 2097168 | tf_op jit(solution)/shard_map/all_gather | solution.py:71
  70.0 6.0 convolution_convert_fusion.2
  76.2 52.0 %all-gather.16.cloned.1.call-done = bf16[1024,1024]{1,0:T(8,128)(2,1)} async-done(((bf16[32,1024]{1,0:T(8,128)(2,1)}), bf16[1024,1024]{1,0:T(8,128)(2,1)}) %all-gather.16.cloned.1.call-update) | async-done | bytes 2097168 | tf_op jit(solution)/shard_map/all_gather | solution.py:72
  128.2 5.3 convolution_convert_fusion.1
  138.7 38.9 %all-reduce.12 = (bf16[1024]{0:T(1024)(128)(2,1)S(1)}, bf16[1024]{0:T(1024)(128)(2,1)S(1)}, bf16[1024]{0:T(1024)(128)(2,1)S(1)}, bf16[1024]{0:T(1024)(128)(2,1)S(1)}, bf16[1024]{0:T(1024)(128)(2,1)S(1)}) all-reduce(bf16[1024]{0:T(1024)(128)(2,1)S(1)} %dynamic-update-slice.4, ...), channel_id=1, replica_groups=mesh['dp'=8,'blk'=4] {'dp','blk'}, use_global_device_ids=true, to_apply=%add.4 | all-reduce | flops 5120 | bytes 20480
  177.7 40.3 %all-gather = bf16[32,1,128]{2,1,0:T(2,128)(2,1)S(1)} all-gather(bf16[1,1,128]{2,1,0:T(2,128)(2,1)S(1)} %bitcast.139), channel_id=1, replica_groups=mesh['dp'=8,'blk'=4] {'dp','blk'}, dimensions={0}, use_global_device_ids=true | all-gather | bytes 8448 | tf_op jit(solution)/shard_map/all_gather | solution.py:79
  219.8 37.9 %psum.15 = f32[]{:T(128)} all-reduce(f32[]{:T(128)} %get-tuple-element.103), channel_id=1, replica_groups=mesh['dp'=8,'blk'=4] {'dp','blk'}, use_global_device_ids=true, to_apply=%region_9.10 | all-reduce | flops 1 | bytes 8 | tf_op jit(solution)/shard_map/psum | solution.py:149
  258.5 5.3 convolution_convert_fusion.3
  267.8 4.9 copy.76
  272.8 12.0 copy.75
  284.8 16.1 fusion.3
  300.9 15.2 fusion
  316.8 11.4 copy.77
  328.2 17.5 %fusion.72 = (bf16[8,128,16,64]{1,3,2,0:T(8,128)(2,1)S(1)}, f32[8,128,16,64]{1,3,2,0:T(8,128)}) fusion(f32[8,128,16]{1,2,0:T(8,128)S(1)} %bitcast.136, bf16[8,512,16,64]{1,3,2,0:T(8,128)(2,1)} %bitcast.123, f32[8,16,128,512]{3,2,1,0:T(8,128)} %get-tuple-element.105, f32[8,16,128]{2,1,0:T(8,128)S(1)} %broadcast_maximum_fusion, ...), kind=kOutput, calls=%fused_computation.126 | convolution fusion | flops 1118830592 | bytes 48435200 | tf_op jit(solution)/shard_map/shqk,skhd->sqhd/dot_general | solution.py:123
  347.5 18.1 %all-gather.20.cloned.1.call-done = bf16[1024,1024]{1,0:T(8,128)(2,1)} async-done(((bf16[32,1024]{1,0:T(8,128)(2,1)}), bf16[1024,1024]{1,0:T(8,128)(2,1)}) %all-gather.20.cloned.1.call-update) | async-done | bytes 2097168 | tf_op jit(solution)/shard_map/all_gather | solution.py:73
  365.6 4.9 fusion.73
  373.0 71.9 %all-gather.22.cloned.1.call-done = bf16[1024,4096]{1,0:T(8,128)(2,1)} async-done(((bf16[32,4096]{1,0:T(8,128)(2,1)}), bf16[1024,4096]{1,0:T(8,128)(2,1)}) %all-gather.22.cloned.1.call-update) | async-done | bytes 8388624 | tf_op jit(solution)/shard_map/all_gather | solution.py:78
  444.9 50.7 %fusion.6 = (bf16[1024,4096]{1,0:T(8,128)(2,1)}, f32[1024,4096]{1,0:T(8,128)}) fusion(f32[4096]{0:T(1024)S(1)} %bitcast.137, bf16[1024,4096]{1,0:T(8,128)(2,1)} %all-gather.22.cloned.1.call-done, f32[1024,1024]{1,0:T(8,128)} %copy-done.4, f32[1024]{0:T(1024)S(1)} %convert_element_type.149, f32[1024]{0:T(1024)S(1)} %convert_element_type.148, ...), kind=kOutput, calls=%fused_computation.12 | convolution fusion | flops 8872001536 | bytes 37781504 | tf_op jit(solution)/shard_map/dot_general | solution.py:137
  495.6 28.3 %all-gather.24.cloned.1.call-done = bf16[4096,1024]{1,0:T(8,128)(2,1)} async-done(((bf16[128,1024]{1,0:T(8,128)(2,1)}), bf16[4096,1024]{1,0:T(8,128)(2,1)}) %all-gather.24.cloned.1.call-update) | async-done | bytes 8388624 | tf_op jit(solution)/shard_map/all_gather | solution.py:80
  524.0 15.0 fusion.74
  541.3 6.6 multiply_reduce_fusion.1
  549.8 20.3 %convert_reduce_fusion = (f32[4096]{0:T(1024)}, bf16[1024,4096]{1,0:T(8,128)(2,1)}) fusion(f32[1024,4096]{1,0:T(8,128)} %get-tuple-element.111, f32[4096]{0:T(1024)S(1)} %bitcast.138, bf16[4096,1024]{1,0:T(8,128)(2,1)S(1)} %bitcast.141, f32[1024,1024]{1,0:T(8,128)S(1)} %get-tuple-element.97), kind=kOutput, calls=%fused_computation.20 | convolution fusion | flops 8645505024 | bytes 37781504 | tf_op jit(solution)/shard_map/dot_general | solution.py:40
  570.1 15.9 multiply_reduce_fusion.2
  596.5 15.9 fusion.30
  612.4 11.5 copy.85
  628.0 27.9 %multiply_convert_fusion = bf16[8,16,128,512]{3,2,1,0:T(8,128)(2,1)} fusion(f32[8,16,128,512]{3,2,1,0:T(8,128)} %get-tuple-element.105, f32[8,16,128]{2,1,0:T(8,128)S(1)} %multiply_reduce_fusion, f32[8,16,128]{2,1,0:T(8,128)S(1)} %copy-done.16, pred[8,512]{1,0:T(8,128)(4,1)S(1)} %copy-done.15, bf16[8,512,16,64]{1,3,2,0:T(8,128)(2,1)} %bitcast.124, ...), kind=kOutput, calls=%fused_computation | convolution fusion | flops 1132462080 | bytes 60952576 | tf_op jit(solution)/shard_map/sqhd,skhd->shqk/dot_general | solution.py:206
  655.9 11.7 multiply_convert_fusion.1
  667.7 11.5 copy.83
  680.7 6.5 fusion.43
  687.5 11.7 fusion.39
  701.0 4.6 convolution_bitcast_fusion.2
  705.6 6.0 copy.99
  711.7 6.8 convolution_bitcast_fusion
  718.6 5.4 copy.103
  724.1 44.6 %reduce-scatter.15.cloned.1.call-done = bf16[8,128,1024]{2,1,0:T(8,128)(2,1)} async-done(((bf16[8,512,1024]{2,1,0:T(8,128)(2,1)}), bf16[8,128,1024]{2,1,0:T(8,128)(2,1)}) %reduce-scatter.15.cloned.1.call-update) | async-done | bytes 2097168 | tf_op jit(solution)/shard_map/reduce_scatter | solution.py:220
  768.7 6.6 convolution_bitcast_fusion.1
  775.3 5.4 copy.101
  781.4 16.8 fusion.67
  798.3 16.5 fusion.58
  815.5 40.4 %all-reduce.11 = (f32[]{:T(128)}, f32[1024]{0:T(1024)S(1)}, f32[1024]{0:T(1024)S(1)}, f32[4096]{0:T(1024)S(1)}, f32[1024]{0:T(1024)S(1)}, /*index=5*/f32[1024]{0:T(1024)S(1)}, f32[1024]{0:T(1024)S(1)}) all-reduce(f32[]{:T(128)} %get-tuple-element.79, f32[1024]{0:T(1024)S(1)} %copy-done.26, ...), channel_id=1, replica_groups=mesh['dp'=8,'blk'=4] {'dp','blk'}, use_global_device_ids=true, to_apply=%region_7.8 | all-reduce | flops 9217 | bytes 73736 | tf_op jit(solution)/shard_map/psum | solution.py:149
  860.1 4.1 fusion.41
  867.8 4.5 add_add_fusion
  872.3 40.7 %reduce-scatter.19.cloned.1.call-done = f32[32,1024]{1,0:T(8,128)} async-done(((f32[1024,1024]{1,0:T(8,128)}), f32[32,1024]{1,0:T(8,128)}) %reduce-scatter.19.cloned.1.call-update) | async-done | bytes 131088 | tf_op jit(solution)/shard_map/reduce_scatter | solution.py:237
  913.0 139.9 %reduce-scatter.25.cloned.1.call-done = f32[32,1024]{1,0:T(8,128)} async-done(((f32[1024,1024]{1,0:T(8,128)}), f32[32,1024]{1,0:T(8,128)}) %reduce-scatter.25.cloned.1.call-update) | async-done | bytes 131088
  1052.9 140.1 %reduce-scatter.29.cloned.1.call-done = f32[32,1024]{1,0:T(8,128)} async-done(((f32[1024,1024]{1,0:T(8,128)}), f32[32,1024]{1,0:T(8,128)}) %reduce-scatter.29.cloned.1.call-update) | async-done | bytes 131088
  1193.0 140.2 %reduce-scatter.27.cloned.1.call-done = f32[32,1024]{1,0:T(8,128)} async-done(((f32[1024,1024]{1,0:T(8,128)}), f32[32,1024]{1,0:T(8,128)}) %reduce-scatter.27.cloned.1.call-update) | async-done | bytes 131088
  1333.2 181.6 %reduce-scatter.21.cloned.1.call-done = f32[32,4096]{1,0:T(8,128)} async-done(((f32[1024,4096]{1,0:T(8,128)}), f32[32,4096]{1,0:T(8,128)}) %reduce-scatter.21.cloned.1.call-update) | async-done | bytes 524304 | tf_op jit(solution)/shard_map/reduce_scatter | solution.py:170
  1514.8 187.3 %reduce-scatter.23.cloned.1.call-done = f32[128,1024]{1,0:T(8,128)} async-done(((f32[4096,1024]{1,0:T(8,128)}), f32[128,1024]{1,0:T(8,128)}) %reduce-scatter.23.cloned.1.call-update) | async-done | bytes 524304 | tf_op jit(solution)/shard_map/reduce_scatter | solution.py:172
  (173 shorter events, 49.0 us)
Async XLA Ops:
  7.2 62.8 %all-gather.12.cloned.1.call-start = ((), (), s32[]{:S(2)}) async-start(), calls=%async_computation.9 | async-start | bytes 2162688 | tf_op jit(solution)/shard_map/all_gather | solution.py:71
  7.9 120.2 %all-gather.16.cloned.1.call-start = ((), (), s32[]{:S(2)}) async-start(), calls=%async_computation.11 | async-start | bytes 2162688 | tf_op jit(solution)/shard_map/all_gather | solution.py:72
  8.7 249.8 %all-gather.10.cloned.1.call-start = ((), (), s32[]{:S(2)}) async-start(), calls=%async_computation.8 | async-start | bytes 2162688 | tf_op jit(solution)/shard_map/all_gather | solution.py:70
  9.4 263.3 %all-gather.14.cloned.1.call-start = ((), (), s32[]{:S(2)}) async-start(), calls=%async_computation.10 | async-start | bytes 10485760 | tf_op jit(solution)/shard_map/all_gather | solution.py:112
  70.0 58.1 %copy-start.32 = (bf16[8,128,1024]{2,1,0:T(8,128)(2,1)S(1)}, bf16[8,128,1024]{2,1,0:T(8,128)(2,1)}, u32[]{:S(2)}) copy-start(bf16[8,128,1024]{2,1,0:T(8,128)(2,1)} %param.16) | copy-start | bytes 6291460
  76.1 59.5 %copy-start.25 = (s32[8]{0:T(128)S(1)}, s32[8]{0:T(128)}, u32[]{:S(2)}) copy-start(s32[8]{0:T(128)} %param.17) | copy-start | bytes 100
  76.1 61.5 %copy-start.37 = (bf16[32]{0:T(256)(128)(2,1)S(1)}, bf16[32]{0:T(256)(128)(2,1)}, u32[]{:S(2)}) copy-start(bf16[32]{0:T(256)(128)(2,1)} %param.24) | copy-start | bytes 196
  76.1 61.7 %copy-start.38 = (bf16[32]{0:T(256)(128)(2,1)S(1)}, bf16[32]{0:T(256)(128)(2,1)}, u32[]{:S(2)}) copy-start(bf16[32]{0:T(256)(128)(2,1)} %param.25) | copy-start | bytes 196
  76.1 61.9 %copy-start.39 = (bf16[32]{0:T(256)(128)(2,1)S(1)}, bf16[32]{0:T(256)(128)(2,1)}, u32[]{:S(2)}) copy-start(bf16[32]{0:T(256)(128)(2,1)} %param.29) | copy-start | bytes 196
  76.1 62.2 %copy-start.40 = (bf16[32]{0:T(256)(128)(2,1)S(1)}, bf16[32]{0:T(256)(128)(2,1)}, u32[]{:S(2)}) copy-start(bf16[32]{0:T(256)(128)(2,1)} %param.30) | copy-start | bytes 196
  76.1 62.4 %copy-start.41 = (bf16[32]{0:T(256)(128)(2,1)S(1)}, bf16[32]{0:T(256)(128)(2,1)}, u32[]{:S(2)}) copy-start(bf16[32]{0:T(256)(128)(2,1)} %param.31) | copy-start | bytes 196
  76.1 101.6 %copy-start.31 = (bf16[128]{0:T(256)(128)(2,1)S(1)}, bf16[128]{0:T(256)(128)(2,1)}, u32[]{:S(2)}) copy-start(bf16[128]{0:T(256)(128)(2,1)} %param.27) | copy-start | bytes 772
  76.1 240.7 %all-gather.18.cloned.1.call-start = ((), (), s32[]{:S(2)}) async-start(), calls=%async_computation.12 | async-start | bytes 10485760 | tf_op jit(solution)/shard_map/all_gather | solution.py:113
  133.4 232.2 %all-gather.20.cloned.1.call-start = ((), (), s32[]{:S(2)}) async-start(), calls=%async_computation.13 | async-start | bytes 2162688 | tf_op jit(solution)/shard_map/all_gather | solution.py:73
  134.0 310.9 %all-gather.22.cloned.1.call-start = ((), (), s32[]{:S(2)}) async-start(), calls=%async_computation.14 | async-start | bytes 8650752 | tf_op jit(solution)/shard_map/all_gather | solution.py:78
  134.8 389.2 %all-gather.24.cloned.1.call-start = ((), (), s32[]{:S(2)}) async-start(), calls=%async_computation.15 | async-start | bytes 8650752 | tf_op jit(solution)/shard_map/all_gather | solution.py:80
  135.5 576.2 %reduce-scatter.17.cloned.1.call-start = ((), (), s32[]{:S(2)}) async-start(), calls=%async_computation.17 | async-start | bytes 10485760 | tf_op jit(solution)/shard_map/reduce_scatter | solution.py:223
  135.7 192.6 %copy-start.14 = (pred[8,512]{1,0:T(8,128)(4,1)}, pred[8,512]{1,0:T(8,128)(4,1)S(1)}, u32[]{:S(2)}) copy-start(pred[8,512]{1,0:T(8,128)(4,1)S(1)} %iota_compare_fusion) | copy-start | bytes 12292
  177.7 346.3 %copy-start.28 = (f32[1024]{0:T(1024)}, f32[1024]{0:T(1024)S(1)}, u32[]{:S(2)}) copy-start(f32[1024]{0:T(1024)S(1)} %convert_element_type.149) | copy-start | bytes 12292
  272.7 12.1 copy-start
  347.5 23.0 %copy-start.12 = (bf16[8,128,16,64]{1,0,3,2:T(8,128)(2,1)}, bf16[8,128,16,64]{1,0,3,2:T(8,128)(2,1)S(1)}, u32[]{:S(2)}) copy-start(bf16[8,128,16,64]{1,0,3,2:T(8,128)(2,1)S(1)} %copy.78) | copy-start | bytes 6291460
  444.9 79.1 %copy-start.30 = (f32[1024]{0:T(1024)S(1)}, f32[1024]{0:T(1024)}, u32[]{:S(2)}) copy-start(f32[1024]{0:T(1024)} %convert_element_type.153) | copy-start | bytes 12292
  539.0 2.2 copy-start.9
  539.0 2.2 copy-start.17
  539.0 2.2 copy-start.21
  539.1 2.2 copy-start.22
  539.1 2.2 copy-start.23
  539.1 10.7 slice-start
  541.3 8.5 slice-start.1
  549.8 20.3 %copy-start.6 = (f32[1024,1024]{1,0:T(8,128)}, f32[1024,1024]{1,0:T(8,128)S(1)}, u32[]{:S(2)}) copy-start(f32[1024,1024]{1,0:T(8,128)S(1)} %get-tuple-element.97) | copy-start | bytes 12582916
  549.8 20.3 %copy-start.5 = (f32[1024,1024]{1,0:T(8,128)S(1)}, f32[1024,1024]{1,0:T(8,128)}, u32[]{:S(2)}) copy-start(f32[1024,1024]{1,0:T(8,128)} %copy-done.4) | copy-start | bytes 12582916
  586.0 3.3 copy-start.35
  591.7 4.8 copy-start.15
  591.7 4.8 copy-start.16
  623.9 144.8 %reduce-scatter.15.cloned.1.call-start = ((), (), s32[]{:S(2)}) async-start(), calls=%async_computation.16 | async-start | bytes 10485760 | tf_op jit(solution)/shard_map/reduce_scatter | solution.py:220
  624.1 2.2 copy-start.7
  628.0 27.9 %copy-start.1 = (bf16[8,128,16,64]{1,3,2,0:T(8,128)(2,1)S(1)}, bf16[8,128,16,64]{1,3,2,0:T(8,128)(2,1)}, u32[]{:S(2)}) copy-start(bf16[8,128,16,64]{1,3,2,0:T(8,128)(2,1)} %copy-done) | copy-start | bytes 6291460
  679.2 233.8 %reduce-scatter.19.cloned.1.call-start = ((), (), s32[]{:S(2)}) async-start(), calls=%async_computation.18 | async-start | bytes 4325376 | tf_op jit(solution)/shard_map/reduce_scatter | solution.py:237
  687.2 365.7 %reduce-scatter.25.cloned.1.call-start = ((), (), s32[]{:S(2)}) async-start(), calls=%async_computation.21 | async-start | bytes 4325376
  711.6 481.3 %reduce-scatter.29.cloned.1.call-start = ((), (), s32[]{:S(2)}) async-start(), calls=%async_computation.23 | async-start | bytes 4325376
  724.0 609.1 %reduce-scatter.27.cloned.1.call-start = ((), (), s32[]{:S(2)}) async-start(), calls=%async_computation.22 | async-start | bytes 4325376
  780.7 734.1 %reduce-scatter.21.cloned.1.call-start = ((), (), s32[]{:S(2)}) async-start(), calls=%async_computation.19 | async-start | bytes 17301504 | tf_op jit(solution)/shard_map/reduce_scatter | solution.py:170
  798.2 903.9 %reduce-scatter.23.cloned.1.call-start = ((), (), s32[]{:S(2)}) async-start(), calls=%async_computation.20 | async-start | bytes 17301504 | tf_op jit(solution)/shard_map/reduce_scatter | solution.py:172
  860.1 4.2 copy-start.34
  860.1 4.2 copy-start.36
  864.3 2.4 copy-start.3
  864.3 2.9 copy-start.10
  864.3 3.5 copy-start.11
  (12 other events, 13.8 us)
Sparse Core Ops, SparseCore 0:
  10.9 59.0 all-gather.11
  72.9 55.2 all-gather.15
  131.0 55.6 all-gather.9
  188.7 57.9 all-gather.13
  248.1 58.3 all-gather.17
  309.2 56.4 all-gather.19
  368.5 76.3 all-gather.21
  447.8 76.1 all-gather.23
  624.0 70.2 reduce-scatter.16
  697.0 71.6 reduce-scatter.14
  771.6 141.3 reduce-scatter.18
  915.7 137.1 reduce-scatter.24
  1055.8 137.1 reduce-scatter.28
  1195.7 137.4 reduce-scatter.26
  1335.9 178.8 reduce-scatter.20
  1517.5 184.5 reduce-scatter.22
where the time goes:
time: 1720 us; the launch traced here: 1710 us
  waiting for transfers between devices  1110 us (65%)
  matrix products  296 us (17%)
  blocking collectives  158 us (9%)
  local copies, waits for them, and re-layouts  96 us (6%)
  other arithmetic  32.7 us (2%)
  between operations  17.2 us (1%)
    unnamed x19, waiting for transfers between devices  424 us
    reduce_scatter x1, waiting for transfers between devices, shards(): lax.psum_scatter(grad_w_outer, ('dp', 'blk'), scatter_dimension=0, tiled=...  187 us
    reduce_scatter x1, waiting for transfers between devices, shards(): lax.psum_scatter(grad_w_inner, ('dp', 'blk'), scatter_dimension=0, tiled=...  182 us
    psum x2, blocking collectives, shards(): lax.psum((square_part, count_part), ('dp', 'blk'))  78.4 us
    all_gather x1, waiting for transfers between devices, shards(): lax.all_gather(w_inner, ('dp', 'blk'), axis=0, tiled=True)  71.9 us
    all_gather x1, waiting for transfers between devices, shards(): lax.all_gather(w_key, ('dp', 'blk'), axis=0, tiled=True)  60.6 us
    dot_general x6, matrix products, matmul_t(): lax.dot_general(left, right, (((0,), (0,)), ((), ())), preferred_element_...  57.9 us
    all_gather x1, waiting for transfers between devices, shards(): lax.all_gather(w_value, ('dp', 'blk'), axis=0, tiled=True)  52 us
  transfers between devices with their start and end apart: 16, of which 12 were waited for; matrix products, arithmetic and copies ran while one was open for 19% of the time, Pallas kernels for 0%

commit v1 on v0

v1 whole, which is shorter than its diff:
```python
import math

import jax
import jax.numpy as jnp
from jax import lax
from jax.experimental import pallas as pl
from jax.experimental.pallas import tpu as pltpu
from jax.sharding import PartitionSpec as P

ANY = pl.BlockSpec(memory_space=pl.ANY)
MESH = pl.DeviceIdType.MESH
f32 = jnp.float32
bf16 = jnp.bfloat16


class Layout:
    def __init__(self, mesh):
        dp, blk = mesh.shape["dp"], mesh.shape["blk"]
        if dp == 8 and blk == 4:
            dims = [("z", "dp", 2, 4), ("x", "dp", 1, 2), ("y", "blk", 2, 2), ("c", "blk", 1, 2)]
        else:
            dims = [("z", "dp", dp // 4, 4), ("x", "dp", 2, dp // 8), ("c", "dp", 1, 2), ("y", "blk", 1, blk)]
        self.order = [d[0] for d in dims]
        self.axis = {d[0]: d[1] for d in dims}
        self.stride = {d[0]: d[2] for d in dims}
        self.size = {d[0]: d[3] for d in dims}
        self.dims = tuple(d[3] for d in dims)
        self.blk = blk
        self.devices = dp * blk
        self.slot = {}
        count = 0
        for name in self.order:
            self.slot[name] = count
            count += self.size[name] - 1
        self.slots = count

    def here(self):
        return {
            name: lax.rem(lax.axis_index(self.axis[name]) // self.stride[name], self.size[name])
            for name in self.order
        }

    def step_to(self, here, name, distance):
        there = lax.rem(here[name] + distance, self.size[name])
        index = lax.axis_index(self.axis[name]) + (there - here[name]) * self.stride[name]
        return there, {self.axis[name]: index}

    def at(self, here, whole, changed=(), names=None):
        changed = dict(changed)
        return tuple(
            slice(None) if name in whole else changed.get(name, here[name])
            for name in (names or self.order)
        )

    def greet(self, here):
        barrier = pltpu.get_barrier_semaphore()
        count = 0
        for name in self.order:
            if self.axis[name] == "blk":
                continue
            for distance in range(1, self.size[name]):
                _, device = self.step_to(here, name, distance)
                pl.semaphore_signal(barrier, inc=1, device_id=device, device_id_type=MESH)
                count += 1
        me = lax.axis_index("blk")
        for distance in range(1, self.blk):
            pl.semaphore_signal(
                barrier, inc=1, device_id={"blk": lax.rem(me + distance, self.blk)}, device_id_type=MESH
            )
            count += 1
        pl.semaphore_wait(barrier, count)


def by_core(here, orders, make):
    if orders[0] == orders[1]:
        make(orders[0])
        return
    for core in range(2):
        @pl.when(here["c"] == core)
        def _():
            make(orders[core])


class Gather:
    stages = 5

    def __init__(self, lay, here, src, full, rows, send, recv, own, orders):
        self.lay, self.here = lay, here
        self.rows = (pl.ds(*rows),)
        self.src, self.full = src.at[self.rows], full
        self.send, self.recv, self.own = send, recv, own
        self.orders = orders

    def line(self, name, whole):
        copies = []
        place = self.full.at[self.lay.at(self.here, whole) + self.rows]
        source = self.src if not whole else place
        for distance in range(1, self.lay.size[name]):
            _, device = self.lay.step_to(self.here, name, distance)
            slot = self.lay.slot[name] + distance - 1
            copies.append(
                pltpu.make_async_remote_copy(
                    src_ref=source, dst_ref=place, send_sem=self.send.at[slot], recv_sem=self.recv.at[slot],
                    device_id=device, device_id_type=MESH,
                )
            )
        return copies

    def local(self):
        return pltpu.make_async_copy(self.src, self.full.at[self.lay.at(self.here, ()) + self.rows], self.own)

    def stage(self, k):
        if k == 1:
            self.local().wait()

        def make(order):
            lines = tuple(order) + ("c",)
            if k > 0:
                for c in self.line(lines[k - 1], lines[: k - 1]):
                    c.wait_recv()
            if k < 4:
                for c in self.line(lines[k], lines[:k]):
                    c.start()

        if k == 0:
            self.local().start()
        by_core(self.here, self.orders, make)

    def drain(self):
        def make(order):
            lines = tuple(order) + ("c",)
            for k in range(4):
                for c in self.line(lines[k], lines[:k]):
                    c.wait_send()
        by_core(self.here, self.orders, make)


class Resplit:
    def __init__(self, lay, src, dst, send, recv, own, back=False):
        self.lay, self.src, self.dst = lay, src, dst
        self.send, self.recv, self.own = send, recv, own
        self.me = lax.axis_index("blk")
        self.back = back
        self.seqs = (src if back else dst).shape[0]
        self.span = (dst if back else src).shape[1]

    def ends(self, there):
        if self.back:
            return (self.src.at[:, pl.ds(there * self.span, self.span)],
                    self.dst.at[pl.ds(self.me * self.seqs, self.seqs)])
        return (self.src.at[pl.ds(there * self.seqs, self.seqs)],
                self.dst.at[:, pl.ds(self.me * self.span, self.span)])

    def copies(self):
        out = []
        for distance in range(1, self.lay.blk):
            there = lax.rem(self.me + distance, self.lay.blk)
            src, dst = self.ends(there)
            out.append(
                pltpu.make_async_remote_copy(
                    src_ref=src, dst_ref=dst,
                    send_sem=self.send.at[distance - 1], recv_sem=self.recv.at[distance - 1],
                    device_id={"blk": there}, device_id_type=MESH,
                )
            )
        return out

    def local(self):
        src, dst = self.ends(self.me)
        return pltpu.make_async_copy(src, dst, self.own)

    def start(self):
        self.local().start()
        for c in self.copies():
            c.start()

    def finish(self):
        self.local().wait()
        for c in self.copies():
            c.wait()


class Scatter:
    stages = 5

    def __init__(self, lay, here, grad, out, rows, bufs, send, recv, own, orders):
        self.lay, self.here, self.grad = lay, here, grad
        self.rows = (pl.ds(*rows),)
        self.out = out.at[self.rows]
        self.held, self.recvs = bufs[0], bufs[1:]
        self.send, self.recv, self.own = send, recv, own
        self.orders = orders
        self.names = [n for n in lay.order if n != "c"]

    @staticmethod
    def buffers(lay, shard, orders):
        shape, dtype = tuple(shard.shape), shard.dtype
        names = [n for n in lay.order if n != "c"]
        out = [pltpu.VMEM(tuple(lay.size[n] for n in names) + shape, dtype)]
        out.append(pltpu.VMEM(tuple(lay.size[n] for n in names) + shape, dtype))
        for k in range(3):
            lines = orders[0][k + 1 :]
            left = tuple(lay.size[n] for n in names if n in lines)
            out.append(pltpu.VMEM((lay.size[orders[0][k]] - 1,) + left + shape, dtype))
        return out

    def local(self):
        return pltpu.make_async_copy(
            self.grad.at[self.lay.at(self.here, self.names) + self.rows], self.held, self.own)

    def core(self):
        there, device = self.lay.step_to(self.here, "c", 1)
        slot = self.lay.slot["c"]
        return pltpu.make_async_remote_copy(
            src_ref=self.grad.at[self.lay.at(self.here, self.names, {"c": there}) + self.rows], dst_ref=self.recvs[0],
            send_sem=self.send.at[slot], recv_sem=self.recv.at[slot], device_id=device, device_id_type=MESH)

    def line(self, order, k):
        name, left = order[k], order[k + 1 :]
        copies = []
        for distance in range(1, self.lay.size[name]):
            there, device = self.lay.step_to(self.here, name, distance)
            slot = self.lay.slot[name] + distance - 1
            copies.append(
                pltpu.make_async_remote_copy(
                    src_ref=self.held.at[self.lay.at(self.here, left, {name: there}, self.names)],
                    dst_ref=self.recvs[k + 1].at[distance - 1],
                    send_sem=self.send.at[slot], recv_sem=self.recv.at[slot],
                    device_id=device, device_id_type=MESH,
                )
            )
        return copies

    def add(self, order, k):
        left = [n for n in self.names if k < 0 or n in order[k + 1 :]]
        sizes = [self.lay.size[n] for n in left]
        total = 1
        for s in sizes:
            total *= s
        buf = self.recvs[k + 1]
        many = 1 if k < 0 else self.lay.size[order[k]] - 1

        def one(i, carry):
            index, rest = {}, i
            for n, s in reversed(list(zip(left, sizes))):
                index[n] = lax.rem(rest, s)
                rest = rest // s
            mine = tuple(index.get(n, self.here[n]) for n in self.names)
            theirs = tuple(index[n] for n in left)
            value = self.held[mine].astype(f32)
            for d in range(many):
                at = theirs if k < 0 else (d,) + theirs
                value = value + buf[at].astype(f32)
            if k == 2:
                self.out[...] = value
            else:
                self.held[mine] = value.astype(self.held.dtype)
            return carry

        lax.fori_loop(0, total, one, 0)

    def stage(self, k):
        if k == 0:
            self.core().start()
            self.local().start()
            return
        if k == 1:
            self.local().wait()
            self.core().wait_recv()
            self.add(None, -1)

        def make(order):
            if k > 1:
                for c in self.line(order, k - 2):
                    c.wait_recv()
                self.add(order, k - 2)
            if k < 4:
                for c in self.line(order, k - 1):
                    c.start()

        by_core(self.here, self.orders, make)

    def drain(self):
        self.core().wait_send()

        def make(order):
            for k in range(3):
                for c in self.line(order, k):
                    c.wait_send()

        by_core(self.here, self.orders, make)


def skewed(parts, stages=5):
    for t in range(len(parts) + stages - 1):
        for i, part in enumerate(parts):
            if 0 <= t - i < stages:
                part.stage(t - i)
    for part in parts:
        part.drain()


def sems(lay, n, m):
    dma = pltpu.SemaphoreType.DMA
    n, m = max(n, 1), max(m, 1)
    return [dma((n, lay.slots)), dma((n, lay.slots)), dma((n,)), dma((m, lay.blk - 1)), dma((m, lay.blk - 1)), dma((m,))]


def gather_call(lay, shards, parts, rows, cid):
    n, m, p = len(shards), len(rows), len(parts)

    def kernel(*refs):
        ins, refs = refs[: n + m], refs[n + m :]
        outs, refs = refs[: n + m], refs[n + m :]
        send, recv, own, rsend, rrecv, rown = refs
        here = lay.here()
        lay.greet(here)
        gathers = [
            Gather(lay, here, ins[a], outs[a], (r, c), send.at[i], recv.at[i], own.at[i], orders)
            for i, (a, r, c, orders) in enumerate(parts)
        ]
        splits = [Resplit(lay, ins[n + i], outs[n + i], rsend.at[i], rrecv.at[i], rown.at[i]) for i in range(m)]
        for s in splits:
            s.start()
        skewed(gathers)
        for s in splits:
            s.finish()

    outs = [jax.ShapeDtypeStruct(lay.dims + s.shape, s.dtype) for s in shards]
    outs += [
        jax.ShapeDtypeStruct((r.shape[0] // lay.blk, r.shape[1] * lay.blk, r.shape[2]), r.dtype) for r in rows
    ]
    return pl.pallas_call(
        kernel, out_shape=outs, in_specs=[ANY] * (n + m), out_specs=[ANY] * (n + m),
        scratch_shapes=sems(lay, p, m),
        compiler_params=pltpu.CompilerParams(collective_id=cid, has_side_effects=True),
        name=f"gather_{cid}",
    )(*shards, *rows)


def scatter_call(lay, grads, parts, rows, cid):
    n, m, p = len(grads), len(rows), len(parts)
    bufs = [
        Scatter.buffers(lay, jax.ShapeDtypeStruct((c,) + grads[a].shape[2:], grads[a].dtype), orders)
        for a, r, c, orders in parts
    ]

    def kernel(*refs):
        ins, refs = refs[: n + m], refs[n + m :]
        outs, refs = refs[: n + m], refs[n + m :]
        own_bufs = []
        for _ in parts:
            own_bufs.append(refs[:5])
            refs = refs[5:]
        send, recv, own, rsend, rrecv, rown = refs
        here = lay.here()
        lay.greet(here)
        sums = [
            Scatter(lay, here, ins[a], outs[a], (r, c), own_bufs[i], send.at[i], recv.at[i], own.at[i], orders)
            for i, (a, r, c, orders) in enumerate(parts)
        ]
        splits = [
            Resplit(lay, ins[n + i], outs[n + i], rsend.at[i], rrecv.at[i], rown.at[i], True) for i in range(m)
        ]
        for s in splits:
            s.start()
        skewed(sums)
        for s in splits:
            s.finish()

    outs = [jax.ShapeDtypeStruct(g.shape[1:], f32) for g in grads]
    outs += [
        jax.ShapeDtypeStruct((r.shape[0] * lay.blk, r.shape[1] // lay.blk, r.shape[2]), r.dtype) for r in rows
    ]
    grads = [g.reshape(lay.dims + g.shape[1:]) for g in grads]
    return pl.pallas_call(
        kernel, out_shape=outs, in_specs=[ANY] * (n + m),
        out_specs=[pl.BlockSpec(memory_space=pltpu.VMEM)] * n + [ANY] * m,
        scratch_shapes=[b for bs in bufs for b in bs] + sems(lay, p, m),
        compiler_params=pltpu.CompilerParams(
            collective_id=cid, has_side_effects=True, vmem_limit_bytes=60 << 20),
        name=f"scatter_{cid}",
    )(*grads, *rows)


DH = 64
LOG2E = math.log2(math.e)
GROUP = 256


def dot(a, b):
    return lax.dot_general(a, b, (((1,), (0,)), ((), ())), preferred_element_type=f32)


def dot_t(a, b):
    return lax.dot_general(a, b, (((1,), (1,)), ((), ())), preferred_element_type=f32)


def once(shape):
    return pl.BlockSpec(shape, lambda *_: (0,) * len(shape), pipeline_mode=pl.Buffered(1))


def attention_forward(x, lengths, wq, wk, wv, wo):
    rows, width = x.shape
    seqs = lengths.shape[0]
    span = rows // seqs
    groups = width // GROUP
    scale = LOG2E / math.sqrt(DH)

    def kernel(len_ref, x_ref, wq_ref, wk_ref, wv_ref, wo_ref, q_ref, k_ref, v_ref, att_ref, lse_ref, h1_ref):
        g = pl.program_id(0)
        xv = x_ref[...]
        q_ref[...] = dot(xv, wq_ref[...]).astype(bf16)
        k_ref[...] = dot(xv, wk_ref[...]).astype(bf16)
        v_ref[...] = dot(xv, wv_ref[...]).astype(bf16)

        def pair_step(i, carry):
            s, pair = i // 2, lax.rem(i, 2)
            at = (pl.ds(pl.multiple_of(s * span, span), span), pl.ds(pl.multiple_of(pair * 128, 128), 128))
            length = len_ref[s]
            qs, ks, vs = q_ref[at], k_ref[at], v_ref[at]
            lane = lax.broadcasted_iota(jnp.int32, (span, 128), 1)
            keep = lax.broadcasted_iota(jnp.int32, (span, 1), 0) < length
            vt = vs.T
            outs, lses = [], []
            for h in range(2):
                km = jnp.where((lane < DH) if h == 0 else (lane >= DH), ks, jnp.zeros_like(ks))
                st = dot_t(km, qs) * scale
                st = jnp.where(keep, st, -1e30)
                top = jnp.max(st, axis=0, keepdims=True)
                p = jnp.exp2(st - top)
                den = jnp.sum(p, axis=0, keepdims=True)
                ot = dot(vt[h * DH : (h + 1) * DH], p.astype(bf16))
                outs.append(ot * (1.0 / den))
                lses.append(top + jnp.log2(den))
            att_ref[at] = jnp.concatenate(outs, axis=0).T.astype(bf16)
            lse_ref[0, pl.ds(i * 2, 1)] = lses[0]
            lse_ref[0, pl.ds(i * 2 + 1, 1)] = lses[1]
            return carry

        lax.fori_loop(0, seqs * GROUP // 128, pair_step, 0)

        @pl.when(g == 0)
        def _():
            h1_ref[...] = x_ref[...].astype(f32)

        h1_ref[...] += dot(att_ref[...], wo_ref[...])

    col = pl.BlockSpec((width, GROUP), lambda g, *_: (0, g))
    act = pl.BlockSpec((rows, GROUP), lambda g, *_: (0, g))
    heads = seqs * GROUP // DH
    return pl.pallas_call(
        kernel,
        grid_spec=pltpu.PrefetchScalarGridSpec(
            num_scalar_prefetch=1,
            grid=(groups,),
            in_specs=[once((rows, width)), col, col, col, pl.BlockSpec((GROUP, width), lambda g, *_: (g, 0))],
            out_specs=[act, act, act, act, pl.BlockSpec((1, heads, span), lambda g, *_: (g, 0, 0)), once((rows, width))],
        ),
        out_shape=[jax.ShapeDtypeStruct((rows, width), bf16)] * 4
        + [jax.ShapeDtypeStruct((groups, heads, span), f32), jax.ShapeDtypeStruct((rows, width), f32)],
        compiler_params=pltpu.CompilerParams(vmem_limit_bytes=60 << 20),
        name="attention_forward",
    )(lengths, x, wq, wk, wv, wo)


def attention_backward(x, lengths, wq, wk, wv, wo, q, k, v, att, lse, d_branch, d_one):
    rows, width = x.shape
    seqs = lengths.shape[0]
    span = rows // seqs
    groups = width // GROUP
    scale = LOG2E / math.sqrt(DH)

    def kernel(
        len_ref, x_ref, wq_ref, wk_ref, wv_ref, wo_ref, q_ref, k_ref, v_ref, att_ref, lse_ref, db_ref, d1_ref,
        gq_ref, gk_ref, gv_ref, go_ref, dx_ref, xt_ref, do_ref, dq_ref, dk_ref, dv_ref, acc_ref,
    ):
        g = pl.program_id(0)

        @pl.when(g == 0)
        def _():
            xt_ref[...] = x_ref[...].T
            acc_ref[...] = d1_ref[...]

        db = db_ref[...]
        do_ref[...] = dot_t(db, wo_ref[...]).astype(bf16)
        go_ref[...] = dot(att_ref[...].T, db).astype(bf16)

        def pair_step(i, carry):
            s, pair = i // 2, lax.rem(i, 2)
            at = (pl.ds(pl.multiple_of(s * span, span), span), pl.ds(pl.multiple_of(pair * 128, 128), 128))
            length = len_ref[s]
            qs, ks, vs, dos = q_ref[at], k_ref[at], v_ref[at], do_ref[at]
            lane = lax.broadcasted_iota(jnp.int32, (span, 128), 1)
            keep = lax.broadcasted_iota(jnp.int32, (span, 1), 0) < length
            kt = ks.T
            dqs, dks, dvs = [], [], []
            for h in range(2):
                mine = (lane < DH) if h == 0 else (lane >= DH)
                zero = jnp.zeros_like(ks)
                st = dot_t(jnp.where(mine, ks, zero), qs) * scale
                p = jnp.where(keep, jnp.exp2(st - lse_ref[0, pl.ds(i * 2 + h, 1)]), 0.0)
                dp = dot_t(jnp.where(mine, vs, zero), dos)
                delta = jnp.sum(p * dp, axis=0, keepdims=True)
                ds = (p * (dp - delta)).astype(bf16)
                dvs.append(dot(p.astype(bf16), dos))
                dks.append(dot(ds, qs))
                dqs.append(dot(kt[h * DH : (h + 1) * DH], ds))
            first = lane < DH
            unit = 1.0 / math.sqrt(DH)
            dv_ref[at] = jnp.where(first, dvs[0], dvs[1]).astype(bf16)
            dk_ref[at] = (jnp.where(first, dks[0], dks[1]) * unit).astype(bf16)
            dq_ref[at] = (jnp.concatenate(dqs, axis=0).T * unit).astype(bf16)
            return carry

        lax.fori_loop(0, seqs * GROUP // 128, pair_step, 0)
        xt = xt_ref[...]
        gq_ref[...] = dot(xt, dq_ref[...]).astype(bf16)
        gk_ref[...] = dot(xt, dk_ref[...]).astype(bf16)
        gv_ref[...] = dot(xt, dv_ref[...]).astype(bf16)

        acc_ref[...] += (
            dot_t(dq_ref[...], wq_ref[...]) + dot_t(dk_ref[...], wk_ref[...]) + dot_t(dv_ref[...], wv_ref[...])
        )

        @pl.when(g == groups - 1)
        def _():
            dx_ref[...] = acc_ref[...].astype(bf16)

    col = pl.BlockSpec((width, GROUP), lambda g, *_: (0, g))
    row = pl.BlockSpec((GROUP, width), lambda g, *_: (g, 0))
    act = pl.BlockSpec((rows, GROUP), lambda g, *_: (0, g))
    heads = seqs * GROUP // DH
    full = once((rows, width))
    return pl.pallas_call(
        kernel,
        grid_spec=pltpu.PrefetchScalarGridSpec(
            num_scalar_prefetch=1,
            grid=(groups,),
            in_specs=[full, col, col, col, row, act, act, act, act,
                      pl.BlockSpec((1, heads, span), lambda g, *_: (g, 0, 0)), full, full],
            out_specs=[col, col, col, row, full],
            scratch_shapes=[pltpu.VMEM((width, rows), bf16)] + [pltpu.VMEM((rows, GROUP), bf16)] * 4
            + [pltpu.VMEM((rows, width), f32)],
        ),
        out_shape=[jax.ShapeDtypeStruct((width, width), bf16)] * 4 + [jax.ShapeDtypeStruct((rows, width), bf16)],
        compiler_params=pltpu.CompilerParams(vmem_limit_bytes=60 << 20),
        name="attention_backward",
    )(lengths, x, wq, wk, wv, wo, q, k, v, att, lse, d_branch, d_one)


TILE = 512
CHUNK = 256


def feed_forward(h1, teacher, out_grad, lengths, inv_count, vecs, bias_inner, w1, w2, devices):
    rows, width = h1.shape
    hidden = w1.shape[1]
    seqs = lengths.shape[0]
    span = rows // seqs
    tiles = hidden // TILE
    share = hidden // devices
    per_tile = TILE // share
    wide = share % 128 == 0

    def kernel(
        len_ref, inv_ref, h1_ref, teach_ref, og_ref, vec_ref, b1_ref, w1_ref, w2_ref,
        out_ref, d1_ref, db_ref, gw1_ref, gw2_ref, sums_ref, gb1_ref,
        low_ref, lowt_ref, act_ref, slope_ref, acc_ref, do_ref, dot_ref, inv1_ref, di_ref,
    ):
        t = pl.program_id(0)
        gain1, shift1 = vec_ref[0:1], vec_ref[1:2]
        bias2, gain2, shift2 = vec_ref[2:3], vec_ref[3:4], vec_ref[4:5]

        @pl.when(t == 0)
        def _():
            sums_ref[...] = jnp.zeros_like(sums_ref)

            def norm(i, carry):
                at = pl.ds(pl.multiple_of(i * 128, 128), 128)
                h = h1_ref[at]
                centred = h - jnp.mean(h, axis=-1, keepdims=True)
                inverse = lax.rsqrt(jnp.mean(centred * centred, axis=-1, keepdims=True) + 1e-12)
                normal = centred * inverse
                d1_ref[at] = normal
                inv1_ref[at] = inverse
                low = (normal * gain1 + shift1).astype(bf16)
                low_ref[at] = low
                lowt_ref[:, at] = low.T
                return carry

            lax.fori_loop(0, rows // 128, norm, 0)
            acc_ref[...] = jnp.zeros_like(acc_ref)

        @pl.when(t < tiles)
        def _():
            for i in range(rows // CHUNK):
                at = slice(i * CHUNK, (i + 1) * CHUNK)
                inner = dot(low_ref[at], w1_ref[...]) + b1_ref[...]
                cum = 0.5 * (1.0 + lax.erf(inner * (1.0 / math.sqrt(2.0))))
                density = jnp.exp(-0.5 * inner * inner) * (1.0 / math.sqrt(2.0 * math.pi))
                active = (inner * cum).astype(bf16)
                act_ref[t, at] = active
                slope_ref[t, at] = (cum + inner * density).astype(bf16)
                acc_ref[at] += dot(active, w2_ref[...])

        @pl.when(t == tiles)
        def _():
            inv = inv_ref[0]

            def middle(i, carry):
                at = pl.ds(pl.multiple_of(i * 128, 128), 128)
                normed = d1_ref[at] * gain1 + shift1
                h2 = normed + acc_ref[at] + bias2
                centred = h2 - jnp.mean(h2, axis=-1, keepdims=True)
                inverse = lax.rsqrt(jnp.mean(centred * centred, axis=-1, keepdims=True) + 1e-12)
                normal = centred * inverse
                result = normal * gain2 + shift2
                out_ref[at] = result.astype(bf16)
                seq = (i * 128) // span
                pos = i * 128 - seq * span + lax.broadcasted_iota(jnp.int32, (128, 1), 0)
                valid = (pos < len_ref[seq]).astype(f32)
                deviation = (result - teach_ref[at].astype(f32)) * valid
                grad = og_ref[at].astype(f32) * valid + (2.0 * inv) * deviation
                sums_ref[0:1] += jnp.sum(deviation * deviation, axis=0, keepdims=True)
                sums_ref[1:2] += jnp.sum(grad * normal, axis=0, keepdims=True)
                sums_ref[2:3] += jnp.sum(grad, axis=0, keepdims=True)
                scaled = grad * gain2
                mean = jnp.mean(scaled, axis=-1, keepdims=True)
                along = jnp.mean(scaled * normal, axis=-1, keepdims=True)
                d_two = inverse * (scaled - mean - normal * along)
                acc_ref[at] = d_two
                low = d_two.astype(bf16)
                sums_ref[3:4] += jnp.sum(low.astype(f32), axis=0, keepdims=True)
                do_ref[at] = low
                dot_ref[:, at] = low.T
                return carry

            lax.fori_loop(0, rows // 128, middle, 0)

        @pl.when(t > tiles)
        def _():
            j = t - tiles - 1
            total = jnp.zeros((1, TILE), f32)
            for i in range(rows // CHUNK):
                at = slice(i * CHUNK, (i + 1) * CHUNK)
                d_act = dot_t(do_ref[at], w2_ref[...])
                d_in = (d_act * slope_ref[j, at].astype(f32)).astype(bf16)
                total += jnp.sum(d_in.astype(f32), axis=0, keepdims=True)
                di_ref[at] = d_in
                acc_ref[at] += dot_t(d_in, w1_ref[...])
            gb1_ref[...] = total
            gw1_ref[...] = dot(lowt_ref[...], di_ref[...]).astype(bf16)
            gw2 = dot(dot_ref[...], act_ref[j]).astype(bf16)
            if wide:
                for d in range(per_tile):
                    gw2_ref[d] = gw2[:, d * share : (d + 1) * share]
            else:
                gw2_ref[...] = gw2

        @pl.when(t == 2 * tiles)
        def _():
            def back(i, carry):
                at = pl.ds(pl.multiple_of(i * 128, 128), 128)
                grad, normal = acc_ref[at], d1_ref[at]
                sums_ref[4:5] += jnp.sum(grad * normal, axis=0, keepdims=True)
                sums_ref[5:6] += jnp.sum(grad, axis=0, keepdims=True)
                scaled = grad * gain1
                mean = jnp.mean(scaled, axis=-1, keepdims=True)
                along = jnp.mean(scaled * normal, axis=-1, keepdims=True)
                d_one = inv1_ref[at] * (scaled - mean - normal * along)
                d1_ref[at] = d_one
                db_ref[at] = d_one.astype(bf16)
                return carry

            lax.fori_loop(0, rows // 128, back, 0)

    def tile(t, *_):
        return jnp.where(t < tiles, t, jnp.maximum(t - tiles - 1, 0))

    def back_tile(t, *_):
        return jnp.maximum(t - tiles - 1, 0)

    full = once((rows, width))
    vec = pl.BlockSpec((1, TILE), lambda t, *_: (0, tile(t)))
    return pl.pallas_call(
        kernel,
        grid_spec=pltpu.PrefetchScalarGridSpec(
            num_scalar_prefetch=2,
            grid=(2 * tiles + 1,),
            in_specs=[
                full, full, full, once((8, width)), vec,
                pl.BlockSpec((width, TILE), lambda t, *_: (0, tile(t))),
                pl.BlockSpec((TILE, width), lambda t, *_: (tile(t), 0)),
            ],
            out_specs=[
                full, full, full,
                pl.BlockSpec((width, TILE), lambda t, *_: (0, back_tile(t))),
                pl.BlockSpec((per_tile, width, share), lambda t, *_: (back_tile(t), 0, 0))
                if wide else pl.BlockSpec((width, TILE), lambda t, *_: (0, back_tile(t))),
                once((8, width)),
                pl.BlockSpec((1, TILE), lambda t, *_: (0, back_tile(t))),
            ],
            scratch_shapes=[
                pltpu.VMEM((rows, width), bf16), pltpu.VMEM((width, rows), bf16),
                pltpu.VMEM((tiles, rows, TILE), bf16), pltpu.VMEM((tiles, rows, TILE), bf16),
                pltpu.VMEM((rows, width), f32), pltpu.VMEM((rows, width), bf16), pltpu.VMEM((width, rows), bf16),
                pltpu.VMEM((rows, 1), f32), pltpu.VMEM((rows, TILE), bf16),
            ],
        ),
        out_shape=[
            jax.ShapeDtypeStruct((rows, width), bf16),
            jax.ShapeDtypeStruct((rows, width), f32),
            jax.ShapeDtypeStruct((rows, width), bf16),
            jax.ShapeDtypeStruct((width, hidden), bf16),
            jax.ShapeDtypeStruct((devices, width, share) if wide else (width, hidden), bf16),
            jax.ShapeDtypeStruct((8, width), f32),
            jax.ShapeDtypeStruct((1, hidden), f32),
        ],
        compiler_params=pltpu.CompilerParams(vmem_limit_bytes=63 << 20),
        name="feed_forward",
    )(lengths, inv_count, h1, teacher, out_grad, vecs, bias_inner, w1, w2)


def cut(shape, which, pieces, orders):
    rows = shape[0]
    while pieces > 1 and rows % (pieces * 16):
        pieces -= 1
    step = rows // pieces
    return [(which, i * step, step, orders) for i in range(pieces)]


def shards(
    lay, tokens, lengths, teacher, out_grad, w_query, w_key, w_value, w_output, gain_one, shift_one,
    w_inner, bias_inner, w_outer, bias_outer, gain_two, shift_two,
):
    width = tokens.shape[2]
    hidden = w_inner.shape[1]
    devices = lay.devices
    there = (("z", "x", "y"), ("z", "y", "x"))
    back = (("y", "x", "z"), ("x", "y", "z"))
    share, deep = gain_one.shape[0], bias_inner.shape[0]

    small = jnp.concatenate(
        [v.astype(f32) for v in (gain_one, shift_one, bias_outer, gain_two, shift_two, bias_inner)]
        + [jnp.sum(lengths).astype(f32)[None]]
    )
    used = 5 * share + deep
    pack = jnp.pad(small, (0, 1024 - small.shape[0])).reshape(8, 128)
    ins = [w_query, w_key, w_value, w_output]
    parts = [(4, 0, 8, there)]
    for i, w in enumerate(ins):
        parts += cut(w.shape, i, 1, there)
    wq, wk, wv, wo, packs, x = gather_call(lay, ins + [pack], parts, [tokens], 1)
    parts = cut(w_inner.shape, 0, 2, there) + cut(w_outer.shape, 1, 2, there)
    w1, w2, teach, given = gather_call(lay, [w_inner, w_outer], parts, [teacher, out_grad], 2)
    wq, wk, wv, wo = (w.reshape(width, width) for w in (wq, wk, wv, wo))
    w1, w2 = w1.reshape(width, hidden), w2.reshape(hidden, width)
    packs = packs.reshape(devices, 1024)
    vecs = packs[:, : 5 * share].reshape(devices, 5, share).transpose(1, 0, 2).reshape(5, width)
    vecs = jnp.pad(vecs, ((0, 3), (0, 0)))
    bias1 = packs[:, 5 * share : used].reshape(1, hidden)
    inv_count = 1.0 / (jnp.sum(packs[:, used]) / lay.blk * width)

    seqs = x.shape[0]
    own = lax.dynamic_slice(lengths, (lax.axis_index("blk") * seqs,), (seqs,))
    x = x.reshape(-1, width)
    q, k, v, att, lse, h1 = attention_forward(x, own, wq, wk, wv, wo)
    out, d_one, d_branch, gw1, gw2, sums, gb1 = feed_forward(
        h1, teach.reshape(-1, width), given.reshape(-1, width), own, inv_count[None], vecs, bias1, w1, w2, devices
    )
    gq, gk, gv, go, dx = attention_backward(x, own, wq, wk, wv, wo, q, k, v, att, lse, d_branch, d_one)

    span = lambda a: a.reshape(seqs, -1, width)
    by_device = lambda a: a.reshape((devices, a.shape[0] // devices) + a.shape[1:])
    gw1 = by_device(gw1)
    turned = gw2.ndim == 3
    if not turned:
        gw2 = by_device(gw2.T)
    parts = cut(gw1.shape[1:], 0, 2, back) + cut(gw2.shape[1:], 1, 2, back)
    g_inner, g_outer, layer_out = scatter_call(lay, [gw1, gw2], parts, [span(out)], 3)
    loss = jnp.broadcast_to(jnp.sum(sums[0])[None, None], (devices, 1))
    vec_sums = sums[1:6].reshape(5, devices, share).transpose(1, 0, 2).reshape(devices, 5 * share)
    small = jnp.concatenate([vec_sums, gb1.reshape(devices, deep), loss], axis=1)
    small = jnp.pad(small, ((0, 0), (0, 1024 - small.shape[1]))).reshape(devices, 8, 128)
    grads = [by_device(g) for g in (gq, gk, gv, go)] + [small]
    parts = [(4, 0, 8, back)]
    for i in range(4):
        parts += cut(grads[i].shape[1:], i, 1, back)
    g_query, g_key, g_value, g_output, small, d_tokens = scatter_call(lay, grads, parts, [span(dx)], 4)
    small = small.reshape(1024)
    vec = lambda i: small[i * share : (i + 1) * share]
    return (
        small[used] * inv_count,
        layer_out,
        d_tokens.astype(f32),
        g_query,
        g_key,
        g_value,
        g_output,
        vec(3),
        vec(4),
        g_inner,
        small[5 * share : used],
        g_outer.T if turned else g_outer,
        vec(2),
        vec(0),
        vec(1),
    )


def solution(mesh):
    lay = Layout(mesh)
    rows = P("dp", "blk", None)
    weight = P(("dp", "blk"), None)
    vector = P(("dp", "blk"))
    return jax.shard_map(
        lambda *args: shards(lay, *args),
        mesh=mesh,
        in_specs=(
            rows, P("dp"), rows, rows, weight, weight, weight, weight, vector, vector,
            weight, vector, weight, vector, vector, vector,
        ),
        out_specs=(
            P(), rows, rows, weight, weight, weight, weight, vector, vector,
            weight, vector, weight, vector, vector, vector,
        ),
        check_vma=False,
    )
```

time: 1720 us -> 621 us (0.36)
  waiting for transfers between devices: 1110 us -> 0 us
  Pallas kernels: 0 us -> 589 us
  matrix products: 296 us -> 0 us
  blocking collectives: 158 us -> 0 us
  local copies, waits for them, and re-layouts: 96 us -> 20.9 us
  other arithmetic: 32.7 us -> 5.9 us
    pallas_call x0 -> x7, Pallas kernels: none -> 589 us  [the longest x2 206 us: gather_call(): pl.pallas_call(kernel, out_shape=outs, in_specs=[ANY] * (n + m), out_spec...]
    reduce_scatter x5 -> x0, waiting for transfers between devices: 454 us -> none  [the longest x1 187 us: shards(): lax.psum_scatter(grad_w_outer, ('dp', 'blk'), scatter_dimension=0, tiled=...]
    unnamed x19 -> x0, waiting for transfers between devices: 424 us -> none
    dot_general x24 -> x0, matrix products: 296 us -> none  [the longest x6 57.9 us: matmul_t(): lax.dot_general(left, right, (((0,), (0,)), ((), ())), preferred_element_...]
    all_gather x8 -> x0, waiting for transfers between devices: 231 us -> none  [the longest x1 71.9 us: shards(): lax.all_gather(w_inner, ('dp', 'blk'), axis=0, tiled=True)]
    psum x2 -> x0, blocking collectives: 78.4 us -> none  [shards(): lax.psum((square_part, count_part), ('dp', 'blk'))]
    all_gather x1 -> x0, blocking collectives: 40.3 us -> none  [shards(): lax.all_gather(bias_inner, ('dp', 'blk'), axis=0, tiled=True)]
    unnamed x1 -> x0, blocking collectives: 38.9 us -> none
  transfers between devices with their start and end apart: 16 -> 0, of which waited for: 12 -> 0; matrix products, arithmetic and copies ran while one was open for 19% -> 0% of each run, Pallas kernels for 0% -> 0%
where the time goes in v1:
time: 621 us; the launch traced here: 620 us
  Pallas kernels  589 us (95%)
  local copies, waits for them, and re-layouts  20.9 us (3%)
    pallas_call x2, Pallas kernels, gather_call(): pl.pallas_call(kernel, out_shape=outs, in_specs=[ANY] * (n + m), out_spec...  206 us
    pallas_call x2, Pallas kernels, scatter_call(): pl.pallas_call(kernel, out_shape=outs, in_specs=[ANY] * (n + m), out_spec...  202 us
    pallas_call x1, Pallas kernels, feed_forward(): pl.pallas_call(kernel, grid_spec=pltpu.PrefetchScalarGridSpec(num_scalar_...  87.6 us
    pallas_call x1, Pallas kernels, attention_backward(): pl.pallas_call(kernel, grid_spec=pltpu.PrefetchScalarGridSpec(num_scalar_...  58.8 us
    pallas_call x1, Pallas kernels, attention_forward(): pl.pallas_call(kernel, grid_spec=pltpu.PrefetchScalarGridSpec(num_scalar_...  35.1 us

profile of v1, /device:TPU:0, one launch (start us, length us, event | category | flops | bytes accessed | tf_op | source)
XLA Modules:
  0.0 619.9 jit_solution(14272128684179224940)
XLA Ops:
  0.6 1.3 reduce_sum.27
  2.6 1.2 dynamic_slice.3.len_ref
  3.8 4.1 concatenate.6
  7.9 0.6 pad_bitcast_fusion.1.refs_4_
  8.5 77.4 %gather_1.1 = (bf16[4,2,2,2,32,1024]{5,4,3,2,1,0:T(8,128)(2,1)}, bf16[4,2,2,2,32,1024]{5,4,3,2,1,0:T(8,128)(2,1)}, bf16[4,2,2,2,32,1024]{5,4,3,2,1,0:T(8,128)(2,...) custom-call(bf16[32,1024]{1,0:T(8,128)(2,1)} %refs_0_.2, ...), custom_call_target="tpu_custom_call" | custom-call | tf_op jit(solution)/shard_map/gather_1/pallas_call | solution.py:333
  86.0 0.9 copy.49
  86.9 0.7 slice_reduce_fusion
  88.3 0.7 slice.50
  89.0 0.1 copy.45
  89.1 0.1 copy.41
  89.2 0.1 reshape.106
  89.2 0.6 pad.13.vec_ref
  89.9 35.1 %attention_forward.1 = (bf16[1024,1024]{1,0:T(8,128)(2,1)}, bf16[1024,1024]{1,0:T(8,128)(2,1)}, bf16[1024,1024]{1,0:T(8,128)(2,1)}, bf16[1024,1024]{1,0:T(8,128)...) custom-call(s32[2]{0:T(128)} %dynamic_slice.3.len_ref, bf16[1024,1024]{1,0:T(8,128)(2,1)} %bitcast.54, ...), custom_call_target="tpu_custom_call" | custom-call | tf_op jit(solution)/shard_map/attention_forward/pallas_call | solution.py:452
  125.0 128.4 %gather_2.1 = (bf16[4,2,2,2,32,4096]{5,4,3,2,1,0:T(8,128)(2,1)}, bf16[4,2,2,2,128,1024]{5,4,3,2,1,0:T(8,128)(2,1)}, bf16[2,512,1024]{2,1,0:T(8,128)(2,1)}, bf16[2,512,1024]{2,1,0:T(8,128)(2,1)}) custom-call(bf16[32,4096]{1,0:T(8,128)(2,1)} %refs_0_.3, bf16[128,1024]{1,0:T(8,128)(2,1)} %refs_1_.3, bf16[8,128,1024]{2,1,0:T(8,128)(2,1)} %refs_2_.3, ...), custom_call_target="tpu_custom_call" | custom-call | tf_op jit(solution)/shard_map/gather_2/pallas_call | solution.py:333
  253.4 87.6 %feed_forward.1 = (bf16[1024,1024]{1,0:T(8,128)(2,1)}, f32[1024,1024]{1,0:T(8,128)}, bf16[1024,1024]{1,0:T(8,128)(2,1)}, bf16[1024,4096]{1,0:T(8,128)(2,1)}, bf1...) custom-call(s32[2]{0:T(128)} %dynamic_slice.3.len_ref, f32[1]{0:T(128)} %bitcast.7.inv_ref, ...), custom_call_target="tpu_custom_call" | custom-call | tf_op jit(solution)/shard_map/feed_forward/pallas_call | solution.py:686
  341.1 1.4 slice_reduce_fusion.1
  342.4 0.0 copy-start.7
  342.4 58.8 %attention_backward.1 = (bf16[1024,1024]{1,0:T(8,128)(2,1)}, bf16[1024,1024]{1,0:T(8,128)(2,1)}, bf16[1024,1024]{1,0:T(8,128)(2,1)}, bf16[1024,1024]{1,0:T(8,128)(2,1)}, bf16[1024,1024]{1,0:T(8,128)(2,1)}) custom-call(s32[2]{0:T(128)} %dynamic_slice.3.len_ref, bf16[1024,1024]{1,0:T(8,128)(2,1)} %bitcast.55, bf16[1024,1024]{1,0:T(8,128)(2,1)} %bitcast.47, ...), custom_call_target="tpu_custom_call" | custom-call | tf_op jit(solution)/shard_map/attention_backward/pallas_call | solution.py:535
  401.2 0.7 pad.17.clone
  401.9 0.0 copy-done.7
  402.0 0.1 reshape.110
  402.0 0.1 copy.42
  402.1 0.1 copy.43
  402.2 0.0 copy-done.8
  402.2 0.1 maximum_maximum_fusion
  402.3 0.7 copy.47
  403.0 82.1 %scatter_4.1 = (f32[32,1024]{1,0:T(8,128)}, f32[32,1024]{1,0:T(8,128)}, f32[32,1024]{1,0:T(8,128)}, f32[32,1024]{1,0:T(8,128)}, f32[8,128]{1,0:T(8,128)}, /*index=5*/bf16[8,128,1024]{2,1,0:T(8,128)(2,1)}) custom-call(bf16[4,2,2,2,32,1024]{5,4,3,2,1,0:T(8,128)(2,1)} %bitcast.57, bf16[4,2,2,2,32,1024]{5,4,3,2,1,0:T(8,128)(2,1)} %bitcast.58, ...), custom_call_target="tpu_custom_call" | custom-call | tf_op jit(solution)/shard_map/scatter_4/pallas_call | solution.py:376
  485.1 1.3 slice.41
  487.0 1.3 slice.44
  488.3 1.5 fusion
  489.7 119.7 %scatter_3.1 = (f32[32,4096]{1,0:T(8,128)}, f32[1024,128]{1,0:T(8,128)}, bf16[8,128,1024]{2,1,0:T(8,128)(2,1)}) custom-call(bf16[4,2,2,2,32,4096]{5,4,3,2,1,0:T(8,128)(2,1)} %bitcast.42, bf16[4,2,2,2,1024,128]{5,4,3,2,1,0:T(8,128)(2,1)} %bitcast.43, bf16[2,512,1024]{2,1,0:T(8,128)(2,1)} %bitcast.56), custom_call_target="tpu_custom_call" | custom-call | tf_op jit(solution)/shard_map/scatter_3/pallas_call | solution.py:376
  609.5 2.0 copy.44
  611.5 0.0 copy-done
  611.5 2.5 convert_element_type.37
  614.0 0.0 copy-done.1
  614.0 0.0 copy-start.3
  614.0 0.0 copy-start.2
  614.0 1.3 copy.56
  615.4 0.0 copy-done.6
  615.4 0.7 copy.57
  616.0 0.0 copy-done.5
  616.0 0.7 copy.58
  616.7 0.0 copy-done.4
  616.7 0.7 copy.59
  617.3 0.0 copy-done.3
  617.3 0.7 copy.60
  618.0 0.0 copy-done.2
  618.0 0.8 copy.61
  (9 shorter events, 0.0 us)
Async XLA Ops:
  342.4 59.5 %copy-start.7 = (f32[8,1024]{1,0:T(8,128)S(1)}, f32[8,1024]{1,0:T(8,128)}, u32[]{:S(2)}) copy-start(f32[8,1024]{1,0:T(8,128)} %get-tuple-element.74) | copy-start | bytes 98308
  342.4 59.8 %copy-start.8 = (f32[1,4096]{1,0:T(1,128)S(1)}, f32[1,4096]{1,0:T(1,128)}, u32[]{:S(2)}) copy-start(f32[1,4096]{1,0:T(1,128)} %get-tuple-element.75) | copy-start | bytes 49156
  489.7 121.8 %copy-start = (bf16[8,128,1024]{2,1,0:T(8,128)(2,1)S(1)}, bf16[8,128,1024]{2,1,0:T(8,128)(2,1)}, u32[]{:S(2)}) copy-start(bf16[8,128,1024]{2,1,0:T(8,128)(2,1)} %get-tuple-element.82) | copy-start | bytes 6291460
  611.5 2.5 copy-start.1
  614.0 1.4 copy-start.6
  614.0 2.0 copy-start.5
  614.0 2.7 copy-start.4
  614.0 3.3 copy-start.3
  614.0 4.0 copy-start.2

commit v2 on v1

--- a/solution.py
+++ b/solution.py
@@ -52,6 +52,13 @@
             for name in (names or self.order)
         )
 
+    def place(self, device):
+        index = []
+        for size in reversed(self.dims):
+            index.append(lax.rem(device, size))
+            device = device // size
+        return tuple(reversed(index))
+
     def greet(self, here):
         barrier = pltpu.get_barrier_semaphore()
         count = 0
@@ -71,6 +78,12 @@
         pl.semaphore_wait(barrier, count)
 
 
+def window(cut):
+    if len(cut) == 2:
+        return (pl.ds(*cut),)
+    return (pl.ds(cut[0], cut[1]), pl.ds(cut[2], cut[3]))
+
+
 def by_core(here, orders, make):
     if orders[0] == orders[1]:
         make(orders[0])
@@ -86,7 +99,7 @@
 
     def __init__(self, lay, here, src, full, rows, send, recv, own, orders):
         self.lay, self.here = lay, here
-        self.rows = (pl.ds(*rows),)
+        self.rows = window(rows)
         self.src, self.full = src.at[self.rows], full
         self.send, self.recv, self.own = send, recv, own
         self.orders = orders
@@ -185,7 +198,7 @@
 
     def __init__(self, lay, here, grad, out, rows, bufs, send, recv, own, orders):
         self.lay, self.here, self.grad = lay, here, grad
-        self.rows = (pl.ds(*rows),)
+        self.rows = window(rows)
         self.out = out.at[self.rows]
         self.held, self.recvs = bufs[0], bufs[1:]
         self.send, self.recv, self.own = send, recv, own
@@ -193,8 +206,9 @@
         self.names = [n for n in lay.order if n != "c"]
 
     @staticmethod
-    def buffers(lay, shard, orders):
-        shape, dtype = tuple(shard.shape), shard.dtype
+    def buffers(lay, grad, cut, orders):
+        dtype = grad.dtype
+        shape = (cut[1], cut[3] if len(cut) == 4 else grad.shape[-1])
         names = [n for n in lay.order if n != "c"]
         out = [pltpu.VMEM(tuple(lay.size[n] for n in names) + shape, dtype)]
         out.append(pltpu.VMEM(tuple(lay.size[n] for n in names) + shape, dtype))
@@ -291,13 +305,36 @@
         by_core(self.here, self.orders, make)
 
 
-def skewed(parts, stages=5):
-    for t in range(len(parts) + stages - 1):
+def skewed(parts, lag=1, stages=5):
+    events = []
+    for t in range(len(parts) + lag * (stages - 1)):
         for i, part in enumerate(parts):
-            if 0 <= t - i < stages:
-                part.stage(t - i)
+            stage, rest = divmod(t - i, lag)
+            if rest == 0 and 0 <= stage < stages:
+                events.append((part, stage))
+    return events
+
+
+def run(parts, lag=2):
+    for part, stage in skewed(parts, lag):
+        part.stage(stage)
     for part in parts:
         part.drain()
+
+
+class Hooks:
+    def __init__(self, events, steps, first=0):
+        self.slots = {}
+        room = max(steps - first, 1)
+        for n, event in enumerate(events):
+            self.slots.setdefault(first + n * room // max(len(events), 1), []).append(event)
+
+    def at(self, step):
+        for k, events in self.slots.items():
+            @pl.when(step == k)
+            def _():
+                for part, stage in events:
+                    part.stage(stage)
 
 
 def sems(lay, n, m):
@@ -306,43 +343,11 @@
     return [dma((n, lay.slots)), dma((n, lay.slots)), dma((n,)), dma((m, lay.blk - 1)), dma((m, lay.blk - 1)), dma((m,))]
 
 
-def gather_call(lay, shards, parts, rows, cid):
-    n, m, p = len(shards), len(rows), len(parts)
-
-    def kernel(*refs):
-        ins, refs = refs[: n + m], refs[n + m :]
-        outs, refs = refs[: n + m], refs[n + m :]
-        send, recv, own, rsend, rrecv, rown = refs
-        here = lay.here()
-        lay.greet(here)
-        gathers = [
-            Gather(lay, here, ins[a], outs[a], (r, c), send.at[i], recv.at[i], own.at[i], orders)
-            for i, (a, r, c, orders) in enumerate(parts)
-        ]
-        splits = [Resplit(lay, ins[n + i], outs[n + i], rsend.at[i], rrecv.at[i], rown.at[i]) for i in range(m)]
-        for s in splits:
-            s.start()
-        skewed(gathers)
-        for s in splits:
-            s.finish()
-
-    outs = [jax.ShapeDtypeStruct(lay.dims + s.shape, s.dtype) for s in shards]
-    outs += [
-        jax.ShapeDtypeStruct((r.shape[0] // lay.blk, r.shape[1] * lay.blk, r.shape[2]), r.dtype) for r in rows
-    ]
-    return pl.pallas_call(
-        kernel, out_shape=outs, in_specs=[ANY] * (n + m), out_specs=[ANY] * (n + m),
-        scratch_shapes=sems(lay, p, m),
-        compiler_params=pltpu.CompilerParams(collective_id=cid, has_side_effects=True),
-        name=f"gather_{cid}",
-    )(*shards, *rows)
-
-
 def scatter_call(lay, grads, parts, rows, cid):
     n, m, p = len(grads), len(rows), len(parts)
     bufs = [
-        Scatter.buffers(lay, jax.ShapeDtypeStruct((c,) + grads[a].shape[2:], grads[a].dtype), orders)
-        for a, r, c, orders in parts
+        Scatter.buffers(lay, grads[a], cut, orders)
+        for a, cut, orders in parts
     ]
 
     def kernel(*refs):
@@ -356,15 +361,15 @@
         here = lay.here()
         lay.greet(here)
         sums = [
-            Scatter(lay, here, ins[a], outs[a], (r, c), own_bufs[i], send.at[i], recv.at[i], own.at[i], orders)
-            for i, (a, r, c, orders) in enumerate(parts)
+            Scatter(lay, here, ins[a], outs[a], cut, own_bufs[i], send.at[i], recv.at[i], own.at[i], orders)
+            for i, (a, cut, orders) in enumerate(parts)
         ]
         splits = [
             Resplit(lay, ins[n + i], outs[n + i], rsend.at[i], rrecv.at[i], rown.at[i], True) for i in range(m)
         ]
         for s in splits:
             s.start()
-        skewed(sums)
+        run(sums)
         for s in splits:
             s.finish()
 
@@ -400,87 +405,173 @@
     return pl.BlockSpec(shape, lambda *_: (0,) * len(shape), pipeline_mode=pl.Buffered(1))
 
 
-def attention_forward(x, lengths, wq, wk, wv, wo):
-    rows, width = x.shape
-    seqs = lengths.shape[0]
-    span = rows // seqs
+def attention_forward(lay, tokens, lengths, shards, parts, early):
+    width = tokens.shape[2]
+    seqs, span = tokens.shape[0] // lay.blk, tokens.shape[1] * lay.blk
+    rows = seqs * span
     groups = width // GROUP
     scale = LOG2E / math.sqrt(DH)
-
-    def kernel(len_ref, x_ref, wq_ref, wk_ref, wv_ref, wo_ref, q_ref, k_ref, v_ref, att_ref, lse_ref, h1_ref):
-        g = pl.program_id(0)
-        xv = x_ref[...]
-        q_ref[...] = dot(xv, wq_ref[...]).astype(bf16)
-        k_ref[...] = dot(xv, wk_ref[...]).astype(bf16)
-        v_ref[...] = dot(xv, wv_ref[...]).astype(bf16)
-
-        def pair_step(i, carry):
-            s, pair = i // 2, lax.rem(i, 2)
-            at = (pl.ds(pl.multiple_of(s * span, span), span), pl.ds(pl.multiple_of(pair * 128, 128), 128))
-            length = len_ref[s]
+    heads = seqs * GROUP // DH
+    pairs = seqs * GROUP // 128
+    n, p = len(shards), len(parts)
+
+    def kernel(len_ref, tok_ref, *refs):
+        ins, refs = refs[:n], refs[n:]
+        fulls, refs = refs[:n], refs[n:]
+        x_out, q_out, k_out, v_out, att_out, lse_ref, h1_out = refs[:7]
+        x_ref, wq_ref, wk_ref, wv_ref, wo_ref, q_ref, k_ref, v_ref, att_ref, h1_ref = refs[7:17]
+        load, send, recv, own, rsend, rrecv, rown = refs[17:]
+        here = lay.here()
+        lay.greet(here)
+        split = Resplit(lay, tok_ref, x_out, rsend, rrecv, rown)
+        split.start()
+        gathers = [
+            Gather(lay, here, ins[a], fulls[a], cut, send.at[i], recv.at[i], own.at[i], orders)
+            for i, (a, cut, orders) in enumerate(parts)
+        ]
+        events = skewed(gathers, 2)
+        last = max(i for i, (part, stage) in enumerate(events) if part in gathers[:early] and stage == 4)
+        for part, stage in events[: last + 1]:
+            part.stage(stage)
+        split.finish()
+        loads = [
+            pltpu.make_async_copy(src, dst, load.at[i])
+            for i, (src, dst) in enumerate(
+                zip([x_out] + list(fulls[:4]), [x_ref, wq_ref, wk_ref, wv_ref, wo_ref]))
+        ]
+        for c in loads:
+            c.start()
+        for c in loads:
+            c.wait()
+        hooks = Hooks(events[last + 1 :], groups * pairs)
+        base = lax.axis_index("blk") * seqs
+
+        def columns(ref, g):
+            block = ref[(slice(None),) * 5 + (pl.ds(pl.multiple_of(g * GROUP, GROUP), GROUP),)]
+            return block.reshape(width, GROUP)
+
+        def features(ref, g):
+            per = GROUP // ref.shape[-2]
+            return jnp.concatenate([ref[lay.place(g * per + j)] for j in range(per)], axis=0)
+
+        def step(i, carry):
+            g, r = i // pairs, lax.rem(i, pairs)
+            cols = pl.ds(pl.multiple_of(g * GROUP, GROUP), GROUP)
+
+            @pl.when(r == 0)
+            def _():
+                xv = x_ref[...].reshape(rows, width)
+                q_ref[:, cols] = dot(xv, columns(wq_ref, g)).astype(bf16)
+                k_ref[:, cols] = dot(xv, columns(wk_ref, g)).astype(bf16)
+                v_ref[:, cols] = dot(xv, columns(wv_ref, g)).astype(bf16)
+
+            s, pair = r // (GROUP // 128), lax.rem(r, GROUP // 128)
+            at = (pl.ds(pl.multiple_of(s * span, span), span),
+                  pl.ds(pl.multiple_of(g * GROUP + pair * 128, 128), 128))
             qs, ks, vs = q_ref[at], k_ref[at], v_ref[at]
             lane = lax.broadcasted_iota(jnp.int32, (span, 128), 1)
-            keep = lax.broadcasted_iota(jnp.int32, (span, 1), 0) < length
+            keep = lax.broadcasted_iota(jnp.int32, (span, 1), 0) < len_ref[base + s]
             vt = vs.T
-            outs, lses = [], []
+            outs = []
             for h in range(2):
                 km = jnp.where((lane < DH) if h == 0 else (lane >= DH), ks, jnp.zeros_like(ks))
                 st = dot_t(km, qs) * scale
                 st = jnp.where(keep, st, -1e30)
                 top = jnp.max(st, axis=0, keepdims=True)
-                p = jnp.exp2(st - top)
-                den = jnp.sum(p, axis=0, keepdims=True)
-                ot = dot(vt[h * DH : (h + 1) * DH], p.astype(bf16))
+                e = jnp.exp2(st - top)
+                den = jnp.sum(e, axis=0, keepdims=True)
+                ot = dot(vt[h * DH : (h + 1) * DH], e.astype(bf16))
                 outs.append(ot * (1.0 / den))
-                lses.append(top + jnp.log2(den))
+                lse_ref[g, pl.ds(r * 2 + h, 1)] = top + jnp.log2(den)
             att_ref[at] = jnp.concatenate(outs, axis=0).T.astype(bf16)
-            lse_ref[0, pl.ds(i * 2, 1)] = lses[0]
-            lse_ref[0, pl.ds(i * 2 + 1, 1)] = lses[1]
+
+            @pl.when(r == pairs - 1)
+            def _():
+                add = dot(att_ref[:, cols], features(wo_ref, g))
+
+                @pl.when(g == 0)
+                def _():
+                    h1_ref[...] = x_ref[...].reshape(rows, width).astype(f32) + add
+
+                @pl.when(g > 0)
+                def _():
+                    h1_ref[...] += add
+
+            hooks.at(i)
             return carry
 
-        lax.fori_loop(0, seqs * GROUP // 128, pair_step, 0)
-
-        @pl.when(g == 0)
-        def _():
-            h1_ref[...] = x_ref[...].astype(f32)
-
-        h1_ref[...] += dot(att_ref[...], wo_ref[...])
-
-    col = pl.BlockSpec((width, GROUP), lambda g, *_: (0, g))
-    act = pl.BlockSpec((rows, GROUP), lambda g, *_: (0, g))
-    heads = seqs * GROUP // DH
+        lax.fori_loop(0, groups * pairs, step, 0)
+        saves = [
+            pltpu.make_async_copy(src, dst, load.at[i])
+            for i, (src, dst) in enumerate(
+                zip([q_ref, k_ref, v_ref, att_ref, h1_ref], [q_out, k_out, v_out, att_out, h1_out]))
+        ]
+        for c in saves:
+            c.start()
+        for g in gathers:
+            g.drain()
+        for c in saves:
+            c.wait()
+
+    whole = [jax.ShapeDtypeStruct(lay.dims + s.shape, s.dtype) for s in shards]
+    act = jax.ShapeDtypeStruct((rows, width), bf16)
     return pl.pallas_call(
         kernel,
-        grid_spec=pltpu.PrefetchScalarGridSpec(
-            num_scalar_prefetch=1,
-            grid=(groups,),
-            in_specs=[once((rows, width)), col, col, col, pl.BlockSpec((GROUP, width), lambda g, *_: (g, 0))],
-            out_specs=[act, act, act, act, pl.BlockSpec((1, heads, span), lambda g, *_: (g, 0, 0)), once((rows, width))],
-        ),
-        out_shape=[jax.ShapeDtypeStruct((rows, width), bf16)] * 4
-        + [jax.ShapeDtypeStruct((groups, heads, span), f32), jax.ShapeDtypeStruct((rows, width), f32)],
-        compiler_params=pltpu.CompilerParams(vmem_limit_bytes=60 << 20),
+        in_specs=[pl.BlockSpec(memory_space=pltpu.SMEM)] + [ANY] * (n + 1),
+        out_specs=[ANY] * (n + 5) + [pl.BlockSpec(memory_space=pltpu.VMEM), ANY],
+        out_shape=whole
+        + [jax.ShapeDtypeStruct((seqs, span, width), bf16), act, act, act, act,
+           jax.ShapeDtypeStruct((groups, heads, span), f32), jax.ShapeDtypeStruct((rows, width), f32)],
+        scratch_shapes=[pltpu.VMEM((seqs, span, width), bf16)]
+        + [pltpu.VMEM(lay.dims + s.shape, bf16) for s in shards[:4]]
+        + [pltpu.VMEM((rows, width), bf16)] * 4
+        + [pltpu.VMEM((rows, width), f32), pltpu.SemaphoreType.DMA((5,))]
+        + sems(lay, p, 0)[:3]
+        + [pltpu.SemaphoreType.DMA((lay.blk - 1,)), pltpu.SemaphoreType.DMA((lay.blk - 1,)),
+           pltpu.SemaphoreType.DMA],
+        compiler_params=pltpu.CompilerParams(collective_id=1, has_side_effects=True, vmem_limit_bytes=60 << 20),
         name="attention_forward",
-    )(lengths, x, wq, wk, wv, wo)
-
-
-def attention_backward(x, lengths, wq, wk, wv, wo, q, k, v, att, lse, d_branch, d_one):
+    )(lengths, tokens, *shards)
+
+
+def attention_backward(lay, x, lengths, wq, wk, wv, wo, q, k, v, att, lse, d_branch, d_one, grads, parts):
     rows, width = x.shape
-    seqs = lengths.shape[0]
-    span = rows // seqs
+    seqs, heads, span = lse.shape[1] * DH // GROUP, lse.shape[1], lse.shape[2]
     groups = width // GROUP
+    pairs = seqs * GROUP // 128
     scale = LOG2E / math.sqrt(DH)
-
-    def kernel(
-        len_ref, x_ref, wq_ref, wk_ref, wv_ref, wo_ref, q_ref, k_ref, v_ref, att_ref, lse_ref, db_ref, d1_ref,
+    bufs = [Scatter.buffers(lay, grads[a], cut, orders) for a, cut, orders in parts]
+    n = len(grads)
+    grads = [g.reshape(lay.dims + g.shape[1:]) for g in grads]
+
+    def kernel(*refs):
+        ins, refs = refs[13 : 13 + n], refs[:13] + refs[13 + n :]
+        outs, refs = refs[18 : 18 + n], refs[:18] + refs[18 + n :]
+        *own_bufs, send, recv, own, d1_sem = refs[24:]
+        body(ins, outs, own_bufs, send, recv, own, d1_sem, *refs[:24])
+
+    def body(
+        ins, outs, own_bufs, send, recv, own, d1_sem, len_ref, x_ref, wq_ref, wk_ref, wv_ref, wo_ref, q_ref, k_ref, v_ref, att_ref, lse_ref, db_ref, d1_ref,
         gq_ref, gk_ref, gv_ref, go_ref, dx_ref, xt_ref, do_ref, dq_ref, dk_ref, dv_ref, acc_ref,
     ):
         g = pl.program_id(0)
+        here = lay.here()
+        sums = [
+            Scatter(lay, here, ins[a], outs[a], cut, own_bufs[5 * i : 5 * i + 5], send.at[i], recv.at[i], own.at[i], orders)
+            for i, (a, cut, orders) in enumerate(parts)
+        ]
+        events = skewed(sums, 2)
+        hooks = Hooks(events[1:], groups * pairs)
+        base = lax.axis_index("blk") * seqs
 
         @pl.when(g == 0)
         def _():
+            lay.greet(here)
+            events[0][0].stage(0)
+            fetch = pltpu.make_async_copy(d1_ref, acc_ref, d1_sem)
+            fetch.start()
             xt_ref[...] = x_ref[...].T
-            acc_ref[...] = d1_ref[...]
+            fetch.wait()
 
         db = db_ref[...]
         do_ref[...] = dot_t(db, wo_ref[...]).astype(bf16)
@@ -489,7 +580,7 @@
         def pair_step(i, carry):
             s, pair = i // 2, lax.rem(i, 2)
             at = (pl.ds(pl.multiple_of(s * span, span), span), pl.ds(pl.multiple_of(pair * 128, 128), 128))
-            length = len_ref[s]
+            length = len_ref[base + s]
             qs, ks, vs, dos = q_ref[at], k_ref[at], v_ref[at], do_ref[at]
             lane = lax.broadcasted_iota(jnp.int32, (span, 128), 1)
             keep = lax.broadcasted_iota(jnp.int32, (span, 1), 0) < length
@@ -511,9 +602,10 @@
             dv_ref[at] = jnp.where(first, dvs[0], dvs[1]).astype(bf16)
             dk_ref[at] = (jnp.where(first, dks[0], dks[1]) * unit).astype(bf16)
             dq_ref[at] = (jnp.concatenate(dqs, axis=0).T * unit).astype(bf16)
+            hooks.at(g * pairs + i)
             return carry
 
-        lax.fori_loop(0, seqs * GROUP // 128, pair_step, 0)
+        lax.fori_loop(0, pairs, pair_step, 0)
         xt = xt_ref[...]
         gq_ref[...] = dot(xt, dq_ref[...]).astype(bf16)
         gk_ref[...] = dot(xt, dk_ref[...]).astype(bf16)
@@ -526,54 +618,68 @@
         @pl.when(g == groups - 1)
         def _():
             dx_ref[...] = acc_ref[...].astype(bf16)
+            for part in sums:
+                part.drain()
 
     col = pl.BlockSpec((width, GROUP), lambda g, *_: (0, g))
     row = pl.BlockSpec((GROUP, width), lambda g, *_: (g, 0))
     act = pl.BlockSpec((rows, GROUP), lambda g, *_: (0, g))
-    heads = seqs * GROUP // DH
     full = once((rows, width))
     return pl.pallas_call(
         kernel,
         grid_spec=pltpu.PrefetchScalarGridSpec(
-            num_scalar_prefetch=1,
+            num_scalar_prefetch=0,
             grid=(groups,),
-            in_specs=[full, col, col, col, row, act, act, act, act,
-                      pl.BlockSpec((1, heads, span), lambda g, *_: (g, 0, 0)), full, full],
-            out_specs=[col, col, col, row, full],
+            in_specs=[pl.BlockSpec(memory_space=pltpu.SMEM), full, col, col, col, row, act, act, act, act,
+                      pl.BlockSpec((1, heads, span), lambda g, *_: (g, 0, 0)), full, ANY] + [ANY] * n,
+            out_specs=[col, col, col, row, full] + [pl.BlockSpec(memory_space=pltpu.VMEM)] * n,
             scratch_shapes=[pltpu.VMEM((width, rows), bf16)] + [pltpu.VMEM((rows, GROUP), bf16)] * 4
-            + [pltpu.VMEM((rows, width), f32)],
+            + [pltpu.VMEM((rows, width), f32)]
+            + [b for bs in bufs for b in bs] + sems(lay, len(parts), 0)[:3] + [pltpu.SemaphoreType.DMA],
         ),
-        out_shape=[jax.ShapeDtypeStruct((width, width), bf16)] * 4 + [jax.ShapeDtypeStruct((rows, width), bf16)],
-        compiler_params=pltpu.CompilerParams(vmem_limit_bytes=60 << 20),
+        out_shape=[jax.ShapeDtypeStruct((width, width), bf16)] * 4 + [jax.ShapeDtypeStruct((rows, width), bf16)]
+        + [jax.ShapeDtypeStruct(g.shape[-2:], f32) for g in grads],
+        compiler_params=pltpu.CompilerParams(
+            collective_id=3, has_side_effects=True, vmem_limit_bytes=63 << 20),
         name="attention_backward",
-    )(lengths, x, wq, wk, wv, wo, q, k, v, att, lse, d_branch, d_one)
+    )(lengths, x, wq, wk, wv, wo, q, k, v, att, lse, d_branch, d_one, *grads)
 
 
 TILE = 512
 CHUNK = 256
 
 
-def feed_forward(h1, teacher, out_grad, lengths, inv_count, vecs, bias_inner, w1, w2, devices):
+def feed_forward(lay, h1, teacher, out_grad, lengths, inv_count, vecs, bias_inner, w1, w2):
     rows, width = h1.shape
     hidden = w1.shape[1]
-    seqs = lengths.shape[0]
+    seqs = teacher.shape[0] // lay.blk
     span = rows // seqs
+    devices = lay.devices
     tiles = hidden // TILE
     share = hidden // devices
     per_tile = TILE // share
     wide = share % 128 == 0
 
     def kernel(
-        len_ref, inv_ref, h1_ref, teach_ref, og_ref, vec_ref, b1_ref, w1_ref, w2_ref,
-        out_ref, d1_ref, db_ref, gw1_ref, gw2_ref, sums_ref, gb1_ref,
+        len_ref, inv_ref, h1_ref, teach_in, og_in, vec_ref, b1_ref, w1_ref, w2_ref,
+        layer_out, d1_ref, db_ref, gw1_ref, gw2_ref, sums_ref, gb1_ref,
         low_ref, lowt_ref, act_ref, slope_ref, acc_ref, do_ref, dot_ref, inv1_ref, di_ref,
+        teach_ref, og_ref, out_ref, send, recv, own,
     ):
         t = pl.program_id(0)
+        base = lax.axis_index("blk") * seqs
+        splits = [
+            Resplit(lay, src, dst, send.at[i], recv.at[i], own.at[i], i == 2)
+            for i, (src, dst) in enumerate(((teach_in, teach_ref), (og_in, og_ref), (out_ref, layer_out)))
+        ]
         gain1, shift1 = vec_ref[0:1], vec_ref[1:2]
         bias2, gain2, shift2 = vec_ref[2:3], vec_ref[3:4], vec_ref[4:5]
 
         @pl.when(t == 0)
         def _():
+            lay.greet(lay.here())
+            splits[0].start()
+            splits[1].start()
             sums_ref[...] = jnp.zeros_like(sums_ref)
 
             def norm(i, carry):
@@ -607,6 +713,8 @@
         @pl.when(t == tiles)
         def _():
             inv = inv_ref[0]
+            splits[0].finish()
+            splits[1].finish()
 
             def middle(i, carry):
                 at = pl.ds(pl.multiple_of(i * 128, 128), 128)
@@ -616,12 +724,14 @@
                 inverse = lax.rsqrt(jnp.mean(centred * centred, axis=-1, keepdims=True) + 1e-12)
                 normal = centred * inverse
                 result = normal * gain2 + shift2
-                out_ref[at] = result.astype(bf16)
                 seq = (i * 128) // span
-                pos = i * 128 - seq * span + lax.broadcasted_iota(jnp.int32, (128, 1), 0)
-                valid = (pos < len_ref[seq]).astype(f32)
-                deviation = (result - teach_ref[at].astype(f32)) * valid
-                grad = og_ref[at].astype(f32) * valid + (2.0 * inv) * deviation
+                first = i * 128 - seq * span
+                there = (seq, pl.ds(pl.multiple_of(first, 128), 128))
+                out_ref[there] = result.astype(bf16)
+                pos = first + lax.broadcasted_iota(jnp.int32, (128, 1), 0)
+                valid = (pos < len_ref[base + seq]).astype(f32)
+                deviation = (result - teach_ref[there].astype(f32)) * valid
+                grad = og_ref[there].astype(f32) * valid + (2.0 * inv) * deviation
                 sums_ref[0:1] += jnp.sum(deviation * deviation, axis=0, keepdims=True)
                 sums_ref[1:2] += jnp.sum(grad * normal, axis=0, keepdims=True)
                 sums_ref[2:3] += jnp.sum(grad, axis=0, keepdims=True)
@@ -637,6 +747,7 @@
                 return carry
 
             lax.fori_loop(0, rows // 128, middle, 0)
+            splits[2].start()
 
         @pl.when(t > tiles)
         def _():
@@ -674,6 +785,7 @@
                 return carry
 
             lax.fori_loop(0, rows // 128, back, 0)
+            splits[2].finish()
 
     def tile(t, *_):
         return jnp.where(t < tiles, t, jnp.maximum(t - tiles - 1, 0))
@@ -686,15 +798,16 @@
     return pl.pallas_call(
         kernel,
         grid_spec=pltpu.PrefetchScalarGridSpec(
-            num_scalar_prefetch=2,
+            num_scalar_prefetch=0,
             grid=(2 * tiles + 1,),
             in_specs=[
-                full, full, full, once((8, width)), vec,
+                pl.BlockSpec(memory_space=pltpu.SMEM), pl.BlockSpec(memory_space=pltpu.SMEM),
+                full, ANY, ANY, once((8, width)), vec,
                 pl.BlockSpec((width, TILE), lambda t, *_: (0, tile(t))),
                 pl.BlockSpec((TILE, width), lambda t, *_: (tile(t), 0)),
             ],
             out_specs=[
-                full, full, full,
+                ANY, full, full,
                 pl.BlockSpec((width, TILE), lambda t, *_: (0, back_tile(t))),
                 pl.BlockSpec((per_tile, width, share), lambda t, *_: (back_tile(t), 0, 0))
                 if wide else pl.BlockSpec((width, TILE), lambda t, *_: (0, back_tile(t))),
@@ -706,10 +819,12 @@
                 pltpu.VMEM((tiles, rows, TILE), bf16), pltpu.VMEM((tiles, rows, TILE), bf16),
                 pltpu.VMEM((rows, width), f32), pltpu.VMEM((rows, width), bf16), pltpu.VMEM((width, rows), bf16),
                 pltpu.VMEM((rows, 1), f32), pltpu.VMEM((rows, TILE), bf16),
-            ],
+            ]
+            + [pltpu.VMEM((seqs, span, width), bf16)] * 3
+            + sems(lay, 0, 3)[3:],
         ),
         out_shape=[
-            jax.ShapeDtypeStruct((rows, width), bf16),
+            jax.ShapeDtypeStruct(teacher.shape, bf16),
             jax.ShapeDtypeStruct((rows, width), f32),
             jax.ShapeDtypeStruct((rows, width), bf16),
             jax.ShapeDtypeStruct((width, hidden), bf16),
@@ -717,17 +832,20 @@
             jax.ShapeDtypeStruct((8, width), f32),
             jax.ShapeDtypeStruct((1, hidden), f32),
         ],
-        compiler_params=pltpu.CompilerParams(vmem_limit_bytes=63 << 20),
+        compiler_params=pltpu.CompilerParams(
+            collective_id=2, has_side_effects=True, vmem_limit_bytes=63 << 20),
         name="feed_forward",
     )(lengths, inv_count, h1, teacher, out_grad, vecs, bias_inner, w1, w2)
 
-
-def cut(shape, which, pieces, orders):
-    rows = shape[0]
+def cut(shape, which, pieces, orders, columns=False):
+    rows, wide = shape
+    if columns:
+        step = wide // pieces
+        return [(which, (0, rows, i * step, step), orders) for i in range(pieces)]
     while pieces > 1 and rows % (pieces * 16):
         pieces -= 1
     step = rows // pieces
-    return [(which, i * step, step, orders) for i in range(pieces)]
+    return [(which, (i * step, step), orders) for i in range(pieces)]
 
 
 def shards(
@@ -747,13 +865,15 @@
     )
     used = 5 * share + deep
     pack = jnp.pad(small, (0, 1024 - small.shape[0])).reshape(8, 128)
-    ins = [w_query, w_key, w_value, w_output]
-    parts = [(4, 0, 8, there)]
-    for i, w in enumerate(ins):
-        parts += cut(w.shape, i, 1, there)
-    wq, wk, wv, wo, packs, x = gather_call(lay, ins + [pack], parts, [tokens], 1)
-    parts = cut(w_inner.shape, 0, 2, there) + cut(w_outer.shape, 1, 2, there)
-    w1, w2, teach, given = gather_call(lay, [w_inner, w_outer], parts, [teacher, out_grad], 2)
+    ins = [w_query, w_key, w_value, w_output, pack, w_inner, w_outer]
+    parts = [(4, (0, 8), there)]
+    for i in range(4):
+        parts += cut(ins[i].shape, i, 1, there)
+    early = len(parts)
+    parts += cut(w_inner.shape, 5, 4, there, True) + cut(w_outer.shape, 6, 4, there)
+    wq, wk, wv, wo, packs, w1, w2, x, q, k, v, att, lse, h1 = attention_forward(
+        lay, tokens, lengths, ins, parts, early
+    )
     wq, wk, wv, wo = (w.reshape(width, width) for w in (wq, wk, wv, wo))
     w1, w2 = w1.reshape(width, hidden), w2.reshape(hidden, width)
     packs = packs.reshape(devices, 1024)
@@ -763,31 +883,28 @@
     inv_count = 1.0 / (jnp.sum(packs[:, used]) / lay.blk * width)
 
     seqs = x.shape[0]
-    own = lax.dynamic_slice(lengths, (lax.axis_index("blk") * seqs,), (seqs,))
     x = x.reshape(-1, width)
-    q, k, v, att, lse, h1 = attention_forward(x, own, wq, wk, wv, wo)
-    out, d_one, d_branch, gw1, gw2, sums, gb1 = feed_forward(
-        h1, teach.reshape(-1, width), given.reshape(-1, width), own, inv_count[None], vecs, bias1, w1, w2, devices
+    layer_out, d_one, d_branch, gw1, gw2, sums, gb1 = feed_forward(
+        lay, h1, teacher, out_grad, lengths, inv_count[None], vecs, bias1, w1, w2
     )
-    gq, gk, gv, go, dx = attention_backward(x, own, wq, wk, wv, wo, q, k, v, att, lse, d_branch, d_one)
-
-    span = lambda a: a.reshape(seqs, -1, width)
     by_device = lambda a: a.reshape((devices, a.shape[0] // devices) + a.shape[1:])
     gw1 = by_device(gw1)
     turned = gw2.ndim == 3
     if not turned:
         gw2 = by_device(gw2.T)
-    parts = cut(gw1.shape[1:], 0, 2, back) + cut(gw2.shape[1:], 1, 2, back)
-    g_inner, g_outer, layer_out = scatter_call(lay, [gw1, gw2], parts, [span(out)], 3)
+    parts = cut(gw1.shape[1:], 0, 4, back, True) + cut(gw2.shape[1:], 1, 4, back)
+    gq, gk, gv, go, dx, g_inner, g_outer = attention_backward(
+        lay, x, lengths, wq, wk, wv, wo, q, k, v, att, lse, d_branch, d_one, [gw1, gw2], parts
+    )
     loss = jnp.broadcast_to(jnp.sum(sums[0])[None, None], (devices, 1))
     vec_sums = sums[1:6].reshape(5, devices, share).transpose(1, 0, 2).reshape(devices, 5 * share)
     small = jnp.concatenate([vec_sums, gb1.reshape(devices, deep), loss], axis=1)
     small = jnp.pad(small, ((0, 0), (0, 1024 - small.shape[1]))).reshape(devices, 8, 128)
     grads = [by_device(g) for g in (gq, gk, gv, go)] + [small]
-    parts = [(4, 0, 8, back)]
+    parts = [(4, (0, 8), back)]
     for i in range(4):
         parts += cut(grads[i].shape[1:], i, 1, back)
-    g_query, g_key, g_value, g_output, small, d_tokens = scatter_call(lay, grads, parts, [span(dx)], 4)
+    g_query, g_key, g_value, g_output, small, d_tokens = scatter_call(lay, grads, parts, [dx.reshape(seqs, -1, width)], 4)
     small = small.reshape(1024)
     vec = lambda i: small[i * share : (i + 1) * share]
     return (

time: 621 us -> 454 us (0.73)
  Pallas kernels: 589 us -> 423 us
    pallas_call x2 -> x1, Pallas kernels: 202 us -> 72.6 us  [scatter_call(): pl.pallas_call(kernel, out_shape=outs, in_specs=[ANY] * (n + m), out_spec...]
    pallas_call x3 -> x1, Pallas kernels: 241 us -> 141 us  [attention_forward(): pl.pallas_call(kernel, in_specs=[pl.BlockSpec(memory_space=pltpu.SMEM)] +...]
    pallas_call x1, Pallas kernels: 58.8 us -> 104 us  [attention_backward(): pl.pallas_call(kernel, grid_spec=pltpu.PrefetchScalarGridSpec(num_scalar_...]
    pallas_call x1, Pallas kernels: 87.6 us -> 105 us  [feed_forward(): pl.pallas_call(kernel, grid_spec=pltpu.PrefetchScalarGridSpec(num_scalar_...]
where the time goes in v2:
time: 454 us
  Pallas kernels  423 us (93%)
  local copies, waits for them, and re-layouts  18.6 us (4%)
  other arithmetic  7.64 us (2%)
    pallas_call x1, Pallas kernels, attention_forward(): pl.pallas_call(kernel, in_specs=[pl.BlockSpec(memory_space=pltpu.SMEM)] +...  141 us
    pallas_call x1, Pallas kernels, feed_forward(): pl.pallas_call(kernel, grid_spec=pltpu.PrefetchScalarGridSpec(num_scalar_...  105 us
    pallas_call x1, Pallas kernels, attention_backward(): pl.pallas_call(kernel, grid_spec=pltpu.PrefetchScalarGridSpec(num_scalar_...  104 us
    pallas_call x1, Pallas kernels, scatter_call(): pl.pallas_call(kernel, out_shape=outs, in_specs=[ANY] * (n + m), out_spec...  72.6 us

profile of v2, /device:TPU:0, one launch (start us, length us, event | category | flops | bytes accessed | tf_op | source)
XLA Modules:
  0.0 453.6 jit_solution(13488264863235272401)
XLA Ops:
  0.6 1.3 reduce_sum.27
  2.6 4.1 concatenate.6
  6.7 0.6 pad_bitcast_fusion.1.refs_4_
  7.3 141.4 %attention_forward.1 = (bf16[4,2,2,2,32,1024]{5,4,3,2,1,0:T(8,128)(2,1)}, bf16[4,2,2,2,32,1024]{5,4,3,2,1,0:T(8,128)(2,1)}, bf16[4,2,2,2,32,1024]{5,4,3,2,1,0:T(...) custom-call(s32[8]{0:T(128)} %refs_0_.3, ...), custom_call_target="tpu_custom_call" | custom-call | tf_op jit(solution)/shard_map/attention_forward/pallas_call | solution.py:518
  148.7 0.9 copy.49
  149.6 0.7 slice_reduce_fusion
  151.0 0.7 slice.50
  151.7 0.1 copy.45
  151.8 0.1 copy.41
  151.9 0.1 reshape.95
  152.0 0.6 pad.13.vec_ref
  152.6 105.3 %feed_forward.1 = (bf16[8,128,1024]{2,1,0:T(8,128)(2,1)}, f32[1024,1024]{1,0:T(8,128)}, bf16[1024,1024]{1,0:T(8,128)(2,1)}, bf16[1024,4096]{1,0:T(8,128)(2,1)}, ...) custom-call(s32[8]{0:T(128)} %refs_0_.3, f32[1]{0:T(128)} %bitcast.7.inv_ref, ...), custom_call_target="tpu_custom_call" | custom-call | tf_op jit(solution)/shard_map/feed_forward/pallas_call | solution.py:798
  257.9 1.4 slice_reduce_fusion.1
  259.3 0.0 copy-start.7
  259.3 0.0 copy-start.8
  259.3 104.1 %attention_backward.1 = (bf16[1024,1024]{1,0:T(8,128)(2,1)}, bf16[1024,1024]{1,0:T(8,128)(2,1)}, bf16[1024,1024]{1,0:T(8,128)(2,1)}, bf16[1024,1024]{1,0:T(8,128...) custom-call(s32[8]{0:T(128)} %refs_0_.3, bf16[1024,1024]{1,0:T(8,128)(2,1)} %bitcast.47, ...), custom_call_target="tpu_custom_call" | custom-call | tf_op jit(solution)/shard_map/attention_backward/pallas_call | solution.py:628
  363.5 0.7 pad.17.clone
  364.2 0.0 copy-done.7
  364.2 0.1 reshape.100
  364.3 0.1 copy.42
  364.4 0.1 copy.43
  364.4 0.0 copy-done.8
  364.4 0.1 maximum_maximum_fusion
  364.6 0.7 copy.47
  365.2 0.0 copy-start.2
  365.2 72.6 %scatter_4.1 = (f32[32,1024]{1,0:T(8,128)}, f32[32,1024]{1,0:T(8,128)}, f32[32,1024]{1,0:T(8,128)}, f32[32,1024]{1,0:T(8,128)}, f32[8,128]{1,0:T(8,128)}, /*index=5*/bf16[8,128,1024]{2,1,0:T(8,128)(2,1)}) custom-call(bf16[4,2,2,2,32,1024]{5,4,3,2,1,0:T(8,128)(2,1)} %bitcast.48, bf16[4,2,2,2,32,1024]{5,4,3,2,1,0:T(8,128)(2,1)} %bitcast.49, ...), custom_call_target="tpu_custom_call" | custom-call | tf_op jit(solution)/shard_map/scatter_4/pallas_call | solution.py:381
  437.8 1.3 slice.41
  439.7 1.3 slice.44
  441.0 1.5 fusion
  442.5 0.0 copy-done.2
  442.5 1.0 copy.44
  443.5 0.0 copy-start
  443.5 4.2 convert_element_type.37
  447.7 0.0 copy-done
  447.7 0.0 copy-start.6
  447.7 0.0 copy-start.3
  447.7 0.0 copy-start.1
  447.7 1.3 copy.56
  449.0 0.0 copy-done.6
  449.0 0.7 copy.57
  449.7 0.0 copy-done.5
  449.7 0.7 copy.58
  450.4 0.0 copy-done.4
  450.4 0.7 copy.59
  451.0 0.0 copy-done.3
  451.0 0.7 copy.60
  451.7 0.0 copy-done.1
  451.7 0.8 copy.61
  (5 shorter events, 0.0 us)
Async XLA Ops:
  259.3 104.9 %copy-start.7 = (f32[8,1024]{1,0:T(8,128)S(1)}, f32[8,1024]{1,0:T(8,128)}, u32[]{:S(2)}) copy-start(f32[8,1024]{1,0:T(8,128)} %get-tuple-element.71) | copy-start | bytes 98308
  259.3 105.1 %copy-start.8 = (f32[1,4096]{1,0:T(1,128)S(1)}, f32[1,4096]{1,0:T(1,128)}, u32[]{:S(2)}) copy-start(f32[1,4096]{1,0:T(1,128)} %get-tuple-element.72) | copy-start | bytes 49156
  365.2 77.2 %copy-start.2 = (f32[1024,128]{1,0:T(8,128)S(1)}, f32[1024,128]{1,0:T(8,128)}, u32[]{:S(2)}) copy-start(f32[1024,128]{1,0:T(8,128)} %get-tuple-element.82) | copy-start | bytes 1572868
  443.5 4.2 copy-start
  447.7 1.4 copy-start.6
  447.7 2.0 copy-start.5
  447.7 2.7 copy-start.4
  447.7 3.3 copy-start.3
  447.7 4.0 copy-start.1

commit v3 on v2

v3 whole, which is shorter than its diff:
```python
import math

import jax
import jax.numpy as jnp
from jax import lax
from jax.experimental import pallas as pl
from jax.experimental.pallas import tpu as pltpu
from jax.sharding import PartitionSpec as P

ANY = pl.BlockSpec(memory_space=pl.ANY)
MESH = pl.DeviceIdType.MESH
f32 = jnp.float32
bf16 = jnp.bfloat16


class Layout:
    def __init__(self, mesh):
        dp, blk = mesh.shape["dp"], mesh.shape["blk"]
        if dp == 8 and blk == 4:
            dims = [("z", "dp", 2, 4), ("x", "dp", 1, 2), ("y", "blk", 2, 2), ("c", "blk", 1, 2)]
        else:
            dims = [("z", "dp", dp // 4, 4), ("x", "dp", 2, dp // 8), ("c", "dp", 1, 2), ("y", "blk", 1, blk)]
        self.order = [d[0] for d in dims]
        self.axis = {d[0]: d[1] for d in dims}
        self.stride = {d[0]: d[2] for d in dims}
        self.size = {d[0]: d[3] for d in dims}
        self.dims = tuple(d[3] for d in dims)
        self.blk = blk
        self.devices = dp * blk
        self.slot = {}
        count = 0
        for name in self.order:
            self.slot[name] = count
            count += self.size[name] - 1
        self.slots = count

    def here(self):
        return {
            name: lax.rem(lax.axis_index(self.axis[name]) // self.stride[name], self.size[name])
            for name in self.order
        }

    def step_to(self, here, name, distance):
        there = lax.rem(here[name] + distance, self.size[name])
        index = lax.axis_index(self.axis[name]) + (there - here[name]) * self.stride[name]
        return there, {self.axis[name]: index}

    def at(self, here, whole, changed=(), names=None):
        changed = dict(changed)
        return tuple(
            slice(None) if name in whole else changed.get(name, here[name])
            for name in (names or self.order)
        )

    def place(self, device):
        index = []
        for size in reversed(self.dims):
            index.append(lax.rem(device, size))
            device = device // size
        return tuple(reversed(index))

    def greet(self, here):
        barrier = pltpu.get_barrier_semaphore()
        count = 0
        for name in self.order:
            if self.axis[name] == "blk":
                continue
            for distance in range(1, self.size[name]):
                _, device = self.step_to(here, name, distance)
                pl.semaphore_signal(barrier, inc=1, device_id=device, device_id_type=MESH)
                count += 1
        me = lax.axis_index("blk")
        for distance in range(1, self.blk):
            pl.semaphore_signal(
                barrier, inc=1, device_id={"blk": lax.rem(me + distance, self.blk)}, device_id_type=MESH
            )
            count += 1
        pl.semaphore_wait(barrier, count)


def window(cut):
    if len(cut) == 2:
        return (pl.ds(*cut),)
    return (pl.ds(cut[0], cut[1]), pl.ds(cut[2], cut[3]))


def by_core(here, orders, make):
    if orders[0] == orders[1]:
        make(orders[0])
        return
    for core in range(2):
        @pl.when(here["c"] == core)
        def _():
            make(orders[core])


class Gather:
    stages = 5

    def __init__(self, lay, here, src, full, rows, send, recv, own, orders):
        self.lay, self.here = lay, here
        self.rows = window(rows)
        self.src, self.full = src.at[self.rows], full
        self.send, self.recv, self.own = send, recv, own
        self.orders = orders

    def line(self, name, whole):
        copies = []
        place = self.full.at[self.lay.at(self.here, whole) + self.rows]
        source = self.src if not whole else place
        for distance in range(1, self.lay.size[name]):
            _, device = self.lay.step_to(self.here, name, distance)
            slot = self.lay.slot[name] + distance - 1
            copies.append(
                pltpu.make_async_remote_copy(
                    src_ref=source, dst_ref=place, send_sem=self.send.at[slot], recv_sem=self.recv.at[slot],
                    device_id=device, device_id_type=MESH,
                )
            )
        return copies

    def local(self):
        return pltpu.make_async_copy(self.src, self.full.at[self.lay.at(self.here, ()) + self.rows], self.own)

    def stage(self, k):
        if k == 1:
            self.local().wait()

        def make(order):
            lines = tuple(order) + ("c",)
            if k > 0:
                for c in self.line(lines[k - 1], lines[: k - 1]):
                    c.wait_recv()
            if k < 4:
                for c in self.line(lines[k], lines[:k]):
                    c.start()

        if k == 0:
            self.local().start()
        by_core(self.here, self.orders, make)

    def drain(self):
        def make(order):
            lines = tuple(order) + ("c",)
            for k in range(4):
                for c in self.line(lines[k], lines[:k]):
                    c.wait_send()
        by_core(self.here, self.orders, make)


class Resplit:
    def __init__(self, lay, src, dst, send, recv, own, back=False, first=0):
        self.lay, self.src, self.dst = lay, src, dst
        self.first = first
        self.send, self.recv, self.own = send, recv, own
        self.me = lax.axis_index("blk")
        self.back = back
        self.seqs = (src if back else dst).shape[0]
        self.span = (dst if back else src).shape[1]

    def ends(self, there):
        if self.back:
            return (self.src.at[:, pl.ds(there * self.span, self.span)],
                    self.dst.at[pl.ds(self.me * (self.dst.shape[0] // self.lay.blk) + self.first, self.seqs)])
        return (self.src.at[pl.ds(there * self.seqs, self.seqs)],
                self.dst.at[:, pl.ds(self.me * self.span, self.span)])

    def copies(self):
        out = []
        for distance in range(1, self.lay.blk):
            there = lax.rem(self.me + distance, self.lay.blk)
            src, dst = self.ends(there)
            out.append(
                pltpu.make_async_remote_copy(
                    src_ref=src, dst_ref=dst,
                    send_sem=self.send.at[distance - 1], recv_sem=self.recv.at[distance - 1],
                    device_id={"blk": there}, device_id_type=MESH,
                )
            )
        return out

    def local(self):
        src, dst = self.ends(self.me)
        return pltpu.make_async_copy(src, dst, self.own)

    def start(self):
        self.local().start()
        for c in self.copies():
            c.start()

    def finish(self):
        self.local().wait()
        for c in self.copies():
            c.wait()


class Scatter:
    stages = 5

    def __init__(self, lay, here, grad, cut, out, bufs, send, recv, own, orders, staged=None, turn=False):
        self.turn = turn
        self.lay, self.here, self.grad, self.cut = lay, here, grad, window(cut)
        self.out, self.held, self.recvs, self.staged = out, bufs[0], bufs[1:], staged
        self.send, self.recv, self.own = send, recv, own
        self.orders = orders
        self.names = [n for n in lay.order if n != "c"]

    @staticmethod
    def buffers(lay, cut, dtype, orders):
        shape = (cut[1], cut[3])
        names = [n for n in lay.order if n != "c"]
        out = [pltpu.VMEM(tuple(lay.size[n] for n in names) + shape, dtype)]
        for k in range(3):
            lines = orders[0][k + 1 :]
            left = tuple(lay.size[n] for n in names if n in lines)
            out.append(pltpu.VMEM((lay.size[orders[0][k]] - 1,) + left + shape, dtype))
        return out

    def local(self):
        return pltpu.make_async_copy(
            self.grad.at[self.lay.at(self.here, self.names) + self.cut], self.staged, self.own)

    def core(self):
        there, device = self.lay.step_to(self.here, "c", 1)
        slot = self.lay.slot["c"]
        return pltpu.make_async_remote_copy(
            src_ref=self.grad.at[self.lay.at(self.here, self.names, {"c": there}) + self.cut], dst_ref=self.held,
            send_sem=self.send.at[slot], recv_sem=self.recv.at[slot], device_id=device, device_id_type=MESH)

    def line(self, order, k):
        name, left = order[k], order[k + 1 :]
        copies = []
        for distance in range(1, self.lay.size[name]):
            there, device = self.lay.step_to(self.here, name, distance)
            slot = self.lay.slot[name] + distance - 1
            copies.append(
                pltpu.make_async_remote_copy(
                    src_ref=self.held.at[self.lay.at(self.here, left, {name: there}, self.names)],
                    dst_ref=self.recvs[k].at[distance - 1],
                    send_sem=self.send.at[slot], recv_sem=self.recv.at[slot],
                    device_id=device, device_id_type=MESH,
                )
            )
        return copies

    def add(self, order, k):
        left = [n for n in self.names if k < 0 or n in order[k + 1 :]]
        steps = self.lay.size[left[0]] if left else 1

        def one(i, carry):
            index = {n: slice(None) for n in left}
            if left:
                index[left[0]] = i
            mine = tuple(index.get(n, self.here[n]) for n in self.names)
            value = self.held[mine].astype(f32)
            if k >= 0:
                theirs = tuple(index[n] for n in left)
                for d in range(self.lay.size[order[k]] - 1):
                    value = value + self.recvs[k][(d,) + theirs].astype(f32)
            elif self.staged is not None:
                value = value + self.staged[mine].astype(f32)
            else:
                value = value + self.grad[self.lay.at({**self.here, **index}, ()) + self.cut].astype(f32)
            if k == 2:
                self.out[...] = value.T if self.turn else value
            else:
                self.held[mine] = value.astype(self.held.dtype)
            return carry

        lax.fori_loop(0, steps, one, 0)

    def stage(self, k):
        if k == 0:
            self.core().start()
            if self.staged is not None:
                self.local().start()
            return
        if k == 1:
            if self.staged is not None:
                self.local().wait()
            self.core().wait()
            self.add(None, -1)

        def make(order):
            if k > 1:
                for c in self.line(order, k - 2):
                    c.wait_recv()
                self.add(order, k - 2)
            if k < 4:
                for c in self.line(order, k - 1):
                    c.start()

        by_core(self.here, self.orders, make)

    def drain(self):
        def make(order):
            for k in range(3):
                for c in self.line(order, k):
                    c.wait_send()

        by_core(self.here, self.orders, make)


def skewed(parts, lag=1, stages=5):
    events = []
    for t in range(len(parts) + lag * (stages - 1)):
        for i, part in enumerate(parts):
            stage, rest = divmod(t - i, lag)
            if rest == 0 and 0 <= stage < stages:
                events.append((part, stage))
    return events


class Hooks:
    def __init__(self):
        self.slots = {}

    def put(self, slot, event):
        self.slots.setdefault(slot, []).append(event)

    def spread(self, events, first, last):
        for n, event in enumerate(events):
            self.put(first + n * (last - first) // len(events), event)

    def run(self, slot):
        for part, stage in self.slots.get(slot, ()):
            part.stage(stage)

    def at(self, step, slots):
        for k in slots:
            if k in self.slots:
                pl.when(step == k)(lambda k=k: self.run(k))


def sems(lay, n, m):
    dma = pltpu.SemaphoreType.DMA
    n, m = max(n, 1), max(m, 1)
    return [dma((n, lay.slots)), dma((n, lay.slots)), dma((n,)), dma((m, lay.blk - 1)), dma((m, lay.blk - 1)), dma((m,))]


DH = 64
LOG2E = math.log2(math.e)
GROUP = 256


def dot(a, b):
    return lax.dot_general(a, b, (((1,), (0,)), ((), ())), preferred_element_type=f32)


def dot_t(a, b):
    return lax.dot_general(a, b, (((1,), (1,)), ((), ())), preferred_element_type=f32)


def once(shape):
    return pl.BlockSpec(shape, lambda *_: (0,) * len(shape), pipeline_mode=pl.Buffered(1))


def attention_forward(lay, tokens, lengths, vectors, shards, parts, early):
    width = tokens.shape[2]
    seqs, span = tokens.shape[0] // lay.blk, tokens.shape[1] * lay.blk
    rows = seqs * span
    groups = width // GROUP
    scale = LOG2E / math.sqrt(DH)
    heads = seqs * GROUP // DH
    pairs = seqs * GROUP // 128
    n, p, m = len(shards), len(parts), len(vectors)
    share, deep = vectors[0].shape[0], vectors[-1].shape[0]
    slots = pairs + 3

    def kernel(len_ref, *refs):
        vecs, refs = refs[:m], refs[m:]
        tok_ref, refs = refs[0], refs[1:]
        ins, refs = refs[:n], refs[n:]
        fulls, refs = refs[:n], refs[n:]
        x_out, q_out, k_out, v_out, att_out, lse_ref, h1_out, vec_out, bias_out = refs[:9]
        x_ref, wq_ref, wk_ref, wv_ref, wo_ref, q_ref, k_ref, v_ref, att_ref, h1_ref, pack_ref, packs_ref = refs[9:21]
        load, send, recv, own, rsend, rrecv, rown = refs[21:]
        ins, fulls = list(ins) + [pack_ref], list(fulls) + [packs_ref]
        here = lay.here()
        pack_ref[...] = jnp.zeros_like(pack_ref)
        for i, vec in enumerate(vecs):
            pack_ref[i : i + 1, : vec.shape[0]] = vec[...].astype(f32).reshape(1, vec.shape[0])
        tokens_here = len_ref[0]
        for i in range(1, lengths.shape[0]):
            tokens_here = tokens_here + len_ref[i]
        pack_ref[m : m + 1] = jnp.full((1, 128), tokens_here.astype(f32))
        lay.greet(here)
        split = Resplit(lay, tok_ref, x_out, rsend, rrecv, rown)
        split.start()
        gathers = [
            Gather(lay, here, ins[a], fulls[a], cut, send.at[i], recv.at[i], own.at[i], orders)
            for i, (a, cut, orders) in enumerate(parts)
        ]
        events = skewed(gathers, 2)
        last = max(i for i, (part, stage) in enumerate(events) if part in gathers[:early] and stage == 4)
        for part, stage in events[: last + 1]:
            part.stage(stage)
        split.finish()
        loads = [
            pltpu.make_async_copy(src, dst, load.at[i])
            for i, (src, dst) in enumerate(
                zip([x_out] + list(fulls[:4]), [x_ref, wq_ref, wk_ref, wv_ref, wo_ref]))
        ]
        for c in loads:
            c.start()
        for c in loads:
            c.wait()
        hooks = Hooks()
        hooks.spread(events[last + 1 :], 0, groups * slots)
        base = lax.axis_index("blk") * seqs

        def columns(ref, g):
            block = ref[(slice(None),) * 5 + (pl.ds(pl.multiple_of(g * GROUP, GROUP), GROUP),)]
            return block.reshape(width, GROUP)

        def features(ref, g):
            per = GROUP // ref.shape[-2]
            return jnp.concatenate([ref[lay.place(g * per + j)] for j in range(per)], axis=0)

        def step(i, carry):
            g, r = i // pairs, lax.rem(i, pairs)
            cols = pl.ds(pl.multiple_of(g * GROUP, GROUP), GROUP)

            @pl.when(r == 0)
            def _():
                xv = x_ref[...].reshape(rows, width)
                for j, (low, weight) in enumerate(((q_ref, wq_ref), (k_ref, wk_ref), (v_ref, wv_ref))):
                    low[:, cols] = dot(xv, columns(weight, g)).astype(bf16)
                    hooks.at(g * slots + j, range(j, groups * slots, slots))

            @pl.when(i == groups * pairs // 2)
            def _():
                total = jnp.zeros((1, 128), f32)
                for d in range(lay.devices):
                    tile = packs_ref[lay.place(d)]
                    vec_out[0 : m - 1, d * share : (d + 1) * share] = tile[0 : m - 1, :share]
                    bias_out[:, d * deep : (d + 1) * deep] = tile[m - 1 : m, :deep]
                    total = total + tile[m : m + 1]
                inverse = 1.0 / (total / lay.blk * width)
                for d in range(width // 128):
                    vec_out[m - 1 : m, d * 128 : (d + 1) * 128] = inverse

            s, pair = r // (GROUP // 128), lax.rem(r, GROUP // 128)
            at = (pl.ds(pl.multiple_of(s * span, span), span),
                  pl.ds(pl.multiple_of(g * GROUP + pair * 128, 128), 128))
            qs, ks, vs = q_ref[at], k_ref[at], v_ref[at]
            lane = lax.broadcasted_iota(jnp.int32, (span, 128), 1)
            keep = lax.broadcasted_iota(jnp.int32, (span, 1), 0) < len_ref[base + s]
            vt = vs.T
            outs = []
            for h in range(2):
                km = jnp.where((lane < DH) if h == 0 else (lane >= DH), ks, jnp.zeros_like(ks))
                st = dot_t(km, qs) * scale
                st = jnp.where(keep, st, -1e30)
                top = jnp.max(st, axis=0, keepdims=True)
                e = jnp.exp2(st - top)
                den = jnp.sum(e, axis=0, keepdims=True)
                ot = dot(vt[h * DH : (h + 1) * DH], e.astype(bf16))
                outs.append(ot * (1.0 / den))
                lse_ref[g, pl.ds(r * 2 + h, 1)] = top + jnp.log2(den)
            att_ref[at] = jnp.concatenate(outs, axis=0).T.astype(bf16)

            @pl.when(r == pairs - 1)
            def _():
                add = dot(att_ref[:, cols], features(wo_ref, g))

                @pl.when(g == 0)
                def _():
                    h1_ref[...] = x_ref[...].reshape(rows, width).astype(f32) + add

                @pl.when(g > 0)
                def _():
                    h1_ref[...] += add

            hooks.at(g * slots + 3 + r, [k for k in range(groups * slots) if k % slots >= 3])
            return carry

        lax.fori_loop(0, groups * pairs, step, 0)
        saves = [
            pltpu.make_async_copy(src, dst, load.at[i])
            for i, (src, dst) in enumerate(
                zip([q_ref, k_ref, v_ref, att_ref, h1_ref], [q_out, k_out, v_out, att_out, h1_out]))
        ]
        for c in saves:
            c.start()
        for g in gathers:
            g.drain()
        for c in saves:
            c.wait()

    whole = [jax.ShapeDtypeStruct(lay.dims + s.shape, s.dtype) for s in shards]
    vmem = pl.BlockSpec(memory_space=pltpu.VMEM)
    act = jax.ShapeDtypeStruct((rows, width), bf16)
    return pl.pallas_call(
        kernel,
        in_specs=[pl.BlockSpec(memory_space=pltpu.SMEM)] + [vmem] * m + [ANY] * (n + 1),
        out_specs=[ANY] * (n + 5) + [vmem, ANY, vmem, vmem],
        out_shape=whole
        + [jax.ShapeDtypeStruct((seqs, span, width), bf16), act, act, act, act,
           jax.ShapeDtypeStruct((groups, heads, span), f32), jax.ShapeDtypeStruct((rows, width), f32),
           jax.ShapeDtypeStruct((8, width), f32), jax.ShapeDtypeStruct((1, deep * lay.devices), f32)],
        scratch_shapes=[pltpu.VMEM((seqs, span, width), bf16)]
        + [pltpu.VMEM(lay.dims + s.shape, bf16) for s in shards[:4]]
        + [pltpu.VMEM((rows, width), bf16)] * 4
        + [pltpu.VMEM((rows, width), f32), pltpu.VMEM((8, 128), f32), pltpu.VMEM(lay.dims + (8, 128), f32),
           pltpu.SemaphoreType.DMA((5,))]
        + sems(lay, p, 0)[:3]
        + [pltpu.SemaphoreType.DMA((lay.blk - 1,)), pltpu.SemaphoreType.DMA((lay.blk - 1,)),
           pltpu.SemaphoreType.DMA],
        compiler_params=pltpu.CompilerParams(collective_id=1, has_side_effects=True, vmem_limit_bytes=60 << 20),
        name="attention_forward",
    )(lengths, *vectors, tokens, *shards)


def attention_backward(lay, x, lengths, wq, wk, wv, wo, q, k, v, att, lse, d_branch, d_one, outer, small, orders, aside):
    seqs, span, width = x.shape
    rows = seqs * span
    heads = lse.shape[1]
    groups = width // GROUP
    pairs = seqs * GROUP // 128
    steps = pairs + 1
    depth = width // lay.devices
    scale = LOG2E / math.sqrt(DH)
    deep, share = outer.shape[1:]
    pieces, lag = 8, 3
    while deep % (pieces * 16):
        pieces //= 2
    outer_cuts = [(i * deep // pieces, deep // pieces, 0, share) for i in range(pieces)]
    small_cut = (0, 8, 0, 128)
    wo_cuts = [(0, depth, i * width // 2, width // 2) for i in range(2)]
    late_cuts = [((0, depth, c * GROUP, GROUP), c) for c in range(groups)]
    bufs = [Scatter.buffers(lay, small_cut, f32, orders)] + [Scatter.buffers(lay, c, bf16, orders) for c in wo_cuts]
    bufs += [Scatter.buffers(lay, c, bf16, orders) for c in outer_cuts]
    bufs += [Scatter.buffers(lay, c, bf16, aside) for c, _ in late_cuts for _ in range(3)]
    count = len(bufs)
    wide = deep == width
    outer = outer.reshape(lay.dims + outer.shape[1:])

    def kernel(
        len_ref, x_in, wq_ref, wk_ref, wv_ref, wo_ref, q_ref, k_ref, v_ref, att_ref, lse_ref, db_ref, d1_in, outer_in, small_in,
        gq_out, gk_out, gv_out, go_out, outer_out, small_out, dx_out,
        gq_ref, gk_ref, gv_ref, go_ref, xt_ref, do_ref, dq_ref, dk_ref, dv_ref, acc_ref, dx_ref,
        stage_small, stage_ref, send, recv, own, rsend, rrecv, rown, fetch_sem, *held,
    ):
        g = pl.program_id(0)
        here = lay.here()
        base = lax.axis_index("blk") * seqs
        made = []

        def part(grad, cut, out, way, staged=None, turn=False):
            i = len(made)
            made.append(Scatter(
                lay, here, grad, cut, out, held[4 * i : 4 * i + 4], send.at[i], recv.at[i], own.at[i], way, staged, turn))
            return made[-1]

        first = [part(small_in, small_cut, small_out, orders, stage_small)]
        first += [part(go_ref, c, go_out.at[:, pl.ds(c[2], c[3])], orders) for c in wo_cuts]
        first += [
            part(outer_in, c, outer_out.at[:, pl.ds(c[0], c[1])] if wide else outer_out.at[pl.ds(c[0], c[1])], orders,
                 stage_ref.at[i % (lag + 1)], wide)
            for i, c in enumerate(outer_cuts)
        ]
        hooks = Hooks()
        hooks.spread(skewed(first, lag)[1:], 0, groups * steps - 1)
        finals = []
        for c, group in late_cuts:
            parts = [
                part(ref, c, out.at[:, pl.ds(c[2], c[3])], aside)
                for ref, out in ((gq_ref, gq_out), (gk_ref, gk_out), (gv_ref, gv_out))
            ]
            ready = (group + 1) * steps - 1
            for stage in range(5):
                for i, p in enumerate(parts):
                    hooks.put(ready + i + 5 * stage, (p, stage))
        for k in sorted(hooks.slots):
            if k >= groups * steps - 1:
                finals += hooks.slots.pop(k)
        splits = [
            Resplit(lay, dx_ref.at[pl.ds(s, 1)], dx_out, rsend.at[s], rrecv.at[s], rown.at[s], True, s) for s in range(seqs)
        ]

        @pl.when(g == 0)
        def _():
            lay.greet(here)
            first[0].stage(0)
            fetch = [
                pltpu.make_async_copy(x_in, dx_ref, fetch_sem.at[0]),
                pltpu.make_async_copy(d1_in, acc_ref, fetch_sem.at[1]),
            ]
            for c in fetch:
                c.start()
            for c in fetch:
                c.wait()
            for s in range(seqs):
                xt_ref[:, s * span : (s + 1) * span] = dx_ref[s].T

            def output_rows(j, carry):
                cols = pl.ds(pl.multiple_of(j * GROUP, GROUP), GROUP)
                value = dot(att_ref[:, cols].T, db_ref[...].reshape(rows, width)).astype(bf16)
                for d in range(GROUP // depth):
                    go_ref[lay.place(j * (GROUP // depth) + d)] = value[d * depth : (d + 1) * depth]
                return carry

            lax.fori_loop(0, groups, output_rows, 0)

        do_ref[...] = dot_t(db_ref[...].reshape(rows, width), wo_ref[...]).astype(bf16)

        def pair_step(i, carry):
            s, pair = i // (GROUP // 128), lax.rem(i, GROUP // 128)
            at = (pl.ds(pl.multiple_of(s * span, span), span), pl.ds(pl.multiple_of(pair * 128, 128), 128))
            length = len_ref[base + s]
            qs, ks, vs, dos = q_ref[at], k_ref[at], v_ref[at], do_ref[at]
            lane = lax.broadcasted_iota(jnp.int32, (span, 128), 1)
            keep = lax.broadcasted_iota(jnp.int32, (span, 1), 0) < length
            kt = ks.T
            dqs, dks, dvs = [], [], []
            for h in range(2):
                mine = (lane < DH) if h == 0 else (lane >= DH)
                zero = jnp.zeros_like(ks)
                st = dot_t(jnp.where(mine, ks, zero), qs) * scale
                p = jnp.where(keep, jnp.exp2(st - lse_ref[0, pl.ds(i * 2 + h, 1)]), 0.0)
                dp = dot_t(jnp.where(mine, vs, zero), dos)
                delta = jnp.sum(p * dp, axis=0, keepdims=True)
                ds = (p * (dp - delta)).astype(bf16)
                dvs.append(dot(p.astype(bf16), dos))
                dks.append(dot(ds, qs))
                dqs.append(dot(kt[h * DH : (h + 1) * DH], ds))
            low_half = lane < DH
            unit = 1.0 / math.sqrt(DH)
            dv_ref[at] = jnp.where(low_half, dvs[0], dvs[1]).astype(bf16)
            dk_ref[at] = (jnp.where(low_half, dks[0], dks[1]) * unit).astype(bf16)
            dq_ref[at] = (jnp.concatenate(dqs, axis=0).T * unit).astype(bf16)

            @pl.when(pair == GROUP // 128 - 1)
            def _():
                mine = at[0]
                acc_ref[mine] += (
                    dot_t(dq_ref[mine], wq_ref[...]) + dot_t(dk_ref[mine], wk_ref[...]) + dot_t(dv_ref[mine], wv_ref[...])
                )

            for n in range(seqs):
                @pl.when((g == groups - 1) & (i == (n + 1) * (GROUP // 128) - 1))
                def _():
                    dx_ref[n] = acc_ref[n * span : (n + 1) * span].astype(bf16)
                    splits[n].start()

            hooks.at(g * steps + i, [k for k in range(groups * steps) if k % steps < pairs])
            return carry

        lax.fori_loop(0, pairs, pair_step, 0)
        xt = xt_ref[...]
        cols = (slice(None),) * 5 + (pl.ds(pl.multiple_of(g * GROUP, GROUP), GROUP),)
        for grad, low in ((gq_ref, dq_ref), (gk_ref, dk_ref), (gv_ref, dv_ref)):
            grad[cols] = dot(xt, low[...]).astype(bf16).reshape(lay.dims + (depth, GROUP))
        hooks.at(g * steps + pairs, [k for k in range(groups * steps) if k % steps == pairs])

        @pl.when(g == groups - 1)
        def _():
            for p, stage in finals:
                p.stage(stage)
            for p in made:
                p.drain()
            for split in splits:
                split.finish()

    col = pl.BlockSpec((width, GROUP), lambda g, *_: (0, g))
    row = pl.BlockSpec((GROUP, width), lambda g, *_: (g, 0))
    act = pl.BlockSpec((rows, GROUP), lambda g, *_: (0, g))
    vmem = pl.BlockSpec(memory_space=pltpu.VMEM)
    grad = pltpu.VMEM(lay.dims + (depth, width), bf16)
    no_core = tuple(lay.size[n] for n in lay.order if n != "c")
    shard = jax.ShapeDtypeStruct((depth, width), f32)
    return pl.pallas_call(
        kernel,
        grid_spec=pltpu.PrefetchScalarGridSpec(
            num_scalar_prefetch=0,
            grid=(groups,),
            in_specs=[pl.BlockSpec(memory_space=pltpu.SMEM), ANY, col, col, col, row, act, act, act, once((rows, width)),
                      pl.BlockSpec((1, heads, span), lambda g, *_: (g, 0, 0)), once((seqs, span, width)), ANY, ANY, ANY],
            out_specs=[once((depth, width))] * 4 + [once((share, deep) if wide else (deep, share)), once((8, 128)), ANY],
            scratch_shapes=[grad] * 4
            + [pltpu.VMEM((width, rows), bf16)] + [pltpu.VMEM((rows, GROUP), bf16)] * 4
            + [pltpu.VMEM((rows, width), f32), pltpu.VMEM((seqs, span, width), bf16)]
            + [pltpu.VMEM(no_core + (8, 128), f32)] + [pltpu.VMEM((lag + 1,) + no_core + (deep // pieces, share), bf16)]
            + sems(lay, count, 0)[:3]
            + sems(lay, 0, seqs)[3:] + [pltpu.SemaphoreType.DMA((2,))]
            + [b for bs in bufs for b in bs],
        ),
        out_shape=[shard] * 4
        + [jax.ShapeDtypeStruct((share, deep) if wide else (deep, share), f32), jax.ShapeDtypeStruct((8, 128), f32),
           jax.ShapeDtypeStruct((seqs * lay.blk, span // lay.blk, width), bf16)],
        compiler_params=pltpu.CompilerParams(
            collective_id=3, has_side_effects=True, vmem_limit_bytes=63 << 20),
        name="attention_backward",
    )(lengths, x, wq, wk, wv, wo, q, k, v, att, lse, d_branch, d_one, outer, small)


TILE = 512
CHUNK = 512


def feed_forward(lay, h1, teacher, out_grad, lengths, vecs, bias_inner, w1, w2, orders):
    rows, width = h1.shape
    hidden = w1.shape[1]
    seqs = teacher.shape[0] // lay.blk
    span = rows // seqs
    devices = lay.devices
    tiles = hidden // TILE
    share, share1 = hidden // devices, width // devices
    per_tile = TILE // share
    wide = share % 128 == 0
    pieces, depth, lag, kept = tiles, width // devices, 3, 4
    columns = hidden // pieces
    bufs = Scatter.buffers(lay, (0, depth, 0, columns), bf16, orders)

    def kernel(
        len_ref, h1_ref, teach_in, og_in, vec_ref, b1_ref, w1_ref, w2_ref,
        layer_out, d1_ref, db_out, gw1_out, gw2_ref, small_ref,
        low_ref, lowt_ref, act_ref, slope_ref, acc_ref, do_ref, dot_ref, inv1_ref, di_ref, db_ref, gw1_ref, sums_ref, gb1_ref,
        rsend, rrecv, rown, send, recv, own, *held,
    ):
        t = pl.program_id(0)
        here = lay.here()
        base = lax.axis_index("blk") * seqs
        splits = [
            Resplit(lay, src, dst, rsend.at[i], rrecv.at[i], rown.at[i], i == 2)
            for i, (src, dst) in enumerate(((teach_in, do_ref), (og_in, db_ref), (low_ref, layer_out)))
        ]
        sums = [
            Scatter(
                lay, here, gw1_ref.at[i % kept], (0, depth, 0, columns), gw1_out.at[:, pl.ds(i * columns, columns)],
                held[4 * i : 4 * i + 4], send.at[i], recv.at[i], own.at[i], orders)
            for i in range(pieces)
        ]
        hooks = Hooks()
        for slot in range(pieces + 4 * lag):
            for i in range(pieces):
                stage, rest = divmod(slot - i, lag)
                if rest == 0 and 0 <= stage < 5:
                    hooks.put(slot, (sums[i], stage))
        last = max(hooks.slots)
        span_of = lambda row: (row // span, pl.ds(row % span, CHUNK))
        gain1, shift1 = vec_ref[0:1], vec_ref[1:2]
        bias2, gain2, shift2 = vec_ref[2:3], vec_ref[3:4], vec_ref[4:5]

        @pl.when(t == 0)
        def _():
            lay.greet(here)
            splits[0].start()
            splits[1].start()
            fetch = pltpu.make_async_copy(h1_ref, d1_ref, own.at[pieces])
            fetch.start()
            fetch.wait()
            sums_ref[...] = jnp.zeros_like(sums_ref)

            def norm(i, carry):
                at = pl.ds(pl.multiple_of(i * 128, 128), 128)
                seq = (i * 128) // span
                there = (seq, pl.ds(pl.multiple_of(i * 128 - seq * span, 128), 128))
                h = d1_ref[at]
                centred = h - jnp.mean(h, axis=-1, keepdims=True)
                inverse = lax.rsqrt(jnp.mean(centred * centred, axis=-1, keepdims=True) + 1e-12)
                normal = centred * inverse
                d1_ref[at] = normal
                inv1_ref[at] = inverse
                low = (normal * gain1 + shift1).astype(bf16)
                low_ref[there] = low
                lowt_ref[:, at] = low.T
                return carry

            lax.fori_loop(0, rows // 128, norm, 0)
            acc_ref[...] = jnp.zeros_like(acc_ref)

        @pl.when(t < tiles)
        def _():
            for i in range(rows // CHUNK):
                at = slice(i * CHUNK, (i + 1) * CHUNK)
                inner = dot(low_ref[span_of(i * CHUNK)], w1_ref[...]) + b1_ref[...]
                cum = 0.5 * (1.0 + lax.erf(inner * (1.0 / math.sqrt(2.0))))
                density = jnp.exp(-0.5 * inner * inner) * (1.0 / math.sqrt(2.0 * math.pi))
                active = (inner * cum).astype(bf16)
                act_ref[t, at] = active
                slope_ref[t, at] = (cum + inner * density).astype(bf16)
                acc_ref[at] += dot(active, w2_ref[...])

        @pl.when(t == tiles)
        def _():
            inv = vec_ref[5:6]
            splits[0].finish()
            splits[1].finish()

            def middle(i, carry):
                at = pl.ds(pl.multiple_of(i * 128, 128), 128)
                normed = d1_ref[at] * gain1 + shift1
                h2 = normed + acc_ref[at] + bias2
                centred = h2 - jnp.mean(h2, axis=-1, keepdims=True)
                inverse = lax.rsqrt(jnp.mean(centred * centred, axis=-1, keepdims=True) + 1e-12)
                normal = centred * inverse
                result = normal * gain2 + shift2
                seq = (i * 128) // span
                first = i * 128 - seq * span
                there = (seq, pl.ds(pl.multiple_of(first, 128), 128))
                low_ref[there] = result.astype(bf16)
                pos = first + lax.broadcasted_iota(jnp.int32, (128, 1), 0)
                valid = (pos < len_ref[base + seq]).astype(f32)
                deviation = (result - do_ref[there].astype(f32)) * valid
                grad = db_ref[there].astype(f32) * valid + (2.0 * inv) * deviation
                sums_ref[0:1] += jnp.sum(deviation * deviation, axis=0, keepdims=True)
                sums_ref[1:2] += jnp.sum(grad * normal, axis=0, keepdims=True)
                sums_ref[2:3] += jnp.sum(grad, axis=0, keepdims=True)
                scaled = grad * gain2
                mean = jnp.mean(scaled, axis=-1, keepdims=True)
                along = jnp.mean(scaled * normal, axis=-1, keepdims=True)
                d_two = inverse * (scaled - mean - normal * along)
                acc_ref[at] = d_two
                low = d_two.astype(bf16)
                sums_ref[3:4] += jnp.sum(low.astype(f32), axis=0, keepdims=True)
                do_ref[there] = low
                dot_ref[:, at] = low.T
                return carry

            lax.fori_loop(0, rows // 128, middle, 0)
            splits[2].start()

        @pl.when((t > tiles) & (t <= 2 * tiles))
        def _():
            j = t - tiles - 1
            total = jnp.zeros((1, TILE), f32)
            for i in range(rows // CHUNK):
                at = slice(i * CHUNK, (i + 1) * CHUNK)
                d_act = dot_t(do_ref[span_of(i * CHUNK)], w2_ref[...])
                d_in = (d_act * slope_ref[j, at].astype(f32)).astype(bf16)
                total += jnp.sum(d_in.astype(f32), axis=0, keepdims=True)
                di_ref[at] = d_in
                acc_ref[at] += dot_t(d_in, w1_ref[...])
            gb1_ref[:, pl.ds(pl.multiple_of(j * TILE, TILE), TILE)] = total
            value = dot(lowt_ref[...], di_ref[...]).astype(bf16)
            gw1_ref[lax.rem(j, kept)] = value.reshape(lay.dims + (depth, TILE))
            hooks.at(j, range(tiles))

        @pl.when(t == 2 * tiles)
        def _():
            def back(i, carry):
                at = pl.ds(pl.multiple_of(i * 128, 128), 128)
                seq = (i * 128) // span
                there = (seq, pl.ds(pl.multiple_of(i * 128 - seq * span, 128), 128))
                grad, normal = acc_ref[at], d1_ref[at]
                sums_ref[4:5] += jnp.sum(grad * normal, axis=0, keepdims=True)
                sums_ref[5:6] += jnp.sum(grad, axis=0, keepdims=True)
                scaled = grad * gain1
                mean = jnp.mean(scaled, axis=-1, keepdims=True)
                along = jnp.mean(scaled * normal, axis=-1, keepdims=True)
                d_one = inv1_ref[at] * (scaled - mean - normal * along)
                d1_ref[at] = d_one
                db_ref[there] = d_one.astype(bf16)
                return carry

            lax.fori_loop(0, rows // 128, back, 0)

        @pl.when(t > 2 * tiles)
        def _():
            j = t - 2 * tiles - 1
            gw2 = dot(dot_ref[...], act_ref[j]).astype(bf16)
            if wide:
                for d in range(per_tile):
                    gw2_ref[d] = gw2[:, d * share : (d + 1) * share]
            else:
                gw2_ref[...] = gw2
            hooks.at(t - tiles - 1, range(tiles, 2 * tiles))

        @pl.when(t == 2 * tiles + 1)
        def _():
            small_ref[...] = jnp.zeros_like(small_ref)
            loss = jnp.broadcast_to(jnp.sum(sums_ref[0:1], axis=-1, keepdims=True), (1, 128))
            for d in range(devices):
                at = lay.place(d)
                small_ref[at + (slice(0, 5), slice(0, share1))] = sums_ref[1:6, d * share1 : (d + 1) * share1]
                small_ref[at + (slice(5, 6), slice(0, share))] = gb1_ref[:, d * share : (d + 1) * share]
                small_ref[at + (slice(6, 7),)] = loss

        @pl.when(t == 3 * tiles)
        def _():
            save = pltpu.make_async_copy(db_ref, db_out, own.at[pieces])
            save.start()
            for k in range(2 * tiles, last + 1):
                hooks.run(k)
            for part in sums:
                part.drain()
            splits[2].finish()
            save.wait()

    def tile(t, *_):
        return jnp.where(t < tiles, t, jnp.clip(t - tiles - 1, 0, tiles - 1))

    def outer_tile(t, *_):
        return jnp.maximum(t - 2 * tiles - 1, 0)

    full = once((rows, width))
    vec = pl.BlockSpec((1, TILE), lambda t, *_: (0, tile(t)))
    low = pltpu.VMEM((seqs, span, width), bf16)
    return pl.pallas_call(
        kernel,
        grid_spec=pltpu.PrefetchScalarGridSpec(
            num_scalar_prefetch=0,
            grid=(3 * tiles + 1,),
            in_specs=[
                pl.BlockSpec(memory_space=pltpu.SMEM), ANY, ANY, ANY, once((8, width)), vec,
                pl.BlockSpec((width, TILE), lambda t, *_: (0, tile(t))),
                pl.BlockSpec((TILE, width), lambda t, *_: (tile(t), 0)),
            ],
            out_specs=[
                ANY, full, ANY, once((depth, hidden)),
                pl.BlockSpec((per_tile, width, share), lambda t, *_: (outer_tile(t), 0, 0))
                if wide else pl.BlockSpec((width, TILE), lambda t, *_: (0, outer_tile(t))),
                once(lay.dims + (8, 128)),
            ],
            scratch_shapes=[
                low, pltpu.VMEM((width, rows), bf16),
                pltpu.VMEM((tiles, rows, TILE), bf16), pltpu.VMEM((tiles, rows, TILE), bf16),
                pltpu.VMEM((rows, width), f32), low, pltpu.VMEM((width, rows), bf16),
                pltpu.VMEM((rows, 1), f32), pltpu.VMEM((rows, TILE), bf16), low,
                pltpu.VMEM((kept,) + lay.dims + (depth, columns), bf16),
                pltpu.VMEM((8, width), f32), pltpu.VMEM((1, hidden), f32),
            ]
            + sems(lay, 0, 3)[3:]
            + sems(lay, pieces + 1, 0)[:3]
            + bufs * pieces,
        ),
        out_shape=[
            jax.ShapeDtypeStruct(teacher.shape, bf16),
            jax.ShapeDtypeStruct((rows, width), f32),
            jax.ShapeDtypeStruct((seqs, span, width), bf16),
            jax.ShapeDtypeStruct((depth, hidden), f32),
            jax.ShapeDtypeStruct((devices, width, share) if wide else (width, hidden), bf16),
            jax.ShapeDtypeStruct(lay.dims + (8, 128), f32),
        ],
        compiler_params=pltpu.CompilerParams(
            collective_id=2, has_side_effects=True, vmem_limit_bytes=63 << 20),
        name="feed_forward",
    )(lengths, h1, teacher, out_grad, vecs, bias_inner, w1, w2)


def cut(shape, which, pieces, orders, columns=False):
    rows, wide = shape
    if columns:
        step = wide // pieces
        return [(which, (0, rows, i * step, step), orders) for i in range(pieces)]
    while pieces > 1 and rows % (pieces * 16):
        pieces -= 1
    step = rows // pieces
    return [(which, (i * step, step), orders) for i in range(pieces)]


def shards(
    lay, tokens, lengths, teacher, out_grad, w_query, w_key, w_value, w_output, gain_one, shift_one,
    w_inner, bias_inner, w_outer, bias_outer, gain_two, shift_two,
):
    width = tokens.shape[2]
    hidden = w_inner.shape[1]
    devices = lay.devices
    there = (("z", "x", "y"), ("z", "y", "x"))
    back = (("y", "x", "z"), ("x", "y", "z"))
    aside = (("x", "y", "z"),) * 2
    share, deep = gain_one.shape[0], bias_inner.shape[0]
    ins = [w_query, w_key, w_value, w_output, w_inner, w_outer]
    parts = [(6, (0, 8), there)]
    for i in range(4):
        parts += cut(ins[i].shape, i, 1, there)
    early = len(parts)
    parts += cut(w_inner.shape, 4, 8, there, True) + cut(w_outer.shape, 5, 8, there)
    vectors = [gain_one, shift_one, bias_outer, gain_two, shift_two, bias_inner]
    wq, wk, wv, wo, w1, w2, x, q, k, v, att, lse, h1, vecs, bias1 = attention_forward(
        lay, tokens, lengths, vectors, ins, parts, early
    )
    wq, wk, wv, wo = (w.reshape(width, width) for w in (wq, wk, wv, wo))
    w1, w2 = w1.reshape(width, hidden), w2.reshape(hidden, width)
    layer_out, d_one, d_branch, g_inner, gw2, small = feed_forward(
        lay, h1, teacher, out_grad, lengths, vecs, bias1, w1, w2, aside
    )
    if gw2.ndim == 2:
        gw2 = gw2.T.reshape(devices, hidden // devices, width)
    g_query, g_key, g_value, g_output, g_outer, small, d_tokens = attention_backward(
        lay, x, lengths, wq, wk, wv, wo, q, k, v, att, lse, d_branch, d_one, gw2, small, back, aside
    )
    vec = lambda i: small[i, :share]
    return (
        small[6, 0] * vecs[5, 0],
        layer_out,
        d_tokens.astype(f32),
        g_query,
        g_key,
        g_value,
        g_output,
        vec(3),
        vec(4),
        g_inner,
        small[5, :deep],
        g_outer,
        vec(2),
        vec(0),
        vec(1),
    )


def solution(mesh):
    lay = Layout(mesh)
    rows = P("dp", "blk", None)
    weight = P(("dp", "blk"), None)
    vector = P(("dp", "blk"))
    return jax.shard_map(
        lambda *args: shards(lay, *args),
        mesh=mesh,
        in_specs=(
            rows, P("dp"), rows, rows, weight, weight, weight, weight, vector, vector,
            weight, vector, weight, vector, vector, vector,
        ),
        out_specs=(
            P(), rows, rows, weight, weight, weight, weight, vector, vector,
            weight, vector, weight, vector, vector, vector,
        ),
        check_vma=False,
    )
```

time: 454 us -> 411 us (0.905); the launches traced: 454 us -> 405 us
  Pallas kernels: 423 us -> 389 us
  local copies, waits for them, and re-layouts: 18.6 us -> 8.98 us
    pallas_call x1 -> x0, Pallas kernels: 72.6 us -> none  [scatter_call(): pl.pallas_call(kernel, out_shape=outs, in_specs=[ANY] * (n + m), out_spec...]
    pallas_call x1, Pallas kernels: 105 us -> 134 us  [feed_forward(): pl.pallas_call(kernel, grid_spec=pltpu.PrefetchScalarGridSpec(num_scalar_...]
    pallas_call x1, Pallas kernels: 104 us -> 111 us  [attention_backward(): pl.pallas_call(kernel, grid_spec=pltpu.PrefetchScalarGridSpec(num_scalar_...]
    concatenate x2 -> x0, local copies, waits for them, and re-layouts: 4.81 us -> none  [the longest x1 4.09 us: shards(): jnp.concatenate([v.astype(f32) for v in (gain_one, shift_one, bias_outer,...]
where the time goes in v3:
time: 411 us; the launch traced here: 405 us
  Pallas kernels  389 us (95%)
  local copies, waits for them, and re-layouts  8.98 us (2%)
  other arithmetic  4.22 us (1%)
    pallas_call x1, Pallas kernels, attention_forward(): pl.pallas_call(kernel, in_specs=[pl.BlockSpec(memory_space=pltpu.SMEM)] +...  144 us
    pallas_call x1, Pallas kernels, feed_forward(): pl.pallas_call(kernel, grid_spec=pltpu.PrefetchScalarGridSpec(num_scalar_...  134 us
    pallas_call x1, Pallas kernels, attention_backward(): pl.pallas_call(kernel, grid_spec=pltpu.PrefetchScalarGridSpec(num_scalar_...  111 us

profile of v3, /device:TPU:0, one launch (start us, length us, event | category | flops | bytes accessed | tf_op | source)
XLA Modules:
  0.0 404.9 jit_solution(11577273019137633943)
XLA Ops:
  0.7 143.7 %attention_forward.1 = (bf16[4,2,2,2,32,1024]{5,4,3,2,1,0:T(8,128)(2,1)}, bf16[4,2,2,2,32,1024]{5,4,3,2,1,0:T(8,128)(2,1)}, bf16[4,2,2,2,32,1024]{5,4,3,2,1,0:T(...) custom-call(s32[8]{0:T(128)} %len_ref.5, ...), custom_call_target="tpu_custom_call" | custom-call | tf_op jit(solution)/shard_map/attention_forward/pallas_call | solution.py:494
  144.4 134.2 %feed_forward.1 = (bf16[8,128,1024]{2,1,0:T(8,128)(2,1)}, f32[1024,1024]{1,0:T(8,128)}, bf16[2,512,1024]{2,1,0:T(8,128)(2,1)}, f32[32,4096]{1,0:T(8,128)}, bf16[...) custom-call(s32[8]{0:T(128)} %len_ref.5, f32[1024,1024]{1,0:T(8,128)} %get-tuple-element.53.h1_ref, ...), custom_call_target="tpu_custom_call" | custom-call | tf_op jit(solution)/shard_map/feed_forward/pallas_call | solution.py:901
  278.6 110.6 %attention_backward.1 = (f32[32,1024]{1,0:T(8,128)}, f32[32,1024]{1,0:T(8,128)}, f32[32,1024]{1,0:T(8,128)}, f32[32,1024]{1,0:T(8,128)}, f32[128,1024]{1,0:T(8,1...) custom-call(s32[8]{0:T(128)} %len_ref.5, bf16[2,512,1024]{2,1,0:T(8,128)(2,1)} %get-tuple-element.43.x_in, ...), custom_call_target="tpu_custom_call" | custom-call | tf_op jit(solution)/shard_map/attention_backward/pallas_call | solution.py:673
  389.2 1.2 slice.24
  390.4 1.2 slice.25
  392.9 0.0 copy-start.7
  392.9 0.0 copy-start
  392.9 4.2 %convert_element_type.3 = f32[8,128,1024]{2,1,0:T(8,128)} convert(bf16[8,128,1024]{2,1,0:T(8,128)(2,1)} %get-tuple-element.64) | non-fusion elementwise | flops 1048576 | bytes 6291456 | tf_op jit(solution)/shard_map/convert_element_type | solution.py:989
  397.1 0.0 copy-done.7
  397.1 0.5 slice_bitcast_fusion
  397.7 0.5 slice_bitcast_fusion.3
  398.2 0.0 copy-done
  398.2 0.0 copy-start.6
  398.2 0.0 copy-start.5
  398.2 0.0 copy-start.4
  398.2 0.0 copy-start.3
  398.2 0.0 copy-start.1
  398.2 1.3 copy.38
  399.5 0.0 copy-done.6
  399.5 0.0 copy-start.2
  399.5 0.7 copy.39
  400.2 0.0 copy-done.5
  400.2 0.7 copy.40
  400.9 0.0 copy-done.4
  400.9 0.7 copy.41
  401.5 0.0 copy-done.3
  401.5 0.7 copy.42
  402.2 0.0 copy-done.1
  402.2 0.8 copy.43
  403.0 0.0 copy-done.2
  403.0 0.8 copy.44
Async XLA Ops:
  392.9 4.2 %copy-start.7 = (f32[8,128]{1,0:T(8,128)S(1)}, f32[8,128]{1,0:T(8,128)}, u32[]{:S(2)}) copy-start(f32[8,128]{1,0:T(8,128)} %get-tuple-element.62) | copy-start | bytes 12292
  392.9 5.3 %copy-start = (bf16[8,128,1024]{2,1,0:T(8,128)(2,1)S(1)}, bf16[8,128,1024]{2,1,0:T(8,128)(2,1)}, u32[]{:S(2)}) copy-start(bf16[8,128,1024]{2,1,0:T(8,128)(2,1)} %get-tuple-element.92) | copy-start | bytes 6291460
  398.2 1.4 copy-start.6
  398.2 2.0 copy-start.5
  398.2 2.7 copy-start.4
  398.2 3.3 copy-start.3
  398.2 4.0 copy-start.1
  399.5 3.4 copy-start.2

commit v4 on v3

--- a/solution.py
+++ b/solution.py
@@ -156,13 +156,14 @@
         self.me = lax.axis_index("blk")
         self.back = back
         self.seqs = (src if back else dst).shape[0]
+        self.total = (dst if back else src).shape[0] // lay.blk
         self.span = (dst if back else src).shape[1]
 
     def ends(self, there):
         if self.back:
             return (self.src.at[:, pl.ds(there * self.span, self.span)],
-                    self.dst.at[pl.ds(self.me * (self.dst.shape[0] // self.lay.blk) + self.first, self.seqs)])
-        return (self.src.at[pl.ds(there * self.seqs, self.seqs)],
+                    self.dst.at[pl.ds(self.me * self.total + self.first, self.seqs)])
+        return (self.src.at[pl.ds(there * self.total + self.first, self.seqs)],
                 self.dst.at[:, pl.ds(self.me * self.span, self.span)])
 
     def copies(self):
@@ -385,7 +386,7 @@
             tokens_here = tokens_here + len_ref[i]
         pack_ref[m : m + 1] = jnp.full((1, 128), tokens_here.astype(f32))
         lay.greet(here)
-        split = Resplit(lay, tok_ref, x_out, rsend, rrecv, rown)
+        split = Resplit(lay, tok_ref, x_ref, rsend, rrecv, rown)
         split.start()
         gathers = [
             Gather(lay, here, ins[a], fulls[a], cut, send.at[i], recv.at[i], own.at[i], orders)
@@ -399,14 +400,14 @@
         loads = [
             pltpu.make_async_copy(src, dst, load.at[i])
             for i, (src, dst) in enumerate(
-                zip([x_out] + list(fulls[:4]), [x_ref, wq_ref, wk_ref, wv_ref, wo_ref]))
+                zip(fulls[:4], [wq_ref, wk_ref, wv_ref, wo_ref]))
         ]
         for c in loads:
             c.start()
         for c in loads:
             c.wait()
         hooks = Hooks()
-        hooks.spread(events[last + 1 :], 0, groups * slots)
+        hooks.spread(events[last + 1 :], 0, groups * slots * 4 // 3)
         base = lax.axis_index("blk") * seqs
 
         def columns(ref, g):
@@ -479,10 +480,13 @@
         saves = [
             pltpu.make_async_copy(src, dst, load.at[i])
             for i, (src, dst) in enumerate(
-                zip([q_ref, k_ref, v_ref, att_ref, h1_ref], [q_out, k_out, v_out, att_out, h1_out]))
+                zip([x_ref, q_ref, k_ref, v_ref, att_ref, h1_ref], [x_out, q_out, k_out, v_out, att_out, h1_out]))
         ]
         for c in saves:
             c.start()
+        for k in sorted(hooks.slots):
+            if k >= groups * slots:
+                hooks.run(k)
         for g in gathers:
             g.drain()
         for c in saves:
@@ -493,7 +497,7 @@
     act = jax.ShapeDtypeStruct((rows, width), bf16)
     return pl.pallas_call(
         kernel,
-        in_specs=[pl.BlockSpec(memory_space=pltpu.SMEM)] + [vmem] * m + [ANY] * (n + 1),
+        in_specs=[pl.BlockSpec(memory_space=pltpu.SMEM)] + [vmem] * m + [ANY] + [vmem] * n,
         out_specs=[ANY] * (n + 5) + [vmem, ANY, vmem, vmem],
         out_shape=whole
         + [jax.ShapeDtypeStruct((seqs, span, width), bf16), act, act, act, act,
@@ -503,7 +507,7 @@
         + [pltpu.VMEM(lay.dims + s.shape, bf16) for s in shards[:4]]
         + [pltpu.VMEM((rows, width), bf16)] * 4
         + [pltpu.VMEM((rows, width), f32), pltpu.VMEM((8, 128), f32), pltpu.VMEM(lay.dims + (8, 128), f32),
-           pltpu.SemaphoreType.DMA((5,))]
+           pltpu.SemaphoreType.DMA((6,))]
         + sems(lay, p, 0)[:3]
         + [pltpu.SemaphoreType.DMA((lay.blk - 1,)), pltpu.SemaphoreType.DMA((lay.blk - 1,)),
            pltpu.SemaphoreType.DMA],
@@ -529,8 +533,8 @@
     small_cut = (0, 8, 0, 128)
     wo_cuts = [(0, depth, i * width // 2, width // 2) for i in range(2)]
     late_cuts = [((0, depth, c * GROUP, GROUP), c) for c in range(groups)]
-    bufs = [Scatter.buffers(lay, small_cut, f32, orders)] + [Scatter.buffers(lay, c, bf16, orders) for c in wo_cuts]
-    bufs += [Scatter.buffers(lay, c, bf16, orders) for c in outer_cuts]
+    bufs = [Scatter.buffers(lay, c, bf16, orders) for c in outer_cuts + wo_cuts]
+    bufs += [Scatter.buffers(lay, small_cut, f32, orders)]
     bufs += [Scatter.buffers(lay, c, bf16, aside) for c, _ in late_cuts for _ in range(3)]
     count = len(bufs)
     wide = deep == width
@@ -553,15 +557,16 @@
                 lay, here, grad, cut, out, held[4 * i : 4 * i + 4], send.at[i], recv.at[i], own.at[i], way, staged, turn))
             return made[-1]
 
-        first = [part(small_in, small_cut, small_out, orders, stage_small)]
-        first += [part(go_ref, c, go_out.at[:, pl.ds(c[2], c[3])], orders) for c in wo_cuts]
-        first += [
+        first = [
             part(outer_in, c, outer_out.at[:, pl.ds(c[0], c[1])] if wide else outer_out.at[pl.ds(c[0], c[1])], orders,
                  stage_ref.at[i % (lag + 1)], wide)
             for i, c in enumerate(outer_cuts)
         ]
+        first += [part(go_ref, c, go_out.at[:, pl.ds(c[2], c[3])], orders) for c in wo_cuts]
+        first += [part(small_in, small_cut, small_out, orders, stage_small)]
         hooks = Hooks()
-        hooks.spread(skewed(first, lag)[1:], 0, groups * steps - 1)
+        events = skewed(first, lag)
+        hooks.spread(events[lag:], 0, groups * steps - 1)
         finals = []
         for c, group in late_cuts:
             parts = [
@@ -571,7 +576,7 @@
             ready = (group + 1) * steps - 1
             for stage in range(5):
                 for i, p in enumerate(parts):
-                    hooks.put(ready + i + 5 * stage, (p, stage))
+                    hooks.put(ready + i + 3 * stage, (p, stage))
         for k in sorted(hooks.slots):
             if k >= groups * steps - 1:
                 finals += hooks.slots.pop(k)
@@ -582,7 +587,8 @@
         @pl.when(g == 0)
         def _():
             lay.greet(here)
-            first[0].stage(0)
+            for p, stage in events[:lag]:
+                p.stage(stage)
             fetch = [
                 pltpu.make_async_copy(x_in, dx_ref, fetch_sem.at[0]),
                 pltpu.make_async_copy(d1_in, acc_ref, fetch_sem.at[1]),
@@ -709,7 +715,7 @@
     share, share1 = hidden // devices, width // devices
     per_tile = TILE // share
     wide = share % 128 == 0
-    pieces, depth, lag, kept = tiles, width // devices, 3, 4
+    pieces, depth, lag, kept = tiles, width // devices, 2, 4
     columns = hidden // pieces
     bufs = Scatter.buffers(lay, (0, depth, 0, columns), bf16, orders)
 
@@ -722,10 +728,11 @@
         t = pl.program_id(0)
         here = lay.here()
         base = lax.axis_index("blk") * seqs
-        splits = [
-            Resplit(lay, src, dst, rsend.at[i], rrecv.at[i], rown.at[i], i == 2)
-            for i, (src, dst) in enumerate(((teach_in, do_ref), (og_in, db_ref), (low_ref, layer_out)))
+        rows_in = [
+            Resplit(lay, src, dst.at[pl.ds(n, 1)], rsend.at[2 * n + i], rrecv.at[2 * n + i], rown.at[2 * n + i], first=n)
+            for n in range(seqs) for i, (src, dst) in enumerate(((teach_in, do_ref), (og_in, db_ref)))
         ]
+        rows_out = Resplit(lay, low_ref, layer_out, rsend.at[2 * seqs], rrecv.at[2 * seqs], rown.at[2 * seqs], True)
         sums = [
             Scatter(
                 lay, here, gw1_ref.at[i % kept], (0, depth, 0, columns), gw1_out.at[:, pl.ds(i * columns, columns)],
@@ -746,8 +753,8 @@
         @pl.when(t == 0)
         def _():
             lay.greet(here)
-            splits[0].start()
-            splits[1].start()
+            for split in rows_in[:2]:
+                split.start()
             fetch = pltpu.make_async_copy(h1_ref, d1_ref, own.at[pieces])
             fetch.start()
             fetch.wait()
@@ -771,6 +778,12 @@
             lax.fori_loop(0, rows // 128, norm, 0)
             acc_ref[...] = jnp.zeros_like(acc_ref)
 
+        for n in range(1, seqs):
+            @pl.when(t == n * tiles // seqs)
+            def _():
+                for split in rows_in[2 * n : 2 * n + 2]:
+                    split.start()
+
         @pl.when(t < tiles)
         def _():
             for i in range(rows // CHUNK):
@@ -786,8 +799,6 @@
         @pl.when(t == tiles)
         def _():
             inv = vec_ref[5:6]
-            splits[0].finish()
-            splits[1].finish()
 
             def middle(i, carry):
                 at = pl.ds(pl.multiple_of(i * 128, 128), 128)
@@ -819,8 +830,11 @@
                 dot_ref[:, at] = low.T
                 return carry
 
-            lax.fori_loop(0, rows // 128, middle, 0)
-            splits[2].start()
+            for n in range(seqs):
+                for split in rows_in[2 * n : 2 * n + 2]:
+                    split.finish()
+                lax.fori_loop(n * span // 128, (n + 1) * span // 128, middle, 0)
+            rows_out.start()
 
         @pl.when((t > tiles) & (t <= 2 * tiles))
         def _():
@@ -886,7 +900,7 @@
                 hooks.run(k)
             for part in sums:
                 part.drain()
-            splits[2].finish()
+            rows_out.finish()
             save.wait()
 
     def tile(t, *_):
@@ -922,7 +936,7 @@
                 pltpu.VMEM((kept,) + lay.dims + (depth, columns), bf16),
                 pltpu.VMEM((8, width), f32), pltpu.VMEM((1, hidden), f32),
             ]
-            + sems(lay, 0, 3)[3:]
+            + sems(lay, 0, 2 * seqs + 1)[3:]
             + sems(lay, pieces + 1, 0)[:3]
             + bufs * pieces,
         ),
@@ -938,6 +952,39 @@
             collective_id=2, has_side_effects=True, vmem_limit_bytes=63 << 20),
         name="feed_forward",
     )(lengths, h1, teacher, out_grad, vecs, bias_inner, w1, w2)
+
+
+def finish(d_tokens, small, vecs, share, deep, whole):
+    seqs, span, width = d_tokens.shape
+    n, steps = len(whole), 4
+
+    def kernel(dx_ref, small_ref, vec_ref, *refs):
+        ins, refs = refs[:n], refs[n:]
+        dx_out, loss_ref, bias_ref = refs[:3]
+        for a, b in zip(ins, refs[3:]):
+            b[...] = a[...]
+        loss_ref[...] = small_ref[6:7, :1] * vec_ref[5:6, :1]
+        bias_ref[...] = small_ref[5:6, :deep]
+        dx_out[...] = dx_ref[...].astype(f32)
+
+    def block(a):
+        if a.ndim == 3:
+            return pl.BlockSpec((a.shape[0] // steps,) + a.shape[1:], lambda i: (i, 0, 0))
+        return pl.BlockSpec((a.shape[0], a.shape[1] // steps), lambda i: (0, i))
+
+    like = lambda a, dtype: jax.ShapeDtypeStruct(a.shape, dtype)
+    blocks = [block(a) for a in whole]
+    out = pl.pallas_call(
+        kernel,
+        grid=(steps,),
+        in_specs=[block(d_tokens), once((8, 128)), once((8, width))] + blocks,
+        out_specs=[block(d_tokens), once((1, 1)), once((1, deep))] + blocks,
+        out_shape=[like(d_tokens, f32), jax.ShapeDtypeStruct((1, 1), f32), jax.ShapeDtypeStruct((1, deep), f32)]
+        + [like(a, a.dtype) for a in whole],
+        compiler_params=pltpu.CompilerParams(vmem_limit_bytes=63 << 20),
+        name="finish",
+    )(d_tokens, small, vecs, *whole)
+    return out[0], out[1], out[2], out[3:]
 
 
 def cut(shape, which, pieces, orders, columns=False):
@@ -975,18 +1022,22 @@
     wq, wk, wv, wo = (w.reshape(width, width) for w in (wq, wk, wv, wo))
     w1, w2 = w1.reshape(width, hidden), w2.reshape(hidden, width)
     layer_out, d_one, d_branch, g_inner, gw2, small = feed_forward(
-        lay, h1, teacher, out_grad, lengths, vecs, bias1, w1, w2, aside
+        lay, h1, teacher, out_grad, lengths, vecs, bias1, w1, w2, back
     )
     if gw2.ndim == 2:
         gw2 = gw2.T.reshape(devices, hidden // devices, width)
     g_query, g_key, g_value, g_output, g_outer, small, d_tokens = attention_backward(
         lay, x, lengths, wq, wk, wv, wo, q, k, v, att, lse, d_branch, d_one, gw2, small, back, aside
     )
+    d_tokens, loss, g_bias, copied = finish(
+        d_tokens, small, vecs, share, deep, [layer_out, g_query, g_key, g_value, g_output, g_inner, g_outer]
+    )
+    layer_out, g_query, g_key, g_value, g_output, g_inner, g_outer = copied
     vec = lambda i: small[i, :share]
     return (
-        small[6, 0] * vecs[5, 0],
+        loss[0, 0],
         layer_out,
-        d_tokens.astype(f32),
+        d_tokens,
         g_query,
         g_key,
         g_value,
@@ -994,7 +1045,7 @@
         vec(3),
         vec(4),
         g_inner,
-        small[5, :deep],
+        g_bias[0],
         g_outer,
         vec(2),
         vec(0),

time: 411 us -> 390 us (0.949); the launches traced: 405 us -> 389 us
  local copies, waits for them, and re-layouts: 8.98 us -> 1.4 us
  other arithmetic: 4.22 us -> 0 us
    pallas_call x1, Pallas kernels: 134 us -> 125 us  [feed_forward(): pl.pallas_call(kernel, grid_spec=pltpu.PrefetchScalarGridSpec(num_scalar_...]
    pallas_call x0 -> x1, Pallas kernels: none -> 6.36 us  [finish(): pl.pallas_call(kernel, grid=(steps,), in_specs=[block(d_tokens), once((8,...]
    unnamed x23 -> x0, local copies, waits for them, and re-layouts: 5.56 us -> none
    pallas_call x1, Pallas kernels: 111 us -> 115 us  [attention_backward(): pl.pallas_call(kernel, grid_spec=pltpu.PrefetchScalarGridSpec(num_scalar_...]
    convert_element_type x1 -> x0, other arithmetic: 4.22 us -> none  [shards(): d_tokens.astype(f32)]
where the time goes in v4:
time: 390 us; the launch traced here: 389 us
  Pallas kernels  387 us (99%)
    pallas_call x1, Pallas kernels, attention_forward(): pl.pallas_call(kernel, in_specs=[pl.BlockSpec(memory_space=pltpu.SMEM)] +...  140 us
    pallas_call x1, Pallas kernels, feed_forward(): pl.pallas_call(kernel, grid_spec=pltpu.PrefetchScalarGridSpec(num_scalar_...  125 us
    pallas_call x1, Pallas kernels, attention_backward(): pl.pallas_call(kernel, grid_spec=pltpu.PrefetchScalarGridSpec(num_scalar_...  115 us

profile of v4, /device:TPU:0, one launch (start us, length us, event | category | flops | bytes accessed | tf_op | source)
XLA Modules:
  0.0 388.9 jit_solution(5888698445591316649)
XLA Ops:
  0.7 140.3 %attention_forward.1 = (bf16[4,2,2,2,32,1024]{5,4,3,2,1,0:T(8,128)(2,1)}, bf16[4,2,2,2,32,1024]{5,4,3,2,1,0:T(8,128)(2,1)}, bf16[4,2,2,2,32,1024]{5,4,3,2,1,0:T(...) custom-call(s32[8]{0:T(128)} %len_ref.5, ...), custom_call_target="tpu_custom_call" | custom-call | tf_op jit(solution)/shard_map/attention_forward/pallas_call | solution.py:498
  140.9 125.0 %feed_forward.1 = (bf16[8,128,1024]{2,1,0:T(8,128)(2,1)}, f32[1024,1024]{1,0:T(8,128)}, bf16[2,512,1024]{2,1,0:T(8,128)(2,1)}, f32[32,4096]{1,0:T(8,128)}, bf16[...) custom-call(s32[8]{0:T(128)} %len_ref.5, f32[1024,1024]{1,0:T(8,128)} %get-tuple-element.63.h1_ref, ...), custom_call_target="tpu_custom_call" | custom-call | tf_op jit(solution)/shard_map/feed_forward/pallas_call | solution.py:915
  265.9 115.0 %attention_backward.1 = (f32[32,1024]{1,0:T(8,128)}, f32[32,1024]{1,0:T(8,128)}, f32[32,1024]{1,0:T(8,128)}, f32[32,1024]{1,0:T(8,128)}, f32[128,1024]{1,0:T(8,1...) custom-call(s32[8]{0:T(128)} %len_ref.5, bf16[2,512,1024]{2,1,0:T(8,128)(2,1)} %get-tuple-element.53.x_in, ...), custom_call_target="tpu_custom_call" | custom-call | tf_op jit(solution)/shard_map/attention_backward/pallas_call | solution.py:679
  380.9 1.4 slice_bitcast_fusion
  382.4 6.4 %finish.1 = (f32[8,128,1024]{2,1,0:T(8,128)}, f32[1,1]{1,0:T(1,128)}, f32[1,128]{1,0:T(1,128)}, bf16[8,128,1024]{2,1,0:T(8,128)(2,1)}, f32[32,1024]{1,0:T(8,128)...) custom-call(bf16[8,128,1024]{2,1,0:T(8,128)(2,1)} %get-tuple-element, ...), custom_call_target="tpu_custom_call" | custom-call | tf_op jit(solution)/shard_map/finish/pallas_call | solution.py:977

commit v5 on v4

--- a/solution.py
+++ b/solution.py
@@ -253,15 +253,17 @@
             if left:
                 index[left[0]] = i
             mine = tuple(index.get(n, self.here[n]) for n in self.names)
-            value = self.held[mine].astype(f32)
+            alone = k < 0 or (k < 2 and self.lay.size[order[k]] == 2)
+            wide = self.held.dtype if alone else f32
+            value = self.held[mine].astype(wide)
             if k >= 0:
                 theirs = tuple(index[n] for n in left)
                 for d in range(self.lay.size[order[k]] - 1):
-                    value = value + self.recvs[k][(d,) + theirs].astype(f32)
+                    value = value + self.recvs[k][(d,) + theirs].astype(wide)
             elif self.staged is not None:
-                value = value + self.staged[mine].astype(f32)
+                value = value + self.staged[mine].astype(wide)
             else:
-                value = value + self.grad[self.lay.at({**self.here, **index}, ()) + self.cut].astype(f32)
+                value = value + self.grad[self.lay.at({**self.here, **index}, ()) + self.cut].astype(wide)
             if k == 2:
                 self.out[...] = value.T if self.turn else value
             else:
@@ -373,9 +375,9 @@
         tok_ref, refs = refs[0], refs[1:]
         ins, refs = refs[:n], refs[n:]
         fulls, refs = refs[:n], refs[n:]
-        x_out, q_out, k_out, v_out, att_out, lse_ref, h1_out, vec_out, bias_out = refs[:9]
-        x_ref, wq_ref, wk_ref, wv_ref, wo_ref, q_ref, k_ref, v_ref, att_ref, h1_ref, pack_ref, packs_ref = refs[9:21]
-        load, send, recv, own, rsend, rrecv, rown = refs[21:]
+        xt_out, q_out, k_out, v_out, att_out, lse_ref, h1_out, vec_out, bias_out = refs[:9]
+        x_ref, wq_ref, wk_ref, wv_ref, wo_ref, q_ref, k_ref, v_ref, att_ref, h1_ref, pack_ref, packs_ref, low_ref, xt_ref = refs[9:23]
+        load, send, recv, own, rsend, rrecv, rown = refs[23:]
         ins, fulls = list(ins) + [pack_ref], list(fulls) + [packs_ref]
         here = lay.here()
         pack_ref[...] = jnp.zeros_like(pack_ref)
@@ -392,7 +394,7 @@
             Gather(lay, here, ins[a], fulls[a], cut, send.at[i], recv.at[i], own.at[i], orders)
             for i, (a, cut, orders) in enumerate(parts)
         ]
-        events = skewed(gathers, 2)
+        events = skewed(gathers, 3)
         last = max(i for i, (part, stage) in enumerate(events) if part in gathers[:early] and stage == 4)
         for part, stage in events[: last + 1]:
             part.stage(stage)
@@ -407,7 +409,7 @@
         for c in loads:
             c.wait()
         hooks = Hooks()
-        hooks.spread(events[last + 1 :], 0, groups * slots * 4 // 3)
+        hooks.spread(events[last + 1 :], 0, groups * slots * 6 // 5)
         base = lax.axis_index("blk") * seqs
 
         def columns(ref, g):
@@ -428,6 +430,11 @@
                 for j, (low, weight) in enumerate(((q_ref, wq_ref), (k_ref, wk_ref), (v_ref, wv_ref))):
                     low[:, cols] = dot(xv, columns(weight, g)).astype(bf16)
                     hooks.at(g * slots + j, range(j, groups * slots, slots))
+
+            @pl.when(i == groups * pairs // 4)
+            def _():
+                for n in range(seqs):
+                    xt_ref[:, n * span : (n + 1) * span] = x_ref[n].T
 
             @pl.when(i == groups * pairs // 2)
             def _():
@@ -459,11 +466,13 @@
                 ot = dot(vt[h * DH : (h + 1) * DH], e.astype(bf16))
                 outs.append(ot * (1.0 / den))
                 lse_ref[g, pl.ds(r * 2 + h, 1)] = top + jnp.log2(den)
-            att_ref[at] = jnp.concatenate(outs, axis=0).T.astype(bf16)
+            turned = jnp.concatenate(outs, axis=0)
+            att_ref[at[1], at[0]] = turned.astype(bf16)
+            low_ref[at[0], pl.ds(pl.multiple_of(pair * 128, 128), 128)] = turned.T.astype(bf16)
 
             @pl.when(r == pairs - 1)
             def _():
-                add = dot(att_ref[:, cols], features(wo_ref, g))
+                add = dot(low_ref[...], features(wo_ref, g))
 
                 @pl.when(g == 0)
                 def _():
@@ -480,7 +489,7 @@
         saves = [
             pltpu.make_async_copy(src, dst, load.at[i])
             for i, (src, dst) in enumerate(
-                zip([x_ref, q_ref, k_ref, v_ref, att_ref, h1_ref], [x_out, q_out, k_out, v_out, att_out, h1_out]))
+                zip([xt_ref, q_ref, k_ref, v_ref, att_ref, h1_ref], [xt_out, q_out, k_out, v_out, att_out, h1_out]))
         ]
         for c in saves:
             c.start()
@@ -494,19 +503,20 @@
 
     whole = [jax.ShapeDtypeStruct(lay.dims + s.shape, s.dtype) for s in shards]
     vmem = pl.BlockSpec(memory_space=pltpu.VMEM)
-    act = jax.ShapeDtypeStruct((rows, width), bf16)
+    act, turned = jax.ShapeDtypeStruct((rows, width), bf16), jax.ShapeDtypeStruct((width, rows), bf16)
     return pl.pallas_call(
         kernel,
         in_specs=[pl.BlockSpec(memory_space=pltpu.SMEM)] + [vmem] * m + [ANY] + [vmem] * n,
         out_specs=[ANY] * (n + 5) + [vmem, ANY, vmem, vmem],
         out_shape=whole
-        + [jax.ShapeDtypeStruct((seqs, span, width), bf16), act, act, act, act,
+        + [turned, act, act, act, turned,
            jax.ShapeDtypeStruct((groups, heads, span), f32), jax.ShapeDtypeStruct((rows, width), f32),
            jax.ShapeDtypeStruct((8, width), f32), jax.ShapeDtypeStruct((1, deep * lay.devices), f32)],
         scratch_shapes=[pltpu.VMEM((seqs, span, width), bf16)]
         + [pltpu.VMEM(lay.dims + s.shape, bf16) for s in shards[:4]]
-        + [pltpu.VMEM((rows, width), bf16)] * 4
+        + [pltpu.VMEM((rows, width), bf16)] * 3 + [pltpu.VMEM((width, rows), bf16)]
         + [pltpu.VMEM((rows, width), f32), pltpu.VMEM((8, 128), f32), pltpu.VMEM(lay.dims + (8, 128), f32),
+           pltpu.VMEM((rows, GROUP), bf16), pltpu.VMEM((width, rows), bf16),
            pltpu.SemaphoreType.DMA((6,))]
         + sems(lay, p, 0)[:3]
         + [pltpu.SemaphoreType.DMA((lay.blk - 1,)), pltpu.SemaphoreType.DMA((lay.blk - 1,)),
@@ -516,8 +526,8 @@
     )(lengths, *vectors, tokens, *shards)
 
 
-def attention_backward(lay, x, lengths, wq, wk, wv, wo, q, k, v, att, lse, d_branch, d_one, outer, small, orders, aside):
-    seqs, span, width = x.shape
+def attention_backward(lay, xt, lengths, wq, wk, wv, wo, q, k, v, att, lse, d_branch, d_one, outer, small, orders, aside):
+    seqs, span, width = d_branch.shape
     rows = seqs * span
     heads = lse.shape[1]
     groups = width // GROUP
@@ -541,9 +551,9 @@
     outer = outer.reshape(lay.dims + outer.shape[1:])
 
     def kernel(
-        len_ref, x_in, wq_ref, wk_ref, wv_ref, wo_ref, q_ref, k_ref, v_ref, att_ref, lse_ref, db_ref, d1_in, outer_in, small_in,
+        len_ref, xt_ref, wq_ref, wk_ref, wv_ref, wo_ref, q_ref, k_ref, v_ref, att_ref, lse_ref, db_ref, d1_in, outer_in, small_in,
         gq_out, gk_out, gv_out, go_out, outer_out, small_out, dx_out,
-        gq_ref, gk_ref, gv_ref, go_ref, xt_ref, do_ref, dq_ref, dk_ref, dv_ref, acc_ref, dx_ref,
+        gq_ref, gk_ref, gv_ref, go_ref, do_ref, dq_ref, dk_ref, dv_ref, acc_ref, dx_ref,
         stage_small, stage_ref, send, recv, own, rsend, rrecv, rown, fetch_sem, *held,
     ):
         g = pl.program_id(0)
@@ -589,25 +599,17 @@
             lay.greet(here)
             for p, stage in events[:lag]:
                 p.stage(stage)
-            fetch = [
-                pltpu.make_async_copy(x_in, dx_ref, fetch_sem.at[0]),
-                pltpu.make_async_copy(d1_in, acc_ref, fetch_sem.at[1]),
-            ]
-            for c in fetch:
-                c.start()
-            for c in fetch:
-                c.wait()
-            for s in range(seqs):
-                xt_ref[:, s * span : (s + 1) * span] = dx_ref[s].T
+            fetch = pltpu.make_async_copy(d1_in, acc_ref, fetch_sem)
+            fetch.start()
 
             def output_rows(j, carry):
-                cols = pl.ds(pl.multiple_of(j * GROUP, GROUP), GROUP)
-                value = dot(att_ref[:, cols].T, db_ref[...].reshape(rows, width)).astype(bf16)
+                value = dot(att_ref[pl.ds(pl.multiple_of(j * GROUP, GROUP), GROUP)], db_ref[...].reshape(rows, width)).astype(bf16)
                 for d in range(GROUP // depth):
                     go_ref[lay.place(j * (GROUP // depth) + d)] = value[d * depth : (d + 1) * depth]
                 return carry
 
             lax.fori_loop(0, groups, output_rows, 0)
+            fetch.wait()
 
         do_ref[...] = dot_t(db_ref[...].reshape(rows, width), wo_ref[...]).astype(bf16)
 
@@ -681,15 +683,15 @@
         grid_spec=pltpu.PrefetchScalarGridSpec(
             num_scalar_prefetch=0,
             grid=(groups,),
-            in_specs=[pl.BlockSpec(memory_space=pltpu.SMEM), ANY, col, col, col, row, act, act, act, once((rows, width)),
+            in_specs=[pl.BlockSpec(memory_space=pltpu.SMEM), once((width, rows)), col, col, col, row, act, act, act, once((width, rows)),
                       pl.BlockSpec((1, heads, span), lambda g, *_: (g, 0, 0)), once((seqs, span, width)), ANY, ANY, ANY],
             out_specs=[once((depth, width))] * 4 + [once((share, deep) if wide else (deep, share)), once((8, 128)), ANY],
             scratch_shapes=[grad] * 4
-            + [pltpu.VMEM((width, rows), bf16)] + [pltpu.VMEM((rows, GROUP), bf16)] * 4
+            + [pltpu.VMEM((rows, GROUP), bf16)] * 4
             + [pltpu.VMEM((rows, width), f32), pltpu.VMEM((seqs, span, width), bf16)]
             + [pltpu.VMEM(no_core + (8, 128), f32)] + [pltpu.VMEM((lag + 1,) + no_core + (deep // pieces, share), bf16)]
             + sems(lay, count, 0)[:3]
-            + sems(lay, 0, seqs)[3:] + [pltpu.SemaphoreType.DMA((2,))]
+            + sems(lay, 0, seqs)[3:] + [pltpu.SemaphoreType.DMA]
             + [b for bs in bufs for b in bs],
         ),
         out_shape=[shard] * 4
@@ -698,14 +700,14 @@
         compiler_params=pltpu.CompilerParams(
             collective_id=3, has_side_effects=True, vmem_limit_bytes=63 << 20),
         name="attention_backward",
-    )(lengths, x, wq, wk, wv, wo, q, k, v, att, lse, d_branch, d_one, outer, small)
+    )(lengths, xt, wq, wk, wv, wo, q, k, v, att, lse, d_branch, d_one, outer, small)
 
 
 TILE = 512
 CHUNK = 512
 
 
-def feed_forward(lay, h1, teacher, out_grad, lengths, vecs, bias_inner, w1, w2, orders):
+def feed_forward(lay, h1, teacher, out_grad, lengths, vecs, bias_inner, w1, w2, orders, aside):
     rows, width = h1.shape
     hidden = w1.shape[1]
     seqs = teacher.shape[0] // lay.blk
@@ -717,7 +719,7 @@
     wide = share % 128 == 0
     pieces, depth, lag, kept = tiles, width // devices, 2, 4
     columns = hidden // pieces
-    bufs = Scatter.buffers(lay, (0, depth, 0, columns), bf16, orders)
+    ways = [aside if i % 3 < 2 else orders for i in range(pieces)]
 
     def kernel(
         len_ref, h1_ref, teach_in, og_in, vec_ref, b1_ref, w1_ref, w2_ref,
@@ -736,7 +738,7 @@
         sums = [
             Scatter(
                 lay, here, gw1_ref.at[i % kept], (0, depth, 0, columns), gw1_out.at[:, pl.ds(i * columns, columns)],
-                held[4 * i : 4 * i + 4], send.at[i], recv.at[i], own.at[i], orders)
+                held[4 * i : 4 * i + 4], send.at[i], recv.at[i], own.at[i], ways[i])
             for i in range(pieces)
         ]
         hooks = Hooks()
@@ -938,7 +940,7 @@
             ]
             + sems(lay, 0, 2 * seqs + 1)[3:]
             + sems(lay, pieces + 1, 0)[:3]
-            + bufs * pieces,
+            + [b for way in ways for b in Scatter.buffers(lay, (0, depth, 0, columns), bf16, way)],
         ),
         out_shape=[
             jax.ShapeDtypeStruct(teacher.shape, bf16),
@@ -961,8 +963,13 @@
     def kernel(dx_ref, small_ref, vec_ref, *refs):
         ins, refs = refs[:n], refs[n:]
         dx_out, loss_ref, bias_ref = refs[:3]
-        for a, b in zip(ins, refs[3:]):
-            b[...] = a[...]
+        for i, vec in enumerate(refs[3:8]):
+            vec[...] = small_ref[i : i + 1, :share]
+        for a, b in zip(ins, refs[8:]):
+            if a.ndim == 3:
+                b[...] = a[...]
+            else:
+                pl.when(pl.program_id(0) == 0)(lambda a=a, b=b: b.__setitem__(Ellipsis, a[...]))
         loss_ref[...] = small_ref[6:7, :1] * vec_ref[5:6, :1]
         bias_ref[...] = small_ref[5:6, :deep]
         dx_out[...] = dx_ref[...].astype(f32)
@@ -970,7 +977,7 @@
     def block(a):
         if a.ndim == 3:
             return pl.BlockSpec((a.shape[0] // steps,) + a.shape[1:], lambda i: (i, 0, 0))
-        return pl.BlockSpec((a.shape[0], a.shape[1] // steps), lambda i: (0, i))
+        return once(a.shape)
 
     like = lambda a, dtype: jax.ShapeDtypeStruct(a.shape, dtype)
     blocks = [block(a) for a in whole]
@@ -978,13 +985,14 @@
         kernel,
         grid=(steps,),
         in_specs=[block(d_tokens), once((8, 128)), once((8, width))] + blocks,
-        out_specs=[block(d_tokens), once((1, 1)), once((1, deep))] + blocks,
+        out_specs=[block(d_tokens), once((1, 1)), once((1, deep))] + [once((1, share))] * 5 + blocks,
         out_shape=[like(d_tokens, f32), jax.ShapeDtypeStruct((1, 1), f32), jax.ShapeDtypeStruct((1, deep), f32)]
+        + [jax.ShapeDtypeStruct((1, share), f32)] * 5
         + [like(a, a.dtype) for a in whole],
         compiler_params=pltpu.CompilerParams(vmem_limit_bytes=63 << 20),
         name="finish",
     )(d_tokens, small, vecs, *whole)
-    return out[0], out[1], out[2], out[3:]
+    return out[0], out[1], out[2], out[3:8], out[8:]
 
 
 def cut(shape, which, pieces, orders, columns=False):
@@ -1016,24 +1024,24 @@
     early = len(parts)
     parts += cut(w_inner.shape, 4, 8, there, True) + cut(w_outer.shape, 5, 8, there)
     vectors = [gain_one, shift_one, bias_outer, gain_two, shift_two, bias_inner]
-    wq, wk, wv, wo, w1, w2, x, q, k, v, att, lse, h1, vecs, bias1 = attention_forward(
+    wq, wk, wv, wo, w1, w2, xt, q, k, v, att, lse, h1, vecs, bias1 = attention_forward(
         lay, tokens, lengths, vectors, ins, parts, early
     )
     wq, wk, wv, wo = (w.reshape(width, width) for w in (wq, wk, wv, wo))
     w1, w2 = w1.reshape(width, hidden), w2.reshape(hidden, width)
     layer_out, d_one, d_branch, g_inner, gw2, small = feed_forward(
-        lay, h1, teacher, out_grad, lengths, vecs, bias1, w1, w2, back
+        lay, h1, teacher, out_grad, lengths, vecs, bias1, w1, w2, back, aside
     )
     if gw2.ndim == 2:
         gw2 = gw2.T.reshape(devices, hidden // devices, width)
     g_query, g_key, g_value, g_output, g_outer, small, d_tokens = attention_backward(
-        lay, x, lengths, wq, wk, wv, wo, q, k, v, att, lse, d_branch, d_one, gw2, small, back, aside
+        lay, xt, lengths, wq, wk, wv, wo, q, k, v, att, lse, d_branch, d_one, gw2, small, back, aside
     )
-    d_tokens, loss, g_bias, copied = finish(
+    d_tokens, loss, g_bias, vec_grads, copied = finish(
         d_tokens, small, vecs, share, deep, [layer_out, g_query, g_key, g_value, g_output, g_inner, g_outer]
     )
     layer_out, g_query, g_key, g_value, g_output, g_inner, g_outer = copied
-    vec = lambda i: small[i, :share]
+    vec = lambda i: vec_grads[i][0]
     return (
         loss[0, 0],
         layer_out,

time: 390 us -> 380 us (0.974)
  Pallas kernels: 387 us -> 377 us
    pallas_call x1, Pallas kernels: 115 us -> 110 us  [attention_backward(): pl.pallas_call(kernel, grid_spec=pltpu.PrefetchScalarGridSpec(num_scalar_...]
where the time goes in v5:
time: 380 us; the launch traced here: 378 us
  Pallas kernels  377 us (99%)
    pallas_call x1, Pallas kernels, attention_forward(): pl.pallas_call(kernel, in_specs=[pl.BlockSpec(memory_space=pltpu.SMEM)] +...  138 us
    pallas_call x1, Pallas kernels, feed_forward(): pl.pallas_call(kernel, grid_spec=pltpu.PrefetchScalarGridSpec(num_scalar_...  122 us
    pallas_call x1, Pallas kernels, attention_backward(): pl.pallas_call(kernel, grid_spec=pltpu.PrefetchScalarGridSpec(num_scalar_...  110 us

profile of v5, /device:TPU:0, one launch (start us, length us, event | category | flops | bytes accessed | tf_op | source)
XLA Modules:
  0.0 378.0 jit_solution(1649256605560887906)
XLA Ops:
  0.7 137.8 %attention_forward.1 = (bf16[4,2,2,2,32,1024]{5,4,3,2,1,0:T(8,128)(2,1)}, bf16[4,2,2,2,32,1024]{5,4,3,2,1,0:T(8,128)(2,1)}, bf16[4,2,2,2,32,1024]{5,4,3,2,1,0:T(...) custom-call(s32[8]{0:T(128)} %len_ref.5, ...), custom_call_target="tpu_custom_call" | custom-call | tf_op jit(solution)/shard_map/attention_forward/pallas_call | solution.py:507
  138.5 122.4 %feed_forward.1 = (bf16[8,128,1024]{2,1,0:T(8,128)(2,1)}, f32[1024,1024]{1,0:T(8,128)}, bf16[2,512,1024]{2,1,0:T(8,128)(2,1)}, f32[32,4096]{1,0:T(8,128)}, bf16[...) custom-call(s32[8]{0:T(128)} %len_ref.5, f32[1024,1024]{1,0:T(8,128)} %get-tuple-element.68.h1_ref, ...), custom_call_target="tpu_custom_call" | custom-call | tf_op jit(solution)/shard_map/feed_forward/pallas_call | solution.py:917
  260.9 110.5 %attention_backward.1 = (f32[32,1024]{1,0:T(8,128)}, f32[32,1024]{1,0:T(8,128)}, f32[32,1024]{1,0:T(8,128)}, f32[32,1024]{1,0:T(8,128)}, f32[128,1024]{1,0:T(8,1...) custom-call(s32[8]{0:T(128)} %len_ref.5, bf16[1024,1024]{1,0:T(8,128)(2,1)} %get-tuple-element.58.xt_ref, ...), custom_call_target="tpu_custom_call" | custom-call | tf_op jit(solution)/shard_map/attention_backward/pallas_call | solution.py:681
  371.4 6.4 %finish.1 = (f32[8,128,1024]{2,1,0:T(8,128)}, f32[1,1]{1,0:T(1,128)}, f32[1,128]{1,0:T(1,128)}, f32[1,32]{1,0:T(1,128)}, f32[1,32]{1,0:T(1,128)}, /*index=5*/f32...) custom-call(bf16[8,128,1024]{2,1,0:T(8,128)(2,1)} %get-tuple-element, ...), custom_call_target="tpu_custom_call" | custom-call | tf_op jit(solution)/shard_map/finish/pallas_call | solution.py:984

commit v6 on v5

--- a/solution.py
+++ b/solution.py
@@ -848,11 +848,13 @@
                 d_in = (d_act * slope_ref[j, at].astype(f32)).astype(bf16)
                 total += jnp.sum(d_in.astype(f32), axis=0, keepdims=True)
                 di_ref[at] = d_in
-                acc_ref[at] += dot_t(d_in, w1_ref[...])
             gb1_ref[:, pl.ds(pl.multiple_of(j * TILE, TILE), TILE)] = total
             value = dot(lowt_ref[...], di_ref[...]).astype(bf16)
             gw1_ref[lax.rem(j, kept)] = value.reshape(lay.dims + (depth, TILE))
             hooks.at(j, range(tiles))
+            for i in range(rows // CHUNK):
+                at = slice(i * CHUNK, (i + 1) * CHUNK)
+                acc_ref[at] += dot_t(di_ref[at], w1_ref[...])
 
         @pl.when(t == 2 * tiles)
         def _():
@@ -958,7 +960,7 @@
 
 def finish(d_tokens, small, vecs, share, deep, whole):
     seqs, span, width = d_tokens.shape
-    n, steps = len(whole), 4
+    n, steps = len(whole), 2
 
     def kernel(dx_ref, small_ref, vec_ref, *refs):
         ins, refs = refs[:n], refs[n:]

time: 380 us -> 378 us (level)
  no operation moved by 1% of the time
where the time goes in v6:
time: 378 us; the launch traced here: 377 us
  Pallas kernels  376 us (99%)
    pallas_call x1, Pallas kernels, attention_forward(): pl.pallas_call(kernel, in_specs=[pl.BlockSpec(memory_space=pltpu.SMEM)] +...  138 us
    pallas_call x1, Pallas kernels, feed_forward(): pl.pallas_call(kernel, grid_spec=pltpu.PrefetchScalarGridSpec(num_scalar_...  122 us
    pallas_call x1, Pallas kernels, attention_backward(): pl.pallas_call(kernel, grid_spec=pltpu.PrefetchScalarGridSpec(num_scalar_...  110 us

profile of v6, /device:TPU:0, one launch (start us, length us, event | category | flops | bytes accessed | tf_op | source)
XLA Modules:
  0.0 376.6 jit_solution(10986907611741155920)
XLA Ops:
  0.7 137.8 %attention_forward.1 = (bf16[4,2,2,2,32,1024]{5,4,3,2,1,0:T(8,128)(2,1)}, bf16[4,2,2,2,32,1024]{5,4,3,2,1,0:T(8,128)(2,1)}, bf16[4,2,2,2,32,1024]{5,4,3,2,1,0:T(...) custom-call(s32[8]{0:T(128)} %len_ref.5, ...), custom_call_target="tpu_custom_call" | custom-call | tf_op jit(solution)/shard_map/attention_forward/pallas_call | solution.py:507
  138.5 121.9 %feed_forward.1 = (bf16[8,128,1024]{2,1,0:T(8,128)(2,1)}, f32[1024,1024]{1,0:T(8,128)}, bf16[2,512,1024]{2,1,0:T(8,128)(2,1)}, f32[32,4096]{1,0:T(8,128)}, bf16[...) custom-call(s32[8]{0:T(128)} %len_ref.5, f32[1024,1024]{1,0:T(8,128)} %get-tuple-element.68.h1_ref, ...), custom_call_target="tpu_custom_call" | custom-call | tf_op jit(solution)/shard_map/feed_forward/pallas_call | solution.py:919
  260.4 110.4 %attention_backward.1 = (f32[32,1024]{1,0:T(8,128)}, f32[32,1024]{1,0:T(8,128)}, f32[32,1024]{1,0:T(8,128)}, f32[32,1024]{1,0:T(8,128)}, f32[128,1024]{1,0:T(8,1...) custom-call(s32[8]{0:T(128)} %len_ref.5, bf16[1024,1024]{1,0:T(8,128)(2,1)} %get-tuple-element.58.xt_ref, ...), custom_call_target="tpu_custom_call" | custom-call | tf_op jit(solution)/shard_map/attention_backward/pallas_call | solution.py:681
  370.8 5.5 %finish.1 = (f32[8,128,1024]{2,1,0:T(8,128)}, f32[1,1]{1,0:T(1,128)}, f32[1,128]{1,0:T(1,128)}, f32[1,32]{1,0:T(1,128)}, f32[1,32]{1,0:T(1,128)}, /*index=5*/f32...) custom-call(bf16[8,128,1024]{2,1,0:T(8,128)(2,1)} %get-tuple-element, ...), custom_call_target="tpu_custom_call" | custom-call | tf_op jit(solution)/shard_map/finish/pallas_call | solution.py:986

commit v7 on v6

--- a/solution.py
+++ b/solution.py
@@ -1022,7 +1022,7 @@
     ins = [w_query, w_key, w_value, w_output, w_inner, w_outer]
     parts = [(6, (0, 8), there)]
     for i in range(4):
-        parts += cut(ins[i].shape, i, 1, there)
+        parts += cut(ins[i].shape, i, 2, there, True)
     early = len(parts)
     parts += cut(w_inner.shape, 4, 8, there, True) + cut(w_outer.shape, 5, 8, there)
     vectors = [gain_one, shift_one, bias_outer, gain_two, shift_two, bias_inner]

time: 378 us -> 379 us (level)
  no operation moved by 1% of the time
where the time goes in v7:
time: 379 us; the launch traced here: 377 us
  Pallas kernels  376 us (99%)
    pallas_call x1, Pallas kernels, attention_forward(): pl.pallas_call(kernel, in_specs=[pl.BlockSpec(memory_space=pltpu.SMEM)] +...  138 us
    pallas_call x1, Pallas kernels, feed_forward(): pl.pallas_call(kernel, grid_spec=pltpu.PrefetchScalarGridSpec(num_scalar_...  122 us
    pallas_call x1, Pallas kernels, attention_backward(): pl.pallas_call(kernel, grid_spec=pltpu.PrefetchScalarGridSpec(num_scalar_...  110 us

profile of v7, /device:TPU:0, one launch (start us, length us, event | category | flops | bytes accessed | tf_op | source)
XLA Modules:
  0.0 377.1 jit_solution(9393164188370754997)
XLA Ops:
  0.7 138.3 %attention_forward.1 = (bf16[4,2,2,2,32,1024]{5,4,3,2,1,0:T(8,128)(2,1)}, bf16[4,2,2,2,32,1024]{5,4,3,2,1,0:T(8,128)(2,1)}, bf16[4,2,2,2,32,1024]{5,4,3,2,1,0:T(...) custom-call(s32[8]{0:T(128)} %len_ref.5, ...), custom_call_target="tpu_custom_call" | custom-call | tf_op jit(solution)/shard_map/attention_forward/pallas_call | solution.py:507
  139.0 121.9 %feed_forward.1 = (bf16[8,128,1024]{2,1,0:T(8,128)(2,1)}, f32[1024,1024]{1,0:T(8,128)}, bf16[2,512,1024]{2,1,0:T(8,128)(2,1)}, f32[32,4096]{1,0:T(8,128)}, bf16[...) custom-call(s32[8]{0:T(128)} %len_ref.5, f32[1024,1024]{1,0:T(8,128)} %get-tuple-element.68.h1_ref, ...), custom_call_target="tpu_custom_call" | custom-call | tf_op jit(solution)/shard_map/feed_forward/pallas_call | solution.py:919
  260.9 110.4 %attention_backward.1 = (f32[32,1024]{1,0:T(8,128)}, f32[32,1024]{1,0:T(8,128)}, f32[32,1024]{1,0:T(8,128)}, f32[32,1024]{1,0:T(8,128)}, f32[128,1024]{1,0:T(8,1...) custom-call(s32[8]{0:T(128)} %len_ref.5, bf16[1024,1024]{1,0:T(8,128)(2,1)} %get-tuple-element.58.xt_ref, ...), custom_call_target="tpu_custom_call" | custom-call | tf_op jit(solution)/shard_map/attention_backward/pallas_call | solution.py:681
  371.4 5.5 %finish.1 = (f32[8,128,1024]{2,1,0:T(8,128)}, f32[1,1]{1,0:T(1,128)}, f32[1,128]{1,0:T(1,128)}, f32[1,32]{1,0:T(1,128)}, f32[1,32]{1,0:T(1,128)}, /*index=5*/f32...) custom-call(bf16[8,128,1024]{2,1,0:T(8,128)(2,1)} %get-tuple-element, ...), custom_call_target="tpu_custom_call" | custom-call | tf_op jit(solution)/shard_map/finish/pallas_call | solution.py:986
